TPU v7x, 32 devices: a whole 2x2x4 slice. The times are simulated.
32 devices in a mesh: dp: 16 (over z, y, core), mp: 2 (over x).
Axes of the slice: x: 2, y: 2, z: 4, core: 2. Of those that a mesh axis runs over, the one named last changes fastest.
Arguments:
- attention: bfloat16 [2048, 2048], P('dp', 'mp'), may hold values from -6 to 6
- residual: bfloat16 [2048, 2048], P('dp', 'mp'), may hold values from -6 to 6
- out_weight: bfloat16 [2048, 2048], P('mp', 'dp'), may hold values from -0.125 to 0.125
- ffn_gain: float32 [2048], P('mp'), may hold values from 0.1 to 1.9
- shared_gate: bfloat16 [2048, 2816], P('dp', 'mp'), may hold values from -0.125 to 0.125
- shared_up: bfloat16 [2048, 2816], P('dp', 'mp'), may hold values from -0.125 to 0.125
- shared_down: bfloat16 [2816, 2048], P('mp', 'dp'), may hold values from -0.109375 to 0.109375
- expert_gate: bfloat16 [16, 2048, 1408], P('dp', None, 'mp'), may hold values from -0.125 to 0.125
- expert_up: bfloat16 [16, 2048, 1408], P('dp', None, 'mp'), may hold values from -0.125 to 0.125
- expert_down: bfloat16 [16, 1408, 2048], P('dp', 'mp'), may hold values from -0.15625 to 0.15625
- route_ids: int32 [2048, 6], P('dp'), may hold values from 0 to 15, all different within a row; in each aligned block of 128 rows (0 to 127, 128 to 255, ...) at most 64 rows name the same one
- route_scores: float32 [2048, 6], P('dp'), may hold values from 0.05 to 1
- placement: int32 [16], replicated, may hold values from 0 to 15, each once
- next_gain: float32 [2048], P('mp'), may hold values from 0.1 to 1.9
Outputs:
- final: bfloat16 [2048, 2048], P('dp', 'mp')
- next_normed: bfloat16 [2048, 2048], P('dp', 'mp')
Inputs may be any that keep to these rules, and one draw needn't show every extreme that they name: `route_ids`: A token's 6 experts differ. In each aligned block of 128 rows (the rows of one index of dp) no expert is named by more than 64 rows, a bound that some block reaches. `placement`: each storage index is used by exactly one expert.
All inputs are finite; a program needn't handle non-finite values.
Results may differ from a plain program's by a relative error of at most 0.0075.
Values may be sent and summed in bfloat16 or wider, within the bound.
No kernel may reach another device: no remote copies, remote signals or barrier semaphores. Data moves between devices by JAX's collectives and lax.ppermute only.
A program may use at most 128 MiB of HBM per device.

v0:
```python
import functools

import jax
import jax.numpy as jnp
import numpy as np
from jax import lax
from jax.experimental import pallas as pl
from jax.experimental.pallas import tpu as pltpu
from jax.sharding import PartitionSpec as P

D = 2048
EPSILON = 1e-06
CORES = 2
LANES = 128
VMEM_BYTES = 8 * 2**20
FFN_VMEM = 16 * 2**20


def matmul(left, right):
    return jnp.dot(left, right, preferred_element_type=jnp.float32)


def matmul_nt(left, right):
    return lax.dot_general(
        left, right, (((1,), (1,)), ((), ())), preferred_element_type=jnp.float32
    )


def round_up(count, multiple):
    return -(-count // multiple) * multiple


def chip_cycle(deep, wide):
    if deep == 1 or wide == 1:
        return list(range(deep * wide))
    walk = []
    for y in range(wide):
        line = range(1, deep) if y % 2 == 0 else range(deep - 1, 0, -1)
        walk += [z * wide + y for z in line]
    return walk + list(range(wide - 1, -1, -1))


class Moves:
    def __init__(self, dp_count, mp_count):
        self.chips = dp_count // CORES
        self.mp_count = mp_count
        wide = mp_count if self.chips % mp_count == 0 else 1
        self.cycle = chip_cycle(self.chips // wide, wide)
        self.left = self.chips // 2
        self.right = (self.chips - 1) // 2

    def info(self):
        table = np.zeros((self.chips * CORES, self.mp_count, self.chips + 2), np.int32)
        for at, chip in enumerate(self.cycle):
            for core in range(CORES):
                row = table[chip * CORES + core]
                row[:, : self.chips] = np.roll(self.cycle, -at)
                row[:, self.chips] = core
                row[:, self.chips + 1] = np.arange(self.mp_count)
        return jnp.asarray(table)[lax.axis_index("dp"), lax.axis_index("mp")]

    def step(self, value, way):
        count = self.chips
        pairs = [
            (self.cycle[i] * CORES + c, self.cycle[(i + way) % count] * CORES + c)
            for i in range(count)
            for c in range(CORES)
        ]
        return lax.ppermute(value, "dp", pairs)

    def gather(self, values):
        ahead = [[value] for value in values]
        behind = [[value] for value in values]
        for s in range(1, self.left + 1):
            moved = [self.step(a[-1], 1) for a in ahead]
            if s <= self.right:
                moved += [self.step(b[-1], -1) for b in behind]
            moved = lax.optimization_barrier(moved)
            for a, value in zip(ahead, moved):
                a.append(value)
            for b, value in zip(behind, moved[len(values) :]):
                b.append(value)
        return list(zip(ahead, behind))

    def swap_core(self, value):
        count = self.chips * CORES
        return lax.ppermute(value, "dp", [(d, d ^ 1) for d in range(count)])

    def from_mp(self, value, k):
        count = self.mp_count
        return lax.ppermute(value, "mp", [((i + k) % count, i) for i in range(count)])

    def all_mp(self, value):
        return [value] + [self.from_mp(value, k) for k in range(1, self.mp_count)]


def after(value, *others):
    return lax.optimization_barrier((value, *others))[0]


def vmem():
    return pl.BlockSpec(memory_space=pltpu.VMEM)


def smem():
    return pl.BlockSpec(memory_space=pltpu.SMEM)


def params(*held):
    size = 0
    for shape, dtype in held:
        lanes = round_up(shape[-1], LANES)
        size += np.prod(shape[:-1], dtype=np.int64) * lanes * jnp.dtype(dtype).itemsize
    return pltpu.CompilerParams(vmem_limit_bytes=max(VMEM_BYTES, 2 * int(size)))


def project_kernel(at, blocks, *refs):
    left_ref, other_ref = refs[:2]
    out_ref, other_out_ref = refs[-2:]
    for i in range(blocks):
        block = refs[2 + i][...]
        out_ref[at + i] = matmul(left_ref[...], block).astype(out_ref.dtype)
        other_out_ref[at + i] = matmul(other_ref[...], block).astype(out_ref.dtype)


def project(left, other, blocks, at, into):
    fresh = isinstance(into, int)
    shape = (into if fresh else into[0].shape[0], left.shape[0], blocks[0].shape[1])
    given = [] if fresh else list(into)
    first = 2 + len(blocks)
    return pl.pallas_call(
        functools.partial(project_kernel, at, len(blocks)),
        out_shape=[jax.ShapeDtypeStruct(shape, jnp.bfloat16)] * 2,
        in_specs=[vmem()] * (first + len(given)),
        out_specs=[vmem()] * 2,
        input_output_aliases={first + i: i for i in range(len(given))},
        compiler_params=params(),
        cost_estimate=pl.CostEstimate(
            flops=4 * left.size * shape[2] * len(blocks),
            bytes_accessed=2 * blocks[0].size * len(blocks),
            transcendentals=0,
        ),
    )(left, other, *blocks, *given)


def norm_kernel(offsets, mp_count, info_ref, *refs):
    stacks, refs = refs[: len(offsets) * mp_count], refs[len(offsets) * mp_count :]
    residuals, refs = refs[:mp_count], refs[mp_count:]
    gains, refs = refs[:mp_count], refs[mp_count:]
    normed_ref, own_ref, sums_ref, rest_ref, gain_ref, hidden_ref, sems, *held = refs
    copies = [
        pltpu.make_async_copy(stack, to, sems.at[i])
        for i, (stack, to) in enumerate(zip(stacks, held))
    ]
    for copy in copies:
        copy.start()
    chips = sums_ref.shape[0] // CORES
    core, mp = info_ref[chips], info_ref[chips + 1]
    for s, listed in enumerate(offsets):
        for k in range(mp_count):
            copies[s * mp_count + k].wait()
        for i, (offset, other) in enumerate(listed):
            total = held[s * mp_count][i].astype(jnp.float32)
            for k in range(1, mp_count):
                total = total + held[s * mp_count + k][i].astype(jnp.float32)
            lane = 1 - core if other else core
            sums_ref[info_ref[offset % chips] * CORES + lane] = total
    for k in range(mp_count):
        at = lax.rem(mp + k, mp_count)
        rest_ref[at] = residuals[k][...]
        gain_ref[at] = gains[k][...]
    rows, half = own_ref.shape
    width = sums_ref.shape[2]
    per_half = half // width
    squares = jnp.zeros((rows, 1), jnp.float32)
    for k in range(mp_count):
        pieces = [sums_ref[k * per_half + j] for j in range(per_half)]
        total = rest_ref[k].astype(jnp.float32) + jnp.concatenate(pieces, axis=1)
        hidden = total.astype(jnp.bfloat16).astype(jnp.float32)
        hidden_ref[k] = hidden
        squares += jnp.sum(hidden * hidden, axis=1, keepdims=True)
    scale = lax.rsqrt(squares / (half * mp_count) + EPSILON)
    for k in range(mp_count):
        value = hidden_ref[k] * scale * gain_ref[k]
        normed_ref[:, k * half : (k + 1) * half] = value.astype(normed_ref.dtype)
    own_ref[...] = hidden_ref[mp].astype(own_ref.dtype)


def norm(info, offsets, stacks, residuals, gains):
    mp_count = len(residuals)
    rows, half = residuals[0].shape
    width = stacks[0].shape[2]
    count = half * mp_count // width
    return pl.pallas_call(
        functools.partial(norm_kernel, offsets, mp_count),
        out_shape=[
            jax.ShapeDtypeStruct((rows, half * mp_count), jnp.bfloat16),
            jax.ShapeDtypeStruct((rows, half), jnp.bfloat16),
        ],
        in_specs=[smem()]
        + [pl.BlockSpec(memory_space=pl.ANY)] * len(stacks)
        + [vmem()] * (2 * mp_count),
        out_specs=[vmem()] * 2,
        scratch_shapes=[
            pltpu.VMEM((count, rows, width), jnp.float32),
            pltpu.VMEM((mp_count, rows, half), jnp.bfloat16),
            pltpu.VMEM((mp_count, 1, half), jnp.float32),
            pltpu.VMEM((mp_count, rows, half), jnp.float32),
            pltpu.SemaphoreType.DMA((len(stacks),)),
        ]
        + [pltpu.VMEM(stack.shape, stack.dtype) for stack in stacks],
        compiler_params=params(
            ((count, rows, width), jnp.float32), *[(stack.shape, stack.dtype) for stack in stacks]
        ),
    )(info, *stacks, *residuals, *gains)


def ffn_kernel(offsets, pieces, mp_count, info_ref, *refs):
    scores, refs = refs[:2], refs[2:]
    tokens, refs = refs[:pieces], refs[pieces:]
    held, refs = refs[:9], refs[9:]
    outs, (rows_ref, act_ref, shared_act_ref) = refs[:mp_count], refs[mp_count:]
    at = 0
    for token_ref in tokens:
        rows_ref[pl.ds(at, token_ref.shape[0]), :] = token_ref[...]
        at += token_ref.shape[0]
    chips = info_ref.shape[0] - 2
    turned = []
    for e in range(2):
        devices = [info_ref[offset % chips] * CORES + info_ref[chips] for offset in offsets]
        wide = [scores[e][pl.ds(device, 1), :] for device in devices]
        wide = jnp.broadcast_to(jnp.concatenate(wide, axis=1), (8, at))
        turned.append(wide.T[:, :1])
    for e in range(3):
        gate = matmul_nt(rows_ref[...], held[2 * e][...])
        up = matmul_nt(rows_ref[...], held[2 * e + 1][...])
        act = gate / (1.0 + jnp.exp(-gate)) * up
        if e < 2:
            act_ref[e] = (act * turned[e]).astype(act_ref.dtype)
        else:
            shared_act_ref[...] = act.astype(shared_act_ref.dtype)
    half = outs[0].shape[1]
    width = 256 if half % 256 == 0 else half
    mp = info_ref[info_ref.shape[0] - 1]
    for k in range(mp_count):
        start = lax.rem(mp + k, mp_count) * half

        def columns(j, carry, k=k, start=start):
            at = pl.ds(pl.multiple_of(start + j * width, LANES), width)
            total = matmul(act_ref[0], held[6][:, at])
            total += matmul(act_ref[1], held[7][:, at])
            total += matmul(shared_act_ref[...], held[8][:, at])
            to = pl.ds(pl.multiple_of(j * width, LANES), width)
            outs[k][:, to] = total.astype(outs[k].dtype)
            return carry

        lax.fori_loop(0, half // width, columns, 0)


def ffn(offsets, tokens, scores, weights, info, mp_count):
    width = tokens[0].shape[1]
    total = sum(piece.shape[0] for piece in tokens)
    half = width // mp_count
    hidden_units = weights[0].shape[0]
    return pl.pallas_call(
        functools.partial(ffn_kernel, offsets, len(tokens), mp_count),
        out_shape=[
            jax.ShapeDtypeStruct((total, half), jnp.float32 if k == 0 else jnp.bfloat16)
            for k in range(mp_count)
        ],
        in_specs=[smem()] + [vmem()] * (2 + len(tokens) + len(weights)),
        out_specs=[vmem()] * mp_count,
        scratch_shapes=[
            pltpu.VMEM((total, width), jnp.bfloat16),
            pltpu.VMEM((2, total, hidden_units), jnp.bfloat16),
            pltpu.VMEM((total, weights[4].shape[0]), jnp.bfloat16),
        ],
        compiler_params=pltpu.CompilerParams(vmem_limit_bytes=FFN_VMEM),
        cost_estimate=pl.CostEstimate(
            flops=2 * total * sum(w.size for w in weights),
            bytes_accessed=2 * sum(w.size for w in weights),
            transcendentals=0,
        ),
    )(info, *scores, *tokens, *weights)


def local(
    attention,
    residual,
    out_weight,
    ffn_gain,
    shared_gate,
    shared_up,
    shared_down,
    expert_gate,
    expert_up,
    expert_down,
    route_ids,
    route_scores,
    placement,
    next_gain,
):
    rows, half = attention.shape
    mp_count = lax.axis_size("mp")
    dp_count = lax.axis_size("dp")
    moves = Moves(dp_count, mp_count)
    chips, left, right = moves.chips, moves.left, moves.right
    bf16, f32 = jnp.bfloat16, jnp.float32
    info = moves.info()
    core = info[chips]

    ids, weight = route_ids.T, route_scores.T
    stored = jnp.arange(dp_count, dtype=jnp.int32)
    expert_of = jnp.sum(
        jnp.where(placement[None, :] == stored[:, None], stored[None, :], 0), axis=1
    )
    own_scores = jnp.sum(
        jnp.where(ids[None] == expert_of[:, None, None], weight[None], 0.0), axis=1
    )

    units = shared_gate.shape[1] // dp_count
    wide = shared_gate.shape[0]
    dealt = [
        shared_gate.T.reshape(dp_count, units, wide),
        shared_up.T.reshape(dp_count, units, wide),
        shared_down.reshape(dp_count, units, wide),
    ]
    rest = own_scores
    thirds = []
    for _ in range(3):
        third = lax.reduce_precision(rest, 8, 7)
        thirds.append(third.astype(bf16))
        rest = rest - third
    thirds = jnp.stack(thirds, axis=1).reshape(dp_count, 3 * rows // wide, wide)
    used = 3 * units + thirds.shape[1]
    shared, at = 0, 0
    for part in (*dealt, thirds):
        over = round_up(used, 16) - at - part.shape[1]
        shared = shared + jnp.pad(part, ((0, 0), (at, over), (0, 0)))
        at += part.shape[1]
    mine = [expert_gate[0].T, expert_up[0].T, expert_down[0]]
    other = [moves.swap_core(w) for w in mine]
    other_attention = moves.swap_core(attention)
    residuals = moves.all_mp(residual)
    gains = moves.all_mp(ffn_gain.reshape(1, half))
    offsets, stacks, swapped = [], [], []

    def exchange(listed, own, beside):
        swapped.append(moves.swap_core(beside))
        for value, flip in ((own, False), (swapped[-1], True)):
            offsets.append([(offset, flip) for offset in listed])
            stacks.append(moves.all_mp(value))

    early = 1 + 2 * (left - 1)
    listed, filled = [0], 0
    sums = early
    arrived = [out_weight]
    ahead = behind = out_weight
    for s in range(1, left + 1):
        if s > 1:
            sums = project(attention, other_attention, arrived, filled, sums)
            filled += len(arrived)
            arrived = []
        if s == left:
            exchange(listed, *sums)
            listed = []
        moved = [moves.step(ahead, 1)]
        if s <= right:
            moved.append(moves.step(behind, -1))
        ties = []
        if s == left - 1:
            ties = [shared, *other]
        if s == left:
            ties = [*residuals[1:], *gains[1:]]
        if s > 1:
            ties += sums
        moved, ties = lax.optimization_barrier((moved, ties))
        if s > 1:
            sums = ties[-2:]
        if s == left - 1:
            shared, *other = ties[:-2]
        ahead = moved[0]
        arrived.append(ahead)
        listed.append(-s)
        if s <= right:
            behind = moved[1]
            arrived.append(behind)
            listed.append(s)
    shared = lax.all_to_all(after(shared, swapped[0]), "dp", 0, 0, tiled=True)
    exchange(listed, *project(attention, other_attention, arrived, 0, len(arrived)))
    normed, own_hidden = norm(
        info, offsets, [piece for stack in stacks for piece in stack], residuals, gains
    )
    shared = shared.transpose(1, 0, 2)
    shared = [shared, moves.swap_core(shared)]
    spare = round_up(CORES * units, 16) - CORES * units
    parts = []
    for i in range(3):
        part = [value[i * units : (i + 1) * units].reshape(units, D) for value in shared]
        parts.append(jnp.pad(jnp.concatenate(part), ((0, spare), (0, 0))))
    weights = [
        mine[0], mine[1], other[0], other[1], parts[0], parts[1], mine[2], other[2], parts[2]
    ]
    scores = []
    for value in shared:
        thirds = value[3 * units : used].transpose(1, 0, 2).reshape(dp_count, 3, rows)
        scores.append(jnp.sum(thirds.astype(f32), axis=1))

    def swap_mp(sent):
        return [moves.from_mp(sent[k - 1], mp_count - k) for k in range(1, mp_count)]

    ahead = behind = normed
    listed, blocks = [0], [normed]
    done = []
    for s in range(1, left + 1):
        kept, *sent = ffn(listed, blocks, scores, weights, info, mp_count)
        if s <= right:
            moved = [moves.step(ahead, 1), moves.step(behind, -1)]
        else:
            moved = [moves.step(ahead[: rows // 2], 1), moves.step(behind[rows // 2 :], -1)]
        came = done[-1][2] if done else []
        moved, sent, came = lax.optimization_barrier((moved, sent, came))
        if done:
            done[-1][2] = came
        done.append([listed, kept, swap_mp(sent)])
        ahead, behind = blocks = moved
        listed = [-s, s] if s <= right else [s]
    kept, *sent = ffn(listed, blocks, scores, weights, info, mp_count)
    done.append([listed, kept, swap_mp(sent)])
    parts = {}
    for listed, kept, came in done:
        for value in came:
            kept = kept + value.astype(f32)
        for i, offset in enumerate(listed):
            parts[offset % chips] = kept[i * rows : (i + 1) * rows]

    mixture = parts[0]
    if left > right:
        mixture = mixture + moves.step(parts[left].astype(bf16), left).astype(f32)
    for way in (1, -1):
        carried = None
        for s in range(right, 0, -1):
            part = parts[way * s % chips]
            if carried is not None:
                part = part + carried.astype(f32)
            carried = moves.step(part.astype(bf16), way)
        if carried is not None:
            mixture = mixture + carried.astype(f32)

    final = (own_hidden.astype(f32) + mixture).astype(bf16)
    final_float = final.astype(f32)
    final_squares = lax.psum(jnp.sum(final_float * final_float, axis=1), "mp")
    next_normed = (
        final_float * lax.rsqrt(final_squares / D + EPSILON)[:, None] * next_gain
    ).astype(bf16)
    return (final, next_normed)


def solution(mesh):
    in_specs = (
        P("dp", "mp"),
        P("dp", "mp"),
        P("mp", "dp"),
        P("mp"),
        P("dp", "mp"),
        P("dp", "mp"),
        P("mp", "dp"),
        P("dp", None, "mp"),
        P("dp", None, "mp"),
        P("dp", "mp", None),
        P("dp", None),
        P("dp", None),
        P(),
        P("mp"),
    )
    out_specs = (P("dp", "mp"), P("dp", "mp"))
    return jax.shard_map(local, mesh=mesh, in_specs=in_specs, out_specs=out_specs, check_vma=False)
```

profile of v0, /device:TPU:0, one launch (start us, length us, event | category | flops | bytes accessed | tf_op | source)
XLA Modules:
  0.0 201.3 jit_solution(13450489468719075296)
XLA Ops:
  1.7 2.7 %collective-permute-start.1 = (bf16[1024,128]{1,0:T(8,128)(2,1)}, bf16[1024,128]{1,0:T(8,128)(2,1)}, u32[]{:S(2)}, u32[]{:S(2)}) collective-permute-start(bf16[1024,128]{1,0:T(8,128)(2,1)} %refs_2_.1), channel_id=1, source_target_pairs={{8,16},{10,18},{16,24},{18,26},{24,28},{26,30},{28,20},{30,22},{20... | collective-permute-start | bytes 786440 | tf_op jit(solution)/shard_map/ppermute | solution.py:69
  4.3 7.2 %collective-permute-done.1.refs_3_ = bf16[1024,128]{1,0:T(8,128)(2,1)} collective-permute-done((bf16[1024,128]{1,0:T(8,128)(2,1)}, bf16[1024,128]{1,0:T(8,128)(2,1)}, u32[]{:S(2)}, u32[]{:S(2)}) %collective-permute-start.1) | collective-permute-done | bytes 262176 | tf_op jit(solution)/shard_map/ppermute | solution.py:69
  13.0 1.6 collective-permute-start.3
  14.9 2.9 %collective-permute-start.4 = (bf16[1024,128]{1,0:T(8,128)(2,1)}, bf16[1024,128]{1,0:T(8,128)(2,1)}, u32[]{:S(2)}, u32[]{:S(2)}) collective-permute-start(bf16[1024,128]{1,0:T(8,128)(2,1)} %collective-permute-done.2.refs_4_), channel_id=1, source_target_pairs={{8,0},{10,2},{16,8},{18,10},{24,16},{26,18},{28,24},{30,26},{20,28... | collective-permute-start | bytes 786440 | tf_op jit(solution)/shard_map/ppermute | solution.py:69
  18.6 1.9 copy.41
  20.5 1.8 copy.42
  22.3 1.9 copy.43
  24.2 1.1 copy.44
  25.2 1.0 copy.45
  26.3 0.9 copy-done.6
  27.3 1.6 shard_map.158
  29.0 2.0 collective-permute-start.6
  31.1 1.5 shard_map.159
  32.6 4.6 %collective-permute-done.5.refs_2_ = bf16[1024,128]{1,0:T(8,128)(2,1)S(1)} collective-permute-done((bf16[1024,128]{1,0:T(8,128)(2,1)}, bf16[1024,128]{1,0:T(8,128)(2,1)S(1)}, u32[]{:S(2)}, u32[]{:S(2)}) %collective-permute-start.5) | collective-permute-done | bytes 262176 | tf_op jit(solution)/shard_map/ppermute | solution.py:69
  38.4 1.5 collective-permute-done.11.refs_2_
  40.6 1.4 copy.46
  42.0 6.1 %all-to-all-start = ((bf16[16,272,128]{2,1,0:T(8,128)(2,1)}), bf16[16,272,128]{2,1,0:T(8,128)(2,1)}, u32[]{:S(2)}, u32[]{:S(2)}) async-start(bf16[16,272,128]{2,1,0:T(8,128)(2,1)} %copy.46), calls=%async_computation | async-start | bytes 2228224 | tf_op jit(solution)/shard_map/all_to_all | solution.py:389
  48.2 1.6 collective-permute-start.14
  49.7 1.8 collective-permute-start.13
  52.1 1.5 collective-permute-start.12
  54.1 12.8 %collective-permute-done.15.refs_11_ = f32[1,1024]{1,0:T(1,128)S(1)} collective-permute-done((f32[1,1024]{1,0:T(1,128)S(1)}, f32[1,1024]{1,0:T(1,128)S(1)}, u32[]{:S(2)}, u32[]{:S(2)}) %collective-permute-start.15) | collective-permute-done | bytes 4128 | tf_op jit(solution)/shard_map/ppermute | solution.py:91
  67.6 5.3 %collective-permute-done.13.refs_2_ = bf16[1024,128]{1,0:T(8,128)(2,1)S(1)} collective-permute-done((bf16[1024,128]{1,0:T(8,128)(2,1)}, bf16[1024,128]{1,0:T(8,128)(2,1)S(1)}, u32[]{:S(2)}, u32[]{:S(2)}) %collective-permute-start.13) | collective-permute-done | bytes 262176 | tf_op jit(solution)/shard_map/ppermute | solution.py:69
  73.4 1.6 collective-permute-start.16
  74.9 1.1 collective-permute-start.18
  77.3 1.5 collective-permute-done.18.refs_7_
  78.8 0.9 copy-done.5
  79.8 0.9 copy-done.9
  80.7 0.9 copy-done.11
  81.7 0.9 copy-done.14
  82.6 3.6 %shard_map.162 = (bf16[128,2048]{1,0:T(8,128)(2,1)}, bf16[128,1024]{1,0:T(8,128)(2,1)S(1)}) custom-call(s32[10]{0:T(128)S(1)} %dynamic-slice_bitcast_fusion.info_ref, bf16[7,128,128]{2,1,0:T(8,128)(2,1)S(1)} %copy-done.5, bf16[7,128,128]{2,1,0:T(8,128)(2,1)} %collective-permute-done.10.refs_1_, bf16[7,128,128]{2,1,0:T(8,128)(2,1)S(1)} %copy-done.14, ...), custom_call_target="tpu_custom_call" | custom-call | tf_op jit(solution)/shard_map/pallas_call | solution.py:194
  86.9 3.3 %collective-permute-start.21 = (bf16[128,2048]{1,0:T(8,128)(2,1)}, bf16[128,2048]{1,0:T(8,128)(2,1)S(1)}, u32[]{:S(2)}, u32[]{:S(2)}) collective-permute-start(bf16[128,2048]{1,0:T(8,128)(2,1)} %get-tuple-element.75.refs_2_), channel_id=1, source_target_pairs={{8,0},{10,2},{16,8},{18,10},{24,16},{26,18},{28,24},{30,26},{20,28... | collective-permute-start | bytes 1572872 | tf_op jit(solution)/shard_map/ppermute | solution.py:69
  90.2 4.2 %collective-permute-start.20 = (bf16[128,2048]{1,0:T(8,128)(2,1)}, bf16[128,2048]{1,0:T(8,128)(2,1)}, u32[]{:S(2)}, u32[]{:S(2)}) collective-permute-start(bf16[128,2048]{1,0:T(8,128)(2,1)} %get-tuple-element.75.refs_2_), channel_id=1, source_target_pairs={{8,16},{10,18},{16,24},{18,26},{24,28},{26,30},{28,20},{30,22},{20... | collective-permute-start | bytes 1572872 | tf_op jit(solution)/shard_map/ppermute | solution.py:69
  94.4 1.4 slice_bitcast_fusion.1
  97.6 0.9 copy-done.1
  98.5 0.9 copy-done
  99.4 9.4 %shard_map.163 = (f32[128,1024]{1,0:T(8,128)S(1)}, bf16[128,1024]{1,0:T(8,128)(2,1)S(1)}) custom-call(s32[10]{0:T(128)S(1)} %dynamic-slice_bitcast_fusion.info_ref, f32[16,128]{1,0:T(8,128)S(1)} %convert_reduce_fusion.1.refs_0_, f32[16,128]{1,0:T(8,128)S(1)} %convert_reduce_fusion.refs_1_, bf16[128,2048]{1,0:T(8,128)(2,1)} %get-tuple-element.75.refs_2_, ...), custom_call_target="tpu_custom_call" | custom-call | flops 2491416576 | bytes 19464192 | tf_op jit(solution)/shard_map/pallas_call | solution.py:265
  108.9 2.3 %collective-permute-start.22 = (bf16[128,2048]{1,0:T(8,128)(2,1)}, bf16[128,2048]{1,0:T(8,128)(2,1)S(1)}, u32[]{:S(2)}, u32[]{:S(2)}) collective-permute-start(bf16[128,2048]{1,0:T(8,128)(2,1)} %collective-permute-done.20.refs_2_), channel_id=1, source_target_pairs={{8,16},{10,18},{16,24},{18,26},{24,28},{26,30},{28,20},{30,22},{20... | collective-permute-start | bytes 1572872 | tf_op jit(solution)/shard_map/ppermute | solution.py:69
  111.2 1.3 collective-permute-start.23
  112.5 1.1 collective-permute-start.24
  113.6 10.3 %shard_map.164 = (f32[256,1024]{1,0:T(8,128)S(1)}, bf16[256,1024]{1,0:T(8,128)(2,1)S(1)}) custom-call(s32[10]{0:T(128)S(1)} %dynamic-slice_bitcast_fusion.info_ref, f32[16,128]{1,0:T(8,128)S(1)} %convert_reduce_fusion.1.refs_0_, f32[16,128]{1,0:T(8,128)S(1)} %convert_reduce_fusion.refs_1_, bf16[128,2048]{1,0:T(8,128)(2,1)} %collective-permute-done.20.refs_2_, ...), custom_call_target="tpu_custom_call" | custom-call | flops 4982833152 | bytes 19464192 | tf_op jit(solution)/shard_map/pallas_call | solution.py:265
  123.9 1.1 collective-permute-done.22.refs_2_
  125.6 1.1 collective-permute-start.27
  126.7 1.7 collective-permute-start.25
  128.7 10.1 %shard_map.165 = (f32[256,1024]{1,0:T(8,128)S(1)}, bf16[256,1024]{1,0:T(8,128)(2,1)S(1)}) custom-call(s32[10]{0:T(128)S(1)} %dynamic-slice_bitcast_fusion.info_ref, f32[16,128]{1,0:T(8,128)S(1)} %convert_reduce_fusion.1.refs_0_, f32[16,128]{1,0:T(8,128)S(1)} %convert_reduce_fusion.refs_1_, bf16[128,2048]{1,0:T(8,128)(2,1)S(1)} %collective-permute-done.22.refs_2_, ...), custom_call_target="tpu_custom_call" | custom-call | flops 4982833152 | bytes 19464192 | tf_op jit(solution)/shard_map/pallas_call | solution.py:265
  140.0 1.2 collective-permute-done.26.refs_3_
  141.1 0.9 collective-permute-start.30
  142.7 1.4 collective-permute-start.28
  144.1 10.1 %shard_map.166 = (f32[256,1024]{1,0:T(8,128)S(1)}, bf16[256,1024]{1,0:T(8,128)(2,1)S(1)}) custom-call(s32[10]{0:T(128)S(1)} %dynamic-slice_bitcast_fusion.info_ref, f32[16,128]{1,0:T(8,128)S(1)} %convert_reduce_fusion.1.refs_0_, f32[16,128]{1,0:T(8,128)S(1)} %convert_reduce_fusion.refs_1_, bf16[128,2048]{1,0:T(8,128)(2,1)S(1)} %collective-permute-done.25.refs_2_, ...), custom_call_target="tpu_custom_call" | custom-call | flops 4982833152 | bytes 19464192 | tf_op jit(solution)/shard_map/pallas_call | solution.py:265
  154.3 1.2 collective-permute-start.33
  155.5 9.2 %shard_map.167 = (f32[128,1024]{1,0:T(8,128)S(1)}, bf16[128,1024]{1,0:T(8,128)(2,1)S(1)}) custom-call(s32[10]{0:T(128)S(1)} %dynamic-slice_bitcast_fusion.info_ref, f32[16,128]{1,0:T(8,128)S(1)} %convert_reduce_fusion.1.refs_0_, f32[16,128]{1,0:T(8,128)S(1)} %convert_reduce_fusion.refs_1_, bf16[64,2048]{1,0:T(8,128)(2,1)S(1)} %collective-permute-done.28.refs_2_, ...), custom_call_target="tpu_custom_call" | custom-call | flops 2491416576 | bytes 19464192 | tf_op jit(solution)/shard_map/pallas_call | solution.py:265
  164.8 1.0 collective-permute-start.31
  166.5 1.2 collective-permute-start.34
  167.7 0.9 collective-permute-start.37
  168.7 5.4 %collective-permute-done.34 = bf16[128,1024]{1,0:T(8,128)(2,1)S(1)} collective-permute-done((bf16[128,1024]{1,0:T(8,128)(2,1)S(1)}, bf16[128,1024]{1,0:T(8,128)(2,1)S(1)}, u32[]{:S(2)}, u32[]{:S(2)}) %collective-permute-start.34) | collective-permute-done | bytes 262176 | tf_op jit(solution)/shard_map/ppermute | solution.py:69
  174.1 1.3 collective-permute-done.37
  175.6 1.1 collective-permute-start.35
  176.7 1.0 collective-permute-start.38
  177.9 4.1 %collective-permute-start.32 = (bf16[128,1024]{1,0:T(8,128)(2,1)S(1)}, bf16[128,1024]{1,0:T(8,128)(2,1)S(1)}, u32[]{:S(2)}, u32[]{:S(2)}) collective-permute-start(bf16[128,1024]{1,0:T(8,128)(2,1)S(1)} %add_convert_fusion.2), channel_id=1, source_target_pairs={{8,20},{10,22},{16,12},{18,14},{24,4},{26,6},{28,0},{30,2},{20,8},... | collective-permute-start | bytes 786440 | tf_op jit(solution)/shard_map/ppermute | solution.py:69
  182.0 4.7 %collective-permute-done.35 = bf16[128,1024]{1,0:T(8,128)(2,1)S(1)} collective-permute-done((bf16[128,1024]{1,0:T(8,128)(2,1)S(1)}, bf16[128,1024]{1,0:T(8,128)(2,1)S(1)}, u32[]{:S(2)}, u32[]{:S(2)}) %collective-permute-start.35) | collective-permute-done | bytes 262176 | tf_op jit(solution)/shard_map/ppermute | solution.py:69
  188.0 1.3 collective-permute-start.39
  190.0 3.6 %collective-permute-done.36 = bf16[128,1024]{1,0:T(8,128)(2,1)S(1)} collective-permute-done((bf16[128,1024]{1,0:T(8,128)(2,1)S(1)}, bf16[128,1024]{1,0:T(8,128)(2,1)S(1)}, u32[]{:S(2)}, u32[]{:S(2)}) %collective-permute-start.36) | collective-permute-done | bytes 262176 | tf_op jit(solution)/shard_map/ppermute | solution.py:69
  193.6 1.6 collective-permute-done.39
  195.5 4.9 %psum.7 = f32[128]{0:T(128)S(1)} all-reduce(f32[128]{0:T(128)S(1)} %get-tuple-element.104), channel_id=1, replica_groups=mesh['dp'=16,'mp'=2] {'mp'}, use_global_device_ids=true, to_apply=%region_5.6 | all-reduce | flops 128 | bytes 1024 | tf_op jit(solution)/shard_map/psum | solution.py:452
  200.5 0.8 fusion.9
  (99 shorter events, 18.1 us)
Async XLA Ops:
  0.6 25.7 %copy-start.3 = (bf16[128,1024]{1,0:T(8,128)(2,1)S(1)}, bf16[128,1024]{1,0:T(8,128)(2,1)}, u32[]{:S(2)}) copy-start(bf16[128,1024]{1,0:T(8,128)(2,1)} %refs_0_.7) | copy-start | bytes 786436
  0.6 36.6 %collective-permute-start.7 = (bf16[704,2048]{1,0:T(8,128)(2,1)}, bf16[704,2048]{1,0:T(8,128)(2,1)S(1)}, u32[]{:S(2)}, u32[]{:S(2)}) collective-permute-start(bf16[704,2048]{1,0:T(8,128)(2,1)} %bitcast.51), channel_id=1, source_target_pairs={{0,2},{2,0},{4,6},{6,4},{8,10},{10,8},{12,14},{14,12},{16,18},{18,... | collective-permute-start | bytes 8650760 | tf_op jit(solution)/shard_map/ppermute | solution.py:87
  1.2 36.1 %collective-permute-start.8 = (bf16[704,2048]{1,0:T(8,128)(2,1)}, bf16[704,2048]{1,0:T(8,128)(2,1)}, u32[]{:S(2)}, u32[]{:S(2)}) collective-permute-start(bf16[704,2048]{1,0:T(8,128)(2,1)} %bitcast.57), channel_id=1, source_target_pairs={{0,2},{2,0},{4,6},{6,4},{8,10},{10,8},{12,14},{14,12},{16,18},{18,... | collective-permute-start | bytes 8650760 | tf_op jit(solution)/shard_map/ppermute | solution.py:87
  1.2 36.0 %collective-permute-start.9 = (bf16[704,2048]{1,0:T(8,128)(2,1)}, bf16[704,2048]{1,0:T(8,128)(2,1)}, u32[]{:S(2)}, u32[]{:S(2)}) collective-permute-start(bf16[704,2048]{1,0:T(8,128)(2,1)} %bitcast.63), channel_id=1, source_target_pairs={{0,2},{2,0},{4,6},{6,4},{8,10},{10,8},{12,14},{14,12},{16,18},{18,... | collective-permute-start | bytes 8650760 | tf_op jit(solution)/shard_map/ppermute | solution.py:87
  1.7 9.8 %collective-permute-start.1 = (bf16[1024,128]{1,0:T(8,128)(2,1)}, bf16[1024,128]{1,0:T(8,128)(2,1)}, u32[]{:S(2)}, u32[]{:S(2)}) collective-permute-start(bf16[1024,128]{1,0:T(8,128)(2,1)} %refs_2_.1), channel_id=1, source_target_pairs={{8,16},{10,18},{16,24},{18,26},{24,28},{26,30},{28,20},{30,22},{20... | collective-permute-start | bytes 786440 | tf_op jit(solution)/shard_map/ppermute | solution.py:69
  4.3 8.7 %collective-permute-start.2 = (bf16[1024,128]{1,0:T(8,128)(2,1)}, bf16[1024,128]{1,0:T(8,128)(2,1)}, u32[]{:S(2)}, u32[]{:S(2)}) collective-permute-start(bf16[1024,128]{1,0:T(8,128)(2,1)} %refs_2_.1), channel_id=1, source_target_pairs={{8,0},{10,2},{16,8},{18,10},{24,16},{26,18},{28,24},{30,26},{20,28... | collective-permute-start | bytes 786440 | tf_op jit(solution)/shard_map/ppermute | solution.py:69
  11.5 3.4 %collective-permute-start = (bf16[128,1024]{1,0:T(8,128)(2,1)}, bf16[128,1024]{1,0:T(8,128)(2,1)S(1)}, u32[]{:S(2)}, u32[]{:S(2)}) collective-permute-start(bf16[128,1024]{1,0:T(8,128)(2,1)} %refs_0_.7), channel_id=1, source_target_pairs={{0,2},{2,0},{4,6},{6,4},{8,10},{10,8},{12,14},{14,12},{16,18},{18,... | collective-permute-start | bytes 786440 | tf_op jit(solution)/shard_map/ppermute | solution.py:87
  13.0 15.8 %collective-permute-start.3 = (bf16[1024,128]{1,0:T(8,128)(2,1)}, bf16[1024,128]{1,0:T(8,128)(2,1)}, u32[]{:S(2)}, u32[]{:S(2)}) collective-permute-start(bf16[1024,128]{1,0:T(8,128)(2,1)} %collective-permute-done.1.refs_3_), channel_id=1, source_target_pairs={{8,16},{10,18},{16,24},{18,26},{24,28},{26,30},{28,20},{30,22},{20... | collective-permute-start | bytes 786440 | tf_op jit(solution)/shard_map/ppermute | solution.py:69
  14.9 14.0 %collective-permute-start.4 = (bf16[1024,128]{1,0:T(8,128)(2,1)}, bf16[1024,128]{1,0:T(8,128)(2,1)}, u32[]{:S(2)}, u32[]{:S(2)}) collective-permute-start(bf16[1024,128]{1,0:T(8,128)(2,1)} %collective-permute-done.2.refs_4_), channel_id=1, source_target_pairs={{8,0},{10,2},{16,8},{18,10},{24,16},{26,18},{28,24},{30,26},{20,28... | collective-permute-start | bytes 786440 | tf_op jit(solution)/shard_map/ppermute | solution.py:69
  24.2 6.8 %copy-start.16 = (bf16[16,88,128]{2,0,1:T(8,128)(2,1)S(1)}, bf16[16,88,128]{2,0,1:T(8,128)(2,1)}, u32[]{:S(2)}) copy-start(bf16[16,88,128]{2,0,1:T(8,128)(2,1)} %copy.42) | copy-start | bytes 1081348
  26.3 1.0 copy-start.6
  28.9 8.3 %collective-permute-start.5 = (bf16[1024,128]{1,0:T(8,128)(2,1)}, bf16[1024,128]{1,0:T(8,128)(2,1)S(1)}, u32[]{:S(2)}, u32[]{:S(2)}) collective-permute-start(bf16[1024,128]{1,0:T(8,128)(2,1)} %collective-permute-done.3.refs_2_), channel_id=1, source_target_pairs={{8,16},{10,18},{16,24},{18,26},{24,28},{26,30},{28,20},{30,22},{20... | collective-permute-start | bytes 786440 | tf_op jit(solution)/shard_map/ppermute | solution.py:69
  29.0 8.3 %collective-permute-start.6 = (bf16[1024,128]{1,0:T(8,128)(2,1)}, bf16[1024,128]{1,0:T(8,128)(2,1)S(1)}, u32[]{:S(2)}, u32[]{:S(2)}) collective-permute-start(bf16[1024,128]{1,0:T(8,128)(2,1)} %collective-permute-done.4.refs_3_), channel_id=1, source_target_pairs={{8,0},{10,2},{16,8},{18,10},{24,16},{26,18},{28,24},{30,26},{20,28... | collective-permute-start | bytes 786440 | tf_op jit(solution)/shard_map/ppermute | solution.py:69
  37.2 2.7 %copy-start.12 = (bf16[1024,128]{1,0:T(8,128)(2,1)}, bf16[1024,128]{1,0:T(8,128)(2,1)S(1)}, u32[]{:S(2)}) copy-start(bf16[1024,128]{1,0:T(8,128)(2,1)S(1)} %collective-permute-done.5.refs_2_) | copy-start | bytes 786436
  37.7 0.7 copy-start.4
  38.4 15.1 %copy-start.15 = (f32[1024]{0:T(1024)S(1)}, f32[1024]{0:T(1024)}, u32[]{:S(2)}) copy-start(f32[1024]{0:T(1024)} %param.18) | copy-start | bytes 12292
  38.4 1.5 collective-permute-start.11
  39.9 0.7 copy-start.13
  42.0 52.4 %all-to-all-start = ((bf16[16,272,128]{2,1,0:T(8,128)(2,1)}), bf16[16,272,128]{2,1,0:T(8,128)(2,1)}, u32[]{:S(2)}, u32[]{:S(2)}) async-start(bf16[16,272,128]{2,1,0:T(8,128)(2,1)} %copy.46), calls=%async_computation | async-start | bytes 2228224 | tf_op jit(solution)/shard_map/all_to_all | solution.py:389
  48.2 18.8 %collective-permute-start.14 = (bf16[128,1024]{1,0:T(8,128)(2,1)}, bf16[128,1024]{1,0:T(8,128)(2,1)S(1)}, u32[]{:S(2)}, u32[]{:S(2)}) collective-permute-start(bf16[128,1024]{1,0:T(8,128)(2,1)} %refs_8_.1), channel_id=1, source_target_pairs={{1,0},{0,1},{3,2},{2,3},{5,4},{4,5},{7,6},{6,7},{9,8},{8,9},{11,10... | collective-permute-start | bytes 786440 | tf_op jit(solution)/shard_map/ppermute | solution.py:91
  49.7 23.3 %collective-permute-start.13 = (bf16[1024,128]{1,0:T(8,128)(2,1)}, bf16[1024,128]{1,0:T(8,128)(2,1)S(1)}, u32[]{:S(2)}, u32[]{:S(2)}) collective-permute-start(bf16[1024,128]{1,0:T(8,128)(2,1)} %copy-done.12), channel_id=1, source_target_pairs={{8,16},{10,18},{16,24},{18,26},{24,28},{26,30},{28,20},{30,22},{20... | collective-permute-start | bytes 786440 | tf_op jit(solution)/shard_map/ppermute | solution.py:69
  51.5 25.2 %collective-permute-start.10 = (bf16[7,128,128]{2,1,0:T(8,128)(2,1)}, bf16[7,128,128]{2,1,0:T(8,128)(2,1)}, u32[]{:S(2)}, u32[]{:S(2)}) collective-permute-start(bf16[7,128,128]{2,1,0:T(8,128)(2,1)} %copy-done.4), channel_id=1, source_target_pairs={{1,0},{0,1},{3,2},{2,3},{5,4},{4,5},{7,6},{6,7},{9,8},{8,9},{11,10... | collective-permute-start | bytes 688136 | tf_op jit(solution)/shard_map/ppermute | solution.py:91
  52.1 26.8 %collective-permute-start.12 = (bf16[7,128,128]{2,1,0:T(8,128)(2,1)}, bf16[7,128,128]{2,1,0:T(8,128)(2,1)}, u32[]{:S(2)}, u32[]{:S(2)}) collective-permute-start(bf16[7,128,128]{2,1,0:T(8,128)(2,1)} %copy-done.13), channel_id=1, source_target_pairs={{1,0},{0,1},{3,2},{2,3},{5,4},{4,5},{7,6},{6,7},{9,8},{8,9},{11,10... | collective-permute-start | bytes 688136 | tf_op jit(solution)/shard_map/ppermute | solution.py:91
  53.6 13.4 %collective-permute-start.15 = (f32[1,1024]{1,0:T(1,128)S(1)}, f32[1,1024]{1,0:T(1,128)S(1)}, u32[]{:S(2)}, u32[]{:S(2)}) collective-permute-start(f32[1,1024]{1,0:T(1,128)S(1)} %bitcast.69), channel_id=1, source_target_pairs={{1,0},{0,1},{3,2},{2,3},{5,4},{4,5},{7,6},{6,7},{9,8},{8,9},{11,10... | collective-permute-start | bytes 12296 | tf_op jit(solution)/shard_map/ppermute | solution.py:91
  66.9 0.7 copy-start.10
  73.3 1.6 collective-permute-start.17
  73.4 4.0 %collective-permute-start.16 = (bf16[1,128,128]{2,1,0:T(8,128)(2,1)S(1)}, bf16[1,128,128]{2,1,0:T(8,128)(2,1)S(1)}, u32[]{:S(2)}, u32[]{:S(2)}) collective-permute-start(bf16[1,128,128]{2,1,0:T(8,128)(2,1)S(1)} %get-tuple-element.70.refs_4_), channel_id=1, source_target_pairs={{1,0},{0,1},{3,2},{2,3},{5,4},{4,5},{7,6},{6,7},{9,8},{8,9},{11,10... | collective-permute-start | bytes 98312 | tf_op jit(solution)/shard_map/ppermute | solution.py:91
  74.9 3.9 %collective-permute-start.18 = (bf16[1,128,128]{2,1,0:T(8,128)(2,1)S(1)}, bf16[1,128,128]{2,1,0:T(8,128)(2,1)S(1)}, u32[]{:S(2)}, u32[]{:S(2)}) collective-permute-start(bf16[1,128,128]{2,1,0:T(8,128)(2,1)S(1)} %collective-permute-done.17.refs_6_), channel_id=1, source_target_pairs={{1,0},{0,1},{3,2},{2,3},{5,4},{4,5},{7,6},{6,7},{9,8},{8,9},{11,10... | collective-permute-start | bytes 98312 | tf_op jit(solution)/shard_map/ppermute | solution.py:91
  78.8 0.9 copy-start.5
  79.8 0.9 copy-start.9
  80.7 0.9 copy-start.11
  81.7 0.9 copy-start.14
  86.2 0.7 copy-start.7
  86.9 21.9 %collective-permute-start.21 = (bf16[128,2048]{1,0:T(8,128)(2,1)}, bf16[128,2048]{1,0:T(8,128)(2,1)S(1)}, u32[]{:S(2)}, u32[]{:S(2)}) collective-permute-start(bf16[128,2048]{1,0:T(8,128)(2,1)} %get-tuple-element.75.refs_2_), channel_id=1, source_target_pairs={{8,0},{10,2},{16,8},{18,10},{24,16},{26,18},{28,24},{30,26},{20,28... | collective-permute-start | bytes 1572872 | tf_op jit(solution)/shard_map/ppermute | solution.py:69
  90.2 18.7 %collective-permute-start.20 = (bf16[128,2048]{1,0:T(8,128)(2,1)}, bf16[128,2048]{1,0:T(8,128)(2,1)}, u32[]{:S(2)}, u32[]{:S(2)}) collective-permute-start(bf16[128,2048]{1,0:T(8,128)(2,1)} %get-tuple-element.75.refs_2_), channel_id=1, source_target_pairs={{8,16},{10,18},{16,24},{18,26},{24,28},{26,30},{28,20},{30,22},{20... | collective-permute-start | bytes 1572872 | tf_op jit(solution)/shard_map/ppermute | solution.py:69
  94.4 3.0 %collective-permute-start.19 = (bf16[272,16,128]{2,0,1:T(8,128)(2,1)}, bf16[272,16,128]{2,0,1:T(8,128)(2,1)S(1)}, u32[]{:S(2)}, u32[]{:S(2)}) collective-permute-start(bf16[272,16,128]{2,0,1:T(8,128)(2,1)} %bitcast.15), channel_id=1, source_target_pairs={{0,2},{2,0},{4,6},{6,4},{8,10},{10,8},{12,14},{14,12},{16,18},{18,... | collective-permute-start | bytes 3342344 | tf_op jit(solution)/shard_map/ppermute | solution.py:87
  94.4 3.2 %copy-start.2 = (bf16[1,704,2048]{2,1,0:T(8,128)(2,1)S(1)}, bf16[1,704,2048]{2,1,0:T(8,128)(2,1)}, u32[]{:S(2)}) copy-start(bf16[1,704,2048]{2,1,0:T(8,128)(2,1)} %param.24) | copy-start | bytes 8650756
  96.7 1.8 copy-start.1
  96.8 2.6 %copy-start = (bf16[1,2048,704]{1,2,0:T(8,128)(2,1)S(1)}, bf16[1,2048,704]{1,2,0:T(8,128)(2,1)}, u32[]{:S(2)}) copy-start(bf16[1,2048,704]{1,2,0:T(8,128)(2,1)} %param.22) | copy-start | bytes 8650756
  108.9 16.1 %collective-permute-start.22 = (bf16[128,2048]{1,0:T(8,128)(2,1)}, bf16[128,2048]{1,0:T(8,128)(2,1)S(1)}, u32[]{:S(2)}, u32[]{:S(2)}) collective-permute-start(bf16[128,2048]{1,0:T(8,128)(2,1)} %collective-permute-done.20.refs_2_), channel_id=1, source_target_pairs={{8,16},{10,18},{16,24},{18,26},{24,28},{26,30},{28,20},{30,22},{20... | collective-permute-start | bytes 1572872 | tf_op jit(solution)/shard_map/ppermute | solution.py:69
  111.2 14.3 %collective-permute-start.23 = (bf16[128,2048]{1,0:T(8,128)(2,1)S(1)}, bf16[128,2048]{1,0:T(8,128)(2,1)S(1)}, u32[]{:S(2)}, u32[]{:S(2)}) collective-permute-start(bf16[128,2048]{1,0:T(8,128)(2,1)S(1)} %collective-permute-done.21.refs_3_), channel_id=1, source_target_pairs={{8,0},{10,2},{16,8},{18,10},{24,16},{26,18},{28,24},{30,26},{20,28... | collective-permute-start | bytes 1572872 | tf_op jit(solution)/shard_map/ppermute | solution.py:69
  112.5 11.4 %collective-permute-start.24 = (bf16[128,1024]{1,0:T(8,128)(2,1)S(1)}, bf16[128,1024]{1,0:T(8,128)(2,1)S(1)}, u32[]{:S(2)}, u32[]{:S(2)}) collective-permute-start(bf16[128,1024]{1,0:T(8,128)(2,1)S(1)} %get-tuple-element.84), channel_id=1, source_target_pairs={{1,0},{0,1},{3,2},{2,3},{5,4},{4,5},{7,6},{6,7},{9,8},{8,9},{11,10... | collective-permute-start | bytes 786440 | tf_op jit(solution)/shard_map/ppermute | solution.py:91
  125.6 13.5 %collective-permute-start.27 = (bf16[256,1024]{1,0:T(8,128)(2,1)S(1)}, bf16[256,1024]{1,0:T(8,128)(2,1)S(1)}, u32[]{:S(2)}, u32[]{:S(2)}) collective-permute-start(bf16[256,1024]{1,0:T(8,128)(2,1)S(1)} %get-tuple-element.89), channel_id=1, source_target_pairs={{1,0},{0,1},{3,2},{2,3},{5,4},{4,5},{7,6},{6,7},{9,8},{8,9},{11,10... | collective-permute-start | bytes 1572872 | tf_op jit(solution)/shard_map/ppermute | solution.py:91
  126.7 13.3 %collective-permute-start.25 = (bf16[128,2048]{1,0:T(8,128)(2,1)S(1)}, bf16[128,2048]{1,0:T(8,128)(2,1)S(1)}, u32[]{:S(2)}, u32[]{:S(2)}) collective-permute-start(bf16[128,2048]{1,0:T(8,128)(2,1)S(1)} %collective-permute-done.22.refs_2_), channel_id=1, source_target_pairs={{8,16},{10,18},{16,24},{18,26},{24,28},{26,30},{28,20},{30,22},{20... | collective-permute-start | bytes 1572872 | tf_op jit(solution)/shard_map/ppermute | solution.py:69
  128.4 12.7 %collective-permute-start.26 = (bf16[128,2048]{1,0:T(8,128)(2,1)S(1)}, bf16[128,2048]{1,0:T(8,128)(2,1)S(1)}, u32[]{:S(2)}, u32[]{:S(2)}) collective-permute-start(bf16[128,2048]{1,0:T(8,128)(2,1)S(1)} %collective-permute-done.23.refs_3_), channel_id=1, source_target_pairs={{8,0},{10,2},{16,8},{18,10},{24,16},{26,18},{28,24},{30,26},{20,28... | collective-permute-start | bytes 1572872 | tf_op jit(solution)/shard_map/ppermute | solution.py:69
  141.1 13.2 %collective-permute-start.30 = (bf16[256,1024]{1,0:T(8,128)(2,1)S(1)}, bf16[256,1024]{1,0:T(8,128)(2,1)S(1)}, u32[]{:S(2)}, u32[]{:S(2)}) collective-permute-start(bf16[256,1024]{1,0:T(8,128)(2,1)S(1)} %get-tuple-element.93), channel_id=1, source_target_pairs={{1,0},{0,1},{3,2},{2,3},{5,4},{4,5},{7,6},{6,7},{9,8},{8,9},{11,10... | collective-permute-start | bytes 1572872 | tf_op jit(solution)/shard_map/ppermute | solution.py:91
  142.1 12.2 %collective-permute-start.29 = (bf16[64,2048]{1,0:T(8,128)(2,1)S(1)}, bf16[64,2048]{1,0:T(8,128)(2,1)S(1)}, u32[]{:S(2)}, u32[]{:S(2)}) collective-permute-start(bf16[64,2048]{1,0:T(8,128)(2,1)S(1)} %slice.59), channel_id=1, source_target_pairs={{8,0},{10,2},{16,8},{18,10},{24,16},{26,18},{28,24},{30,26},{20,28... | collective-permute-start | bytes 786440 | tf_op jit(solution)/shard_map/ppermute | solution.py:69
  142.7 11.6 %collective-permute-start.28 = (bf16[64,2048]{1,0:T(8,128)(2,1)S(1)}, bf16[64,2048]{1,0:T(8,128)(2,1)S(1)}, u32[]{:S(2)}, u32[]{:S(2)}) collective-permute-start(bf16[64,2048]{1,0:T(8,128)(2,1)S(1)} %slice.58), channel_id=1, source_target_pairs={{8,16},{10,18},{16,24},{18,26},{24,28},{26,30},{28,20},{30,22},{20... | collective-permute-start | bytes 786440 | tf_op jit(solution)/shard_map/ppermute | solution.py:69
  154.3 12.0 %collective-permute-start.33 = (bf16[256,1024]{1,0:T(8,128)(2,1)S(1)}, bf16[256,1024]{1,0:T(8,128)(2,1)S(1)}, u32[]{:S(2)}, u32[]{:S(2)}) collective-permute-start(bf16[256,1024]{1,0:T(8,128)(2,1)S(1)} %get-tuple-element.103), channel_id=1, source_target_pairs={{1,0},{0,1},{3,2},{2,3},{5,4},{4,5},{7,6},{6,7},{9,8},{8,9},{11,10... | collective-permute-start | bytes 1572872 | tf_op jit(solution)/shard_map/ppermute | solution.py:91
  164.8 13.1 %collective-permute-start.31 = (bf16[128,1024]{1,0:T(8,128)(2,1)S(1)}, bf16[128,1024]{1,0:T(8,128)(2,1)S(1)}, u32[]{:S(2)}, u32[]{:S(2)}) collective-permute-start(bf16[128,1024]{1,0:T(8,128)(2,1)S(1)} %get-tuple-element.97), channel_id=1, source_target_pairs={{1,0},{0,1},{3,2},{2,3},{5,4},{4,5},{7,6},{6,7},{9,8},{8,9},{11,10... | collective-permute-start | bytes 786440 | tf_op jit(solution)/shard_map/ppermute | solution.py:91
  166.5 7.6 %collective-permute-start.34 = (bf16[128,1024]{1,0:T(8,128)(2,1)S(1)}, bf16[128,1024]{1,0:T(8,128)(2,1)S(1)}, u32[]{:S(2)}, u32[]{:S(2)}) collective-permute-start(bf16[128,1024]{1,0:T(8,128)(2,1)S(1)} %get-tuple-element.116), channel_id=1, source_target_pairs={{8,16},{10,18},{16,24},{18,26},{24,28},{26,30},{28,20},{30,22},{20... | collective-permute-start | bytes 786440 | tf_op jit(solution)/shard_map/ppermute | solution.py:69
  167.7 7.7 %collective-permute-start.37 = (bf16[128,1024]{1,0:T(8,128)(2,1)S(1)}, bf16[128,1024]{1,0:T(8,128)(2,1)S(1)}, u32[]{:S(2)}, u32[]{:S(2)}) collective-permute-start(bf16[128,1024]{1,0:T(8,128)(2,1)S(1)} %get-tuple-element.117), channel_id=1, source_target_pairs={{8,0},{10,2},{16,8},{18,10},{24,16},{26,18},{28,24},{30,26},{20,28... | collective-permute-start | bytes 786440 | tf_op jit(solution)/shard_map/ppermute | solution.py:69
  175.6 11.1 %collective-permute-start.35 = (bf16[128,1024]{1,0:T(8,128)(2,1)S(1)}, bf16[128,1024]{1,0:T(8,128)(2,1)S(1)}, u32[]{:S(2)}, u32[]{:S(2)}) collective-permute-start(bf16[128,1024]{1,0:T(8,128)(2,1)S(1)} %get-tuple-element.114), channel_id=1, source_target_pairs={{8,16},{10,18},{16,24},{18,26},{24,28},{26,30},{28,20},{30,22},{20... | collective-permute-start | bytes 786440 | tf_op jit(solution)/shard_map/ppermute | solution.py:69
  176.7 10.3 %collective-permute-start.38 = (bf16[128,1024]{1,0:T(8,128)(2,1)S(1)}, bf16[128,1024]{1,0:T(8,128)(2,1)S(1)}, u32[]{:S(2)}, u32[]{:S(2)}) collective-permute-start(bf16[128,1024]{1,0:T(8,128)(2,1)S(1)} %get-tuple-element.115), channel_id=1, source_target_pairs={{8,0},{10,2},{16,8},{18,10},{24,16},{26,18},{28,24},{30,26},{20,28... | collective-permute-start | bytes 786440 | tf_op jit(solution)/shard_map/ppermute | solution.py:69
  177.8 17.3 %copy-start.8 = (bf16[128,1024]{1,0:T(8,128)(2,1)S(1)}, bf16[128,1024]{1,0:T(8,128)(2,1)}, u32[]{:S(2)}) copy-start(bf16[128,1024]{1,0:T(8,128)(2,1)} %copy-done.7) | copy-start | bytes 786436
  177.9 22.6 %copy-start.18 = (f32[1024]{0:T(1024)S(1)}, f32[1024]{0:T(1024)}, u32[]{:S(2)}) copy-start(f32[1024]{0:T(1024)} %param.28) | copy-start | bytes 12292
  177.9 12.1 %collective-permute-start.32 = (bf16[128,1024]{1,0:T(8,128)(2,1)S(1)}, bf16[128,1024]{1,0:T(8,128)(2,1)S(1)}, u32[]{:S(2)}, u32[]{:S(2)}) collective-permute-start(bf16[128,1024]{1,0:T(8,128)(2,1)S(1)} %add_convert_fusion.2), channel_id=1, source_target_pairs={{8,20},{10,22},{16,12},{18,14},{24,4},{26,6},{28,0},{30,2},{20,8},... | collective-permute-start | bytes 786440 | tf_op jit(solution)/shard_map/ppermute | solution.py:69
  187.2 6.4 %collective-permute-start.36 = (bf16[128,1024]{1,0:T(8,128)(2,1)S(1)}, bf16[128,1024]{1,0:T(8,128)(2,1)S(1)}, u32[]{:S(2)}, u32[]{:S(2)}) collective-permute-start(bf16[128,1024]{1,0:T(8,128)(2,1)S(1)} %get-tuple-element.112), channel_id=1, source_target_pairs={{8,16},{10,18},{16,24},{18,26},{24,28},{26,30},{28,20},{30,22},{20... | collective-permute-start | bytes 786440 | tf_op jit(solution)/shard_map/ppermute | solution.py:69
  188.0 7.2 %collective-permute-start.39 = (bf16[128,1024]{1,0:T(8,128)(2,1)S(1)}, bf16[128,1024]{1,0:T(8,128)(2,1)S(1)}, u32[]{:S(2)}, u32[]{:S(2)}) collective-permute-start(bf16[128,1024]{1,0:T(8,128)(2,1)S(1)} %get-tuple-element.113), channel_id=1, source_target_pairs={{8,0},{10,2},{16,8},{18,10},{24,16},{26,18},{28,24},{30,26},{20,28... | collective-permute-start | bytes 786440 | tf_op jit(solution)/shard_map/ppermute | solution.py:69
  195.5 5.8 %copy-start.17 = (bf16[128,1024]{1,0:T(8,128)(2,1)}, bf16[128,1024]{1,0:T(8,128)(2,1)S(1)}, u32[]{:S(2)}) copy-start(bf16[128,1024]{1,0:T(8,128)(2,1)S(1)} %get-tuple-element.105) | copy-start | bytes 786436
where the time goes:
time: 202 us; the launch traced here: 201 us
  waiting for transfers between devices  57.5 us (28%)
  Pallas kernels  56.5 us (28%)
  starting transfers between devices  55.9 us (28%)
  local copies, waits for them, and re-layouts  20.9 us (10%)
  blocking collectives  4.94 us (2%)
  other arithmetic  4.5 us (2%)
    pallas_call x5, Pallas kernels, ffn(): pl.pallas_call(functools.partial(ffn_kernel, offsets, len(tokens), mp_cou...  49.2 us
    ppermute x22, waiting for transfers between devices, step(): return lax.ppermute(value, 'dp', pairs)  39.3 us
    ppermute x22, starting transfers between devices, step(): return lax.ppermute(value, 'dp', pairs)  36.5 us
    ppermute x11, waiting for transfers between devices, from_mp(): lax.ppermute(value, 'mp', [((i + k) % count, i) for i in range(count)])  15.8 us
    unnamed x44, local copies, waits for them, and re-layouts  14.8 us
    ppermute x11, starting transfers between devices, from_mp(): lax.ppermute(value, 'mp', [((i + k) % count, i) for i in range(count)])  12.1 us
    all_to_all x1, starting transfers between devices, local(): shared = lax.all_to_all(after(shared, swapped[0]), 'dp', 0, 0, tiled=True)  6.14 us
    psum x1, blocking collectives, local(): final_squares = lax.psum(jnp.sum(final_float * final_float, axis=1), 'mp')  4.94 us
  transfers between devices with their start and end apart: 41, of which 25 were waited for; matrix products, arithmetic and copies ran while one was open for 7% of the time, Pallas kernels for 28%

commit v1 on v0

--- a/solution.py
+++ b/solution.py
@@ -13,7 +13,7 @@
 CORES = 2
 LANES = 128
 VMEM_BYTES = 8 * 2**20
-FFN_VMEM = 16 * 2**20
+FFN_VMEM = 28 * 2**20
 
 
 def matmul(left, right):
@@ -82,6 +82,20 @@
                 b.append(value)
         return list(zip(ahead, behind))
 
+    def step_across(self, value, way, k):
+        count = self.chips
+        pairs = [
+            (
+                (self.cycle[i] * CORES + c) * self.mp_count + m,
+                (self.cycle[(i + way) % count] * CORES + c) * self.mp_count
+                + (m + k) % self.mp_count,
+            )
+            for i in range(count)
+            for c in range(CORES)
+            for m in range(self.mp_count)
+        ]
+        return lax.ppermute(value, ("dp", "mp"), pairs)
+
     def swap_core(self, value):
         count = self.chips * CORES
         return lax.ppermute(value, "dp", [(d, d ^ 1) for d in range(count)])
@@ -112,6 +126,10 @@
         lanes = round_up(shape[-1], LANES)
         size += np.prod(shape[:-1], dtype=np.int64) * lanes * jnp.dtype(dtype).itemsize
     return pltpu.CompilerParams(vmem_limit_bytes=max(VMEM_BYTES, 2 * int(size)))
+
+
+def brief():
+    return pl.CostEstimate(flops=1, bytes_accessed=1, transcendentals=0)
 
 
 def project_kernel(at, blocks, *refs):
@@ -135,12 +153,37 @@
         out_specs=[vmem()] * 2,
         input_output_aliases={first + i: i for i in range(len(given))},
         compiler_params=params(),
-        cost_estimate=pl.CostEstimate(
-            flops=4 * left.size * shape[2] * len(blocks),
-            bytes_accessed=2 * blocks[0].size * len(blocks),
-            transcendentals=0,
-        ),
+        cost_estimate=brief(),
     )(left, other, *blocks, *given)
+
+
+def deal_kernel(gate_ref, up_ref, down_ref, thirds_ref, out_ref):
+    count = out_ref.shape[0]
+    units = down_ref.shape[0] // count
+    gate = gate_ref[...].astype(jnp.float32).T
+    up = up_ref[...].astype(jnp.float32).T
+    down = down_ref[...].astype(jnp.float32)
+    for i in range(count):
+        at = slice(i * units, (i + 1) * units)
+        listed = [gate[at], up[at], down[at], thirds_ref[i]]
+        out_ref[i] = jnp.concatenate(listed, axis=0).astype(out_ref.dtype)
+
+
+def deal(gate, up, down, thirds):
+    count, extra, wide = thirds.shape
+    units = down.shape[0] // count
+    rows = 3 * units + extra
+    if units % 8 or extra % 8 or rows % 16 or wide % LANES:
+        parts = [part.reshape(count, units, wide) for part in (gate.T, up.T, down)]
+        return jnp.concatenate([*parts, thirds.astype(gate.dtype)], axis=1)
+    return pl.pallas_call(
+        deal_kernel,
+        out_shape=jax.ShapeDtypeStruct((count, rows, wide), gate.dtype),
+        in_specs=[vmem()] * 4,
+        out_specs=vmem(),
+        compiler_params=params(*[((4 * gate.shape[1], wide), jnp.float32)]),
+        cost_estimate=brief(),
+    )(gate, up, down, thirds)
 
 
 def norm_kernel(offsets, mp_count, info_ref, *refs):
@@ -212,14 +255,19 @@
         compiler_params=params(
             ((count, rows, width), jnp.float32), *[(stack.shape, stack.dtype) for stack in stacks]
         ),
+        cost_estimate=brief(),
     )(info, *stacks, *residuals, *gains)
 
 
 def ffn_kernel(offsets, pieces, mp_count, info_ref, *refs):
     scores, refs = refs[:2], refs[2:]
     tokens, refs = refs[:pieces], refs[pieces:]
-    held, refs = refs[:9], refs[9:]
-    outs, (rows_ref, act_ref, shared_act_ref) = refs[:mp_count], refs[mp_count:]
+    near, far, refs = refs[:6], refs[6:9], refs[9:]
+    outs, refs = refs[:mp_count], refs[mp_count:]
+    rows_ref, act_ref, shared_act_ref, sems, *held = refs
+    copies = [pltpu.make_async_copy(far[i], held[i], sems.at[i]) for i in range(3)]
+    for copy in copies:
+        copy.start()
     at = 0
     for token_ref in tokens:
         rows_ref[pl.ds(at, token_ref.shape[0]), :] = token_ref[...]
@@ -231,30 +279,30 @@
         wide = [scores[e][pl.ds(device, 1), :] for device in devices]
         wide = jnp.broadcast_to(jnp.concatenate(wide, axis=1), (8, at))
         turned.append(wide.T[:, :1])
-    for e in range(3):
-        gate = matmul_nt(rows_ref[...], held[2 * e][...])
-        up = matmul_nt(rows_ref[...], held[2 * e + 1][...])
+    for gate_ref, up_ref, e in ((near[0], near[1], 0), (near[3], near[4], None), (*held[:2], 1)):
+        if e == 1:
+            copies[0].wait()
+            copies[1].wait()
+        gate = matmul_nt(rows_ref[...], gate_ref[...])
+        up = matmul_nt(rows_ref[...], up_ref[...])
         act = gate / (1.0 + jnp.exp(-gate)) * up
-        if e < 2:
+        if e is None:
+            shared_act_ref[...] = act.astype(shared_act_ref.dtype)
+        else:
             act_ref[e] = (act * turned[e]).astype(act_ref.dtype)
-        else:
-            shared_act_ref[...] = act.astype(shared_act_ref.dtype)
+    copies[2].wait()
     half = outs[0].shape[1]
     width = 256 if half % 256 == 0 else half
     mp = info_ref[info_ref.shape[0] - 1]
     for k in range(mp_count):
         start = lax.rem(mp + k, mp_count) * half
 
-        def columns(j, carry, k=k, start=start):
+        for j in range(half // width):
             at = pl.ds(pl.multiple_of(start + j * width, LANES), width)
-            total = matmul(act_ref[0], held[6][:, at])
-            total += matmul(act_ref[1], held[7][:, at])
-            total += matmul(shared_act_ref[...], held[8][:, at])
-            to = pl.ds(pl.multiple_of(j * width, LANES), width)
-            outs[k][:, to] = total.astype(outs[k].dtype)
-            return carry
-
-        lax.fori_loop(0, half // width, columns, 0)
+            total = matmul(act_ref[0], near[2][:, at])
+            total += matmul(act_ref[1], held[2][:, at])
+            total += matmul(shared_act_ref[...], near[5][:, at])
+            outs[k][:, j * width : (j + 1) * width] = total.astype(outs[k].dtype)
 
 
 def ffn(offsets, tokens, scores, weights, info, mp_count):
@@ -268,19 +316,19 @@
             jax.ShapeDtypeStruct((total, half), jnp.float32 if k == 0 else jnp.bfloat16)
             for k in range(mp_count)
         ],
-        in_specs=[smem()] + [vmem()] * (2 + len(tokens) + len(weights)),
+        in_specs=[smem()]
+        + [vmem()] * (2 + len(tokens) + 6)
+        + [pl.BlockSpec(memory_space=pl.ANY)] * 3,
         out_specs=[vmem()] * mp_count,
         scratch_shapes=[
             pltpu.VMEM((total, width), jnp.bfloat16),
             pltpu.VMEM((2, total, hidden_units), jnp.bfloat16),
-            pltpu.VMEM((total, weights[4].shape[0]), jnp.bfloat16),
-        ],
+            pltpu.VMEM((total, weights[3].shape[0]), jnp.bfloat16),
+            pltpu.SemaphoreType.DMA((3,)),
+        ]
+        + [pltpu.VMEM(w.shape, w.dtype) for w in weights[6:]],
         compiler_params=pltpu.CompilerParams(vmem_limit_bytes=FFN_VMEM),
-        cost_estimate=pl.CostEstimate(
-            flops=2 * total * sum(w.size for w in weights),
-            bytes_accessed=2 * sum(w.size for w in weights),
-            transcendentals=0,
-        ),
+        cost_estimate=brief(),
     )(info, *scores, *tokens, *weights)
 
 
@@ -320,26 +368,17 @@
 
     units = shared_gate.shape[1] // dp_count
     wide = shared_gate.shape[0]
-    dealt = [
-        shared_gate.T.reshape(dp_count, units, wide),
-        shared_up.T.reshape(dp_count, units, wide),
-        shared_down.reshape(dp_count, units, wide),
-    ]
     rest = own_scores
     thirds = []
     for _ in range(3):
-        third = lax.reduce_precision(rest, 8, 7)
-        thirds.append(third.astype(bf16))
-        rest = rest - third
+        thirds.append(lax.reduce_precision(rest, 8, 7))
+        rest = rest - thirds[-1]
     thirds = jnp.stack(thirds, axis=1).reshape(dp_count, 3 * rows // wide, wide)
     used = 3 * units + thirds.shape[1]
-    shared, at = 0, 0
-    for part in (*dealt, thirds):
-        over = round_up(used, 16) - at - part.shape[1]
-        shared = shared + jnp.pad(part, ((0, 0), (at, over), (0, 0)))
-        at += part.shape[1]
+    thirds = jnp.pad(thirds, ((0, 0), (0, round_up(used, 16) - used), (0, 0)))
+    shared = deal(shared_gate, shared_up, shared_down, thirds)
+
     mine = [expert_gate[0].T, expert_up[0].T, expert_down[0]]
-    other = [moves.swap_core(w) for w in mine]
     other_attention = moves.swap_core(attention)
     residuals = moves.all_mp(residual)
     gains = moves.all_mp(ffn_gain.reshape(1, half))
@@ -369,16 +408,14 @@
             moved.append(moves.step(behind, -1))
         ties = []
         if s == left - 1:
-            ties = [shared, *other]
-        if s == left:
-            ties = [*residuals[1:], *gains[1:]]
+            ties = [shared, *residuals[1:], *gains[1:]]
         if s > 1:
             ties += sums
         moved, ties = lax.optimization_barrier((moved, ties))
         if s > 1:
             sums = ties[-2:]
         if s == left - 1:
-            shared, *other = ties[:-2]
+            shared = ties[0]
         ahead = moved[0]
         arrived.append(ahead)
         listed.append(-s)
@@ -386,7 +423,8 @@
             behind = moved[1]
             arrived.append(behind)
             listed.append(s)
-    shared = lax.all_to_all(after(shared, swapped[0]), "dp", 0, 0, tiled=True)
+    shared = lax.all_to_all(after(shared, ahead, stacks[0][-1]), "dp", 0, 0, tiled=True)
+    other = [moves.swap_core(after(w, ahead)) for w in mine]
     exchange(listed, *project(attention, other_attention, arrived, 0, len(arrived)))
     normed, own_hidden = norm(
         info, offsets, [piece for stack in stacks for piece in stack], residuals, gains
@@ -398,9 +436,7 @@
     for i in range(3):
         part = [value[i * units : (i + 1) * units].reshape(units, D) for value in shared]
         parts.append(jnp.pad(jnp.concatenate(part), ((0, spare), (0, 0))))
-    weights = [
-        mine[0], mine[1], other[0], other[1], parts[0], parts[1], mine[2], other[2], parts[2]
-    ]
+    weights = [*mine, *parts, *other]
     scores = []
     for value in shared:
         thirds = value[3 * units : used].transpose(1, 0, 2).reshape(dp_count, 3, rows)
@@ -413,39 +449,47 @@
     listed, blocks = [0], [normed]
     done = []
     for s in range(1, left + 1):
-        kept, *sent = ffn(listed, blocks, scores, weights, info, mp_count)
+        outs = list(ffn(listed, blocks, scores, weights, info, mp_count))
+        done.append([listed, outs, None])
         if s <= right:
             moved = [moves.step(ahead, 1), moves.step(behind, -1)]
         else:
             moved = [moves.step(ahead[: rows // 2], 1), moves.step(behind[rows // 2 :], -1)]
-        came = done[-1][2] if done else []
-        moved, sent, came = lax.optimization_barrier((moved, sent, came))
-        if done:
-            done[-1][2] = came
-        done.append([listed, kept, swap_mp(sent)])
+        came = done[-2][2] if s >= 2 else []
+        moved, ties, came = lax.optimization_barrier((moved, outs[1:], came))
+        if s >= 2:
+            done[-2][2] = came
+        done[-1][2] = swap_mp(ties)
         ahead, behind = blocks = moved
         listed = [-s, s] if s <= right else [s]
-    kept, *sent = ffn(listed, blocks, scores, weights, info, mp_count)
-    done.append([listed, kept, swap_mp(sent)])
-    parts = {}
-    for listed, kept, came in done:
-        for value in came:
+    done.append([listed, ffn(listed, blocks, scores, weights, info, mp_count), None])
+    parts, whole = {}, {}
+    for listed, (kept, *sent), came in done:
+        if right in listed:
+            for i, offset in enumerate(listed):
+                whole[offset] = [value[i * rows : (i + 1) * rows] for value in (kept, *sent)]
+            continue
+        for value in swap_mp(sent) if came is None else came:
             kept = kept + value.astype(f32)
         for i, offset in enumerate(listed):
-            parts[offset % chips] = kept[i * rows : (i + 1) * rows]
-
+            parts[offset] = kept[i * rows : (i + 1) * rows]
+
+    carried = []
+    for way in (1, -1):
+        kept, *sent = whole[way * right]
+        came = [moves.step(kept.astype(bf16), way)]
+        came += [moves.step_across(value, way, k + 1) for k, value in enumerate(sent)]
+        for s in range(right - 1, 0, -1):
+            part = parts[way * s]
+            for value in came:
+                part = part + value.astype(f32)
+            came = [moves.step(part.astype(bf16), way)]
+        carried += came
     mixture = parts[0]
     if left > right:
-        mixture = mixture + moves.step(parts[left].astype(bf16), left).astype(f32)
-    for way in (1, -1):
-        carried = None
-        for s in range(right, 0, -1):
-            part = parts[way * s % chips]
-            if carried is not None:
-                part = part + carried.astype(f32)
-            carried = moves.step(part.astype(bf16), way)
-        if carried is not None:
-            mixture = mixture + carried.astype(f32)
+        carried.append(moves.step(parts[left].astype(bf16), left))
+    for value in carried:
+        mixture = mixture + value.astype(f32)
 
     final = (own_hidden.astype(f32) + mixture).astype(bf16)
     final_float = final.astype(f32)

time: 202 us -> 171 us (0.85)
  waiting for transfers between devices: 57.5 us -> 40.5 us
  local copies, waits for them, and re-layouts: 20.9 us -> 15 us
  Pallas kernels: 56.5 us -> 51.3 us
  starting transfers between devices: 55.9 us -> 53.4 us
    ppermute x22, waiting for transfers between devices: 39.3 us -> 28.4 us  [step(): return lax.ppermute(value, 'dp', pairs)]
    ppermute x11 -> x10, waiting for transfers between devices: 15.8 us -> 6.38 us  [from_mp(): lax.ppermute(value, 'mp', [((i + k) % count, i) for i in range(count)])]
    reshape x3 -> x0, local copies, waits for them, and re-layouts: 3.89 us -> none  [the longest x1 1.78 us: local(): shared_gate.T.reshape(dp_count, units, wide)]
    ppermute x22, starting transfers between devices: 36.5 us -> 32.9 us  [step(): return lax.ppermute(value, 'dp', pairs)]
    pallas_call x5, Pallas kernels: 49.2 us -> 45.7 us  [ffn(): pl.pallas_call(functools.partial(ffn_kernel, offsets, len(tokens), mp_cou...]
    all_to_all x1, waiting for transfers between devices: 0.01 us -> 3.05 us  [local(): lax.all_to_all(after(shared, ahead, stacks[0][-1]), 'dp', 0, 0, tiled=True)]
    ppermute x0 -> x2, starting transfers between devices: none -> 2.98 us  [step_across(): return lax.ppermute(value, ('dp', 'mp'), pairs)]
    pallas_call x4, Pallas kernels: 3.76 us -> 1.69 us  [project(): pl.pallas_call(functools.partial(project_kernel, at, len(blocks)), out_sh...]
  transfers between devices with their start and end apart: 41 -> 42, of which waited for: 25 -> 22; matrix products, arithmetic and copies ran while one was open for 7% -> 3% of each run, Pallas kernels for 28% -> 30%
where the time goes in v1:
time: 171 us
  starting transfers between devices  53.4 us (31%)
  Pallas kernels  51.3 us (30%)
  waiting for transfers between devices  40.5 us (24%)
  local copies, waits for them, and re-layouts  15 us (9%)
  blocking collectives  4.94 us (3%)
  other arithmetic  4.49 us (3%)
    pallas_call x5, Pallas kernels, ffn(): pl.pallas_call(functools.partial(ffn_kernel, offsets, len(tokens), mp_cou...  45.7 us
    ppermute x22, starting transfers between devices, step(): return lax.ppermute(value, 'dp', pairs)  32.9 us
    ppermute x22, waiting for transfers between devices, step(): return lax.ppermute(value, 'dp', pairs)  28.4 us
    unnamed x54, local copies, waits for them, and re-layouts  14.1 us
    ppermute x10, starting transfers between devices, from_mp(): lax.ppermute(value, 'mp', [((i + k) % count, i) for i in range(count)])  11.6 us
    ppermute x10, waiting for transfers between devices, from_mp(): lax.ppermute(value, 'mp', [((i + k) % count, i) for i in range(count)])  6.38 us
    psum x1, blocking collectives, local(): final_squares = lax.psum(jnp.sum(final_float * final_float, axis=1), 'mp')  4.94 us
    all_to_all x1, starting transfers between devices, local(): lax.all_to_all(after(shared, ahead, stacks[0][-1]), 'dp', 0, 0, tiled=True)  4.38 us
  transfers between devices with their start and end apart: 42, of which 22 were waited for; matrix products, arithmetic and copies ran while one was open for 3% of the time, Pallas kernels for 30%

profile of v1, /device:TPU:0, one launch (start us, length us, event | category | flops | bytes accessed | tf_op | source)
XLA Modules:
  0.0 170.7 jit_solution(4328233886629889694)
XLA Ops:
  0.6 3.1 %collective-permute-start.1 = (bf16[1024,128]{1,0:T(8,128)(2,1)}, bf16[1024,128]{1,0:T(8,128)(2,1)S(1)}, u32[]{:S(2)}, u32[]{:S(2)}) collective-permute-start(bf16[1024,128]{1,0:T(8,128)(2,1)} %refs_2_.1), channel_id=1, source_target_pairs={{8,16},{10,18},{16,24},{18,26},{24,28},{26,30},{28,20},{30,22},{20... | collective-permute-start | bytes 786440 | tf_op jit(solution)/shard_map/ppermute | solution.py:69
  3.7 6.4 %collective-permute-done.1.refs_3_ = bf16[1024,128]{1,0:T(8,128)(2,1)S(1)} collective-permute-done((bf16[1024,128]{1,0:T(8,128)(2,1)}, bf16[1024,128]{1,0:T(8,128)(2,1)S(1)}, u32[]{:S(2)}, u32[]{:S(2)}) %collective-permute-start.1) | collective-permute-done | bytes 262176 | tf_op jit(solution)/shard_map/ppermute | solution.py:69
  10.2 1.5 collective-permute-done.2.refs_4_
  11.7 1.6 collective-permute-start.3
  13.7 1.5 collective-permute-start.8
  15.7 0.8 select_reduce_fusion.1
  16.5 0.8 select_reduce_fusion
  17.3 0.9 copy-done.4
  18.3 0.9 copy-done.12
  19.8 1.6 collective-permute-start.5
  22.3 1.0 copy-done.3
  23.7 2.5 %collective-permute-done.5.refs_2_ = bf16[1024,128]{1,0:T(8,128)(2,1)S(1)} collective-permute-done((bf16[1024,128]{1,0:T(8,128)(2,1)S(1)}, bf16[1024,128]{1,0:T(8,128)(2,1)S(1)}, u32[]{:S(2)}, u32[]{:S(2)}) %collective-permute-start.5) | collective-permute-done | bytes 262176 | tf_op jit(solution)/shard_map/ppermute | solution.py:69
  26.2 1.6 collective-permute-done.6.refs_3_
  27.8 1.6 collective-permute-start.12
  30.5 1.5 collective-permute-start.9
  32.7 1.5 collective-permute-done.12.refs_2_
  34.9 1.6 collective-permute-done.9.refs_1_
  37.2 4.4 %all-to-all-start = ((bf16[16,272,128]{2,1,0:T(8,128)(2,1)}), bf16[16,272,128]{2,1,0:T(8,128)(2,1)}, u32[]{:S(2)}, u32[]{:S(2)}) async-start(bf16[16,272,128]{2,1,0:T(8,128)(2,1)} %copy-done.3), calls=%async_computation | async-start | bytes 2228224 | tf_op jit(solution)/shard_map/all_to_all | solution.py:426
  41.8 1.7 collective-permute-done.10.refs_2_
  43.5 1.5 collective-permute-start.11
  45.0 0.9 copy-done.16
  47.5 0.9 collective-permute-start.15
  49.6 2.8 %collective-permute-done.13.refs_5_ = bf16[1,128,128]{2,1,0:T(8,128)(2,1)S(1)} collective-permute-done((bf16[1,128,128]{2,1,0:T(8,128)(2,1)S(1)}, bf16[1,128,128]{2,1,0:T(8,128)(2,1)S(1)}, u32[]{:S(2)}, u32[]{:S(2)}) %collective-permute-start.13) | collective-permute-done | bytes 32800 | tf_op jit(solution)/shard_map/ppermute | solution.py:105
  52.8 0.9 copy-done.7
  53.7 0.9 copy-done.17
  54.7 0.9 copy-done.19
  55.6 0.9 copy-done.21
  56.5 3.6 %shard_map.163 = (bf16[128,2048]{1,0:T(8,128)(2,1)}, bf16[128,1024]{1,0:T(8,128)(2,1)S(1)}) custom-call(s32[10]{0:T(128)S(1)} %dynamic-slice_bitcast_fusion.info_ref, bf16[7,128,128]{2,1,0:T(8,128)(2,1)S(1)} %copy-done.7, bf16[7,128,128]{2,1,0:T(8,128)(2,1)S(1)} %copy-done.21, bf16[7,128,128]{2,1,0:T(8,128)(2,1)} %collective-permute-done.10.refs_2_, ...), custom_call_target="tpu_custom_call" | custom-call | flops 1 | bytes 1 | tf_op jit(solution)/shard_map/pallas_call | solution.py:237
  60.9 1.7 collective-permute-start.21
  62.5 3.0 %all-to-all-done = bf16[16,272,128]{2,1,0:T(8,128)(2,1)} async-done(((bf16[16,272,128]{2,1,0:T(8,128)(2,1)}), bf16[16,272,128]{2,1,0:T(8,128)(2,1)}, u32[]{:S(2)}, u32[]{:S(2)}) %all-to-all-start) | async-done | bytes 1114144 | tf_op jit(solution)/shard_map/all_to_all | solution.py:426
  65.6 0.7 collective-permute-start.16
  66.3 1.3 slice_bitcast_fusion.1
  67.6 0.8 convert_reduce_fusion.1.refs_0_
  68.9 3.6 %collective-permute-start.20 = (bf16[128,2048]{1,0:T(8,128)(2,1)}, bf16[128,2048]{1,0:T(8,128)(2,1)S(1)}, u32[]{:S(2)}, u32[]{:S(2)}) collective-permute-start(bf16[128,2048]{1,0:T(8,128)(2,1)} %get-tuple-element.74.refs_2_), channel_id=1, source_target_pairs={{8,16},{10,18},{16,24},{18,26},{24,28},{26,30},{28,20},{30,22},{20... | collective-permute-start | bytes 1572872 | tf_op jit(solution)/shard_map/ppermute | solution.py:69
  72.7 1.6 copy-done.1
  74.3 9.0 %shard_map.164 = (f32[128,1024]{1,0:T(8,128)S(1)}, bf16[128,1024]{1,0:T(8,128)(2,1)S(1)}) custom-call(s32[10]{0:T(128)S(1)} %dynamic-slice_bitcast_fusion.info_ref, f32[16,128]{1,0:T(8,128)S(1)} %convert_reduce_fusion.1.refs_0_, f32[16,128]{1,0:T(8,128)S(1)} %convert_reduce_fusion.refs_1_, bf16[128,2048]{1,0:T(8,128)(2,1)} %get-tuple-element.74.refs_2_, ...), custom_call_target="tpu_custom_call" | custom-call | flops 1 | bytes 1 | tf_op jit(solution)/shard_map/pallas_call | solution.py:313
  83.3 1.2 collective-permute-done.20.refs_2_
  84.5 2.4 %collective-permute-start.22 = (bf16[128,2048]{1,0:T(8,128)(2,1)S(1)}, bf16[128,2048]{1,0:T(8,128)(2,1)S(1)}, u32[]{:S(2)}, u32[]{:S(2)}) collective-permute-start(bf16[128,2048]{1,0:T(8,128)(2,1)S(1)} %collective-permute-done.20.refs_2_), channel_id=1, source_target_pairs={{8,16},{10,18},{16,24},{18,26},{24,28},{26,30},{28,20},{30,22},{20... | collective-permute-start | bytes 1572872 | tf_op jit(solution)/shard_map/ppermute | solution.py:69
  87.2 1.5 collective-permute-start.24
  88.7 9.4 %shard_map.165 = (f32[256,1024]{1,0:T(8,128)S(1)}, bf16[256,1024]{1,0:T(8,128)(2,1)S(1)}) custom-call(s32[10]{0:T(128)S(1)} %dynamic-slice_bitcast_fusion.info_ref, f32[16,128]{1,0:T(8,128)S(1)} %convert_reduce_fusion.1.refs_0_, f32[16,128]{1,0:T(8,128)S(1)} %convert_reduce_fusion.refs_1_, bf16[128,2048]{1,0:T(8,128)(2,1)S(1)} %collective-permute-done.20.refs_2_, ...), custom_call_target="tpu_custom_call" | custom-call | flops 1 | bytes 1 | tf_op jit(solution)/shard_map/pallas_call | solution.py:313
  98.1 1.0 collective-permute-done.22.refs_2_
  99.0 1.2 collective-permute-done.23.refs_3_
  100.2 1.5 collective-permute-start.27
  101.7 1.7 %collective-permute-start.25 = (bf16[128,2048]{1,0:T(8,128)(2,1)S(1)}, bf16[128,2048]{1,0:T(8,128)(2,1)S(1)}, u32[]{:S(2)}, u32[]{:S(2)}) collective-permute-start(bf16[128,2048]{1,0:T(8,128)(2,1)S(1)} %collective-permute-done.22.refs_2_), channel_id=1, source_target_pairs={{8,16},{10,18},{16,24},{18,26},{24,28},{26,30},{28,20},{30,22},{20... | collective-permute-start | bytes 1572872 | tf_op jit(solution)/shard_map/ppermute | solution.py:69
  103.8 9.4 %shard_map.166 = (f32[256,1024]{1,0:T(8,128)S(1)}, bf16[256,1024]{1,0:T(8,128)(2,1)S(1)}) custom-call(s32[10]{0:T(128)S(1)} %dynamic-slice_bitcast_fusion.info_ref, f32[16,128]{1,0:T(8,128)S(1)} %convert_reduce_fusion.1.refs_0_, f32[16,128]{1,0:T(8,128)S(1)} %convert_reduce_fusion.refs_1_, bf16[128,2048]{1,0:T(8,128)(2,1)S(1)} %collective-permute-done.22.refs_2_, ...), custom_call_target="tpu_custom_call" | custom-call | flops 1 | bytes 1 | tf_op jit(solution)/shard_map/pallas_call | solution.py:313
  113.7 1.5 collective-permute-done.26.refs_3_
  116.0 1.5 collective-permute-start.28
  117.5 9.4 %shard_map.167 = (f32[256,1024]{1,0:T(8,128)S(1)}, bf16[256,1024]{1,0:T(8,128)(2,1)S(1)}) custom-call(s32[10]{0:T(128)S(1)} %dynamic-slice_bitcast_fusion.info_ref, f32[16,128]{1,0:T(8,128)S(1)} %convert_reduce_fusion.1.refs_0_, f32[16,128]{1,0:T(8,128)S(1)} %convert_reduce_fusion.refs_1_, bf16[128,2048]{1,0:T(8,128)(2,1)S(1)} %collective-permute-done.25.refs_2_, ...), custom_call_target="tpu_custom_call" | custom-call | flops 1 | bytes 1 | tf_op jit(solution)/shard_map/pallas_call | solution.py:313
  127.0 1.0 collective-permute-start.31
  128.0 1.1 collective-permute-start.35
  129.2 1.9 %collective-permute-start.32 = (bf16[128,1024]{1,0:T(8,128)(2,1)S(1)}, bf16[128,1024]{1,0:T(8,128)(2,1)S(1)}, u32[]{:S(2)}, u32[]{:S(2)}) collective-permute-start(bf16[128,1024]{1,0:T(8,128)(2,1)S(1)} %get-tuple-element.116), channel_id=1, source_target_pairs={{8,17},{9,16},{10,19},{11,18},{16,25},{17,24},{18,27},{19,26},{24,... | collective-permute-start | bytes 786440 | tf_op jit(solution)/shard_map/ppermute | solution.py:97
  131.1 1.0 collective-permute-start.36
  132.2 8.5 %shard_map.168 = (f32[128,1024]{1,0:T(8,128)S(1)}, bf16[128,1024]{1,0:T(8,128)(2,1)S(1)}) custom-call(s32[10]{0:T(128)S(1)} %dynamic-slice_bitcast_fusion.info_ref, f32[16,128]{1,0:T(8,128)S(1)} %convert_reduce_fusion.1.refs_0_, f32[16,128]{1,0:T(8,128)S(1)} %convert_reduce_fusion.refs_1_, bf16[64,2048]{1,0:T(8,128)(2,1)S(1)} %collective-permute-done.28.refs_2_, ...), custom_call_target="tpu_custom_call" | custom-call | flops 1 | bytes 1 | tf_op jit(solution)/shard_map/pallas_call | solution.py:313
  140.7 1.9 %collective-permute-start.39 = (bf16[128,1024]{1,0:T(8,128)(2,1)S(1)}, bf16[128,1024]{1,0:T(8,128)(2,1)S(1)}, u32[]{:S(2)}, u32[]{:S(2)}) collective-permute-start(bf16[128,1024]{1,0:T(8,128)(2,1)S(1)} %get-tuple-element.101), channel_id=1, source_target_pairs={{1,0},{0,1},{3,2},{2,3},{5,4},{4,5},{7,6},{6,7},{9,8},{8,9},{11,10... | collective-permute-start | bytes 786440 | tf_op jit(solution)/shard_map/ppermute | solution.py:105
  143.7 1.6 collective-permute-start.37
  145.5 1.6 collective-permute-done.39
  147.2 2.7 %collective-permute-start.40 = (bf16[128,1024]{1,0:T(8,128)(2,1)S(1)}, bf16[128,1024]{1,0:T(8,128)(2,1)S(1)}, u32[]{:S(2)}, u32[]{:S(2)}) collective-permute-start(bf16[128,1024]{1,0:T(8,128)(2,1)S(1)} %add_convert_fusion.1), channel_id=1, source_target_pairs={{8,20},{10,22},{16,12},{18,14},{24,4},{26,6},{28,0},{30,2},{20,8},... | collective-permute-start | bytes 786440 | tf_op jit(solution)/shard_map/ppermute | solution.py:69
  149.9 1.5 collective-permute-done.33
  151.4 3.7 %collective-permute-done.37 = bf16[128,1024]{1,0:T(8,128)(2,1)S(1)} collective-permute-done((bf16[128,1024]{1,0:T(8,128)(2,1)S(1)}, bf16[128,1024]{1,0:T(8,128)(2,1)S(1)}, u32[]{:S(2)}, u32[]{:S(2)}) %collective-permute-start.37) | collective-permute-done | bytes 262176 | tf_op jit(solution)/shard_map/ppermute | solution.py:69
  155.2 1.0 collective-permute-start.34
  156.2 4.1 %collective-permute-start.38 = (bf16[128,1024]{1,0:T(8,128)(2,1)S(1)}, bf16[128,1024]{1,0:T(8,128)(2,1)S(1)}, u32[]{:S(2)}, u32[]{:S(2)}) collective-permute-start(bf16[128,1024]{1,0:T(8,128)(2,1)S(1)} %get-tuple-element.111), channel_id=1, source_target_pairs={{8,0},{10,2},{16,8},{18,10},{24,16},{26,18},{28,24},{30,26},{20,28... | collective-permute-start | bytes 786440 | tf_op jit(solution)/shard_map/ppermute | solution.py:69
  160.3 4.3 %collective-permute-done.34 = bf16[128,1024]{1,0:T(8,128)(2,1)S(1)} collective-permute-done((bf16[128,1024]{1,0:T(8,128)(2,1)S(1)}, bf16[128,1024]{1,0:T(8,128)(2,1)S(1)}, u32[]{:S(2)}, u32[]{:S(2)}) %collective-permute-start.34) | collective-permute-done | bytes 262176 | tf_op jit(solution)/shard_map/ppermute | solution.py:69
  164.9 4.9 %psum.7 = f32[128]{0:T(128)S(1)} all-reduce(f32[128]{0:T(128)S(1)} %get-tuple-element.102), channel_id=1, replica_groups=mesh['dp'=16,'mp'=2] {'mp'}, use_global_device_ids=true, to_apply=%region_5.6 | all-reduce | flops 128 | bytes 1024 | tf_op jit(solution)/shard_map/psum | solution.py:496
  169.9 0.8 fusion.2
  (109 shorter events, 14.6 us)
Async XLA Ops:
  0.6 9.5 %collective-permute-start.1 = (bf16[1024,128]{1,0:T(8,128)(2,1)}, bf16[1024,128]{1,0:T(8,128)(2,1)S(1)}, u32[]{:S(2)}, u32[]{:S(2)}) collective-permute-start(bf16[1024,128]{1,0:T(8,128)(2,1)} %refs_2_.1), channel_id=1, source_target_pairs={{8,16},{10,18},{16,24},{18,26},{24,28},{26,30},{28,20},{30,22},{20... | collective-permute-start | bytes 786440 | tf_op jit(solution)/shard_map/ppermute | solution.py:69
  3.7 8.0 %collective-permute-start.2 = (bf16[1024,128]{1,0:T(8,128)(2,1)}, bf16[1024,128]{1,0:T(8,128)(2,1)S(1)}, u32[]{:S(2)}, u32[]{:S(2)}) collective-permute-start(bf16[1024,128]{1,0:T(8,128)(2,1)} %refs_2_.1), channel_id=1, source_target_pairs={{8,0},{10,2},{16,8},{18,10},{24,16},{26,18},{28,24},{30,26},{20,28... | collective-permute-start | bytes 786440 | tf_op jit(solution)/shard_map/ppermute | solution.py:69
  3.7 13.6 %collective-permute-start = (bf16[128,1024]{1,0:T(8,128)(2,1)}, bf16[128,1024]{1,0:T(8,128)(2,1)S(1)}, u32[]{:S(2)}, u32[]{:S(2)}) collective-permute-start(bf16[128,1024]{1,0:T(8,128)(2,1)} %refs_0_.7), channel_id=1, source_target_pairs={{0,2},{2,0},{4,6},{6,4},{8,10},{10,8},{12,14},{14,12},{16,18},{18,... | collective-permute-start | bytes 786440 | tf_op jit(solution)/shard_map/ppermute | solution.py:101
  11.7 8.1 %collective-permute-start.3 = (bf16[1024,128]{1,0:T(8,128)(2,1)S(1)}, bf16[1024,128]{1,0:T(8,128)(2,1)S(1)}, u32[]{:S(2)}, u32[]{:S(2)}) collective-permute-start(bf16[1024,128]{1,0:T(8,128)(2,1)S(1)} %collective-permute-done.1.refs_3_), channel_id=1, source_target_pairs={{8,16},{10,18},{16,24},{18,26},{24,28},{26,30},{28,20},{30,22},{20... | collective-permute-start | bytes 786440 | tf_op jit(solution)/shard_map/ppermute | solution.py:69
  13.3 6.6 %collective-permute-start.4 = (bf16[1024,128]{1,0:T(8,128)(2,1)S(1)}, bf16[1024,128]{1,0:T(8,128)(2,1)S(1)}, u32[]{:S(2)}, u32[]{:S(2)}) collective-permute-start(bf16[1024,128]{1,0:T(8,128)(2,1)S(1)} %collective-permute-done.2.refs_4_), channel_id=1, source_target_pairs={{8,0},{10,2},{16,8},{18,10},{24,16},{26,18},{28,24},{30,26},{20,28... | collective-permute-start | bytes 786440 | tf_op jit(solution)/shard_map/ppermute | solution.py:69
  13.7 10.0 %collective-permute-start.8 = (f32[1,1024]{1,0:T(1,128)}, f32[1,1024]{1,0:T(1,128)S(1)}, u32[]{:S(2)}, u32[]{:S(2)}) collective-permute-start(f32[1,1024]{1,0:T(1,128)} %bitcast.60), channel_id=1, source_target_pairs={{1,0},{0,1},{3,2},{2,3},{5,4},{4,5},{7,6},{6,7},{9,8},{8,9},{11,10... | collective-permute-start | bytes 12296 | tf_op jit(solution)/shard_map/ppermute | solution.py:105
  15.2 8.5 %collective-permute-start.7 = (bf16[128,1024]{1,0:T(8,128)(2,1)}, bf16[128,1024]{1,0:T(8,128)(2,1)S(1)}, u32[]{:S(2)}, u32[]{:S(2)}) collective-permute-start(bf16[128,1024]{1,0:T(8,128)(2,1)} %refs_8_.1), channel_id=1, source_target_pairs={{1,0},{0,1},{3,2},{2,3},{5,4},{4,5},{7,6},{6,7},{9,8},{8,9},{11,10... | collective-permute-start | bytes 786440 | tf_op jit(solution)/shard_map/ppermute | solution.py:105
  17.3 1.0 copy-start.4
  18.2 0.9 copy-start.12
  19.2 2.7 %copy-start.9 = (bf16[128,1408]{1,0:T(8,128)(2,1)S(1)}, bf16[128,1408]{1,0:T(8,128)(2,1)}, u32[]{:S(2)}) copy-start(bf16[128,1408]{1,0:T(8,128)(2,1)} %gate_ref.1) | copy-start | bytes 1081348
  19.2 2.7 %copy-start.10 = (bf16[128,1408]{1,0:T(8,128)(2,1)S(1)}, bf16[128,1408]{1,0:T(8,128)(2,1)}, u32[]{:S(2)}) copy-start(bf16[128,1408]{1,0:T(8,128)(2,1)} %up_ref.1) | copy-start | bytes 1081348
  19.2 2.7 %copy-start.11 = (bf16[1408,128]{1,0:T(8,128)(2,1)S(1)}, bf16[1408,128]{1,0:T(8,128)(2,1)}, u32[]{:S(2)}) copy-start(bf16[1408,128]{1,0:T(8,128)(2,1)} %down_ref.1) | copy-start | bytes 1081348
  19.8 6.4 %collective-permute-start.5 = (bf16[1024,128]{1,0:T(8,128)(2,1)S(1)}, bf16[1024,128]{1,0:T(8,128)(2,1)S(1)}, u32[]{:S(2)}, u32[]{:S(2)}) collective-permute-start(bf16[1024,128]{1,0:T(8,128)(2,1)S(1)} %collective-permute-done.3.refs_2_), channel_id=1, source_target_pairs={{8,16},{10,18},{16,24},{18,26},{24,28},{26,30},{28,20},{30,22},{20... | collective-permute-start | bytes 786440 | tf_op jit(solution)/shard_map/ppermute | solution.py:69
  21.4 6.4 %collective-permute-start.6 = (bf16[1024,128]{1,0:T(8,128)(2,1)S(1)}, bf16[1024,128]{1,0:T(8,128)(2,1)S(1)}, u32[]{:S(2)}, u32[]{:S(2)}) collective-permute-start(bf16[1024,128]{1,0:T(8,128)(2,1)S(1)} %collective-permute-done.4.refs_3_), channel_id=1, source_target_pairs={{8,0},{10,2},{16,8},{18,10},{24,16},{26,18},{28,24},{30,26},{20,28... | collective-permute-start | bytes 786440 | tf_op jit(solution)/shard_map/ppermute | solution.py:69
  21.9 1.3 copy-start.5
  22.2 1.0 copy-start.3
  23.7 10.5 %copy-start.18 = (bf16[128,1024]{1,0:T(8,128)(2,1)}, bf16[128,1024]{1,0:T(8,128)(2,1)S(1)}, u32[]{:S(2)}) copy-start(bf16[128,1024]{1,0:T(8,128)(2,1)S(1)} %collective-permute-done.7.refs_9_) | copy-start | bytes 786436
  27.8 6.4 %collective-permute-start.12 = (bf16[1024,128]{1,0:T(8,128)(2,1)S(1)}, bf16[1024,128]{1,0:T(8,128)(2,1)S(1)}, u32[]{:S(2)}, u32[]{:S(2)}) collective-permute-start(bf16[1024,128]{1,0:T(8,128)(2,1)S(1)} %collective-permute-done.5.refs_2_), channel_id=1, source_target_pairs={{8,16},{10,18},{16,24},{18,26},{24,28},{26,30},{28,20},{30,22},{20... | collective-permute-start | bytes 786440 | tf_op jit(solution)/shard_map/ppermute | solution.py:69
  29.4 23.4 %copy-start.22 = (f32[1024]{0:T(1024)S(1)}, f32[1024]{0:T(1024)}, u32[]{:S(2)}) copy-start(f32[1024]{0:T(1024)} %param.18) | copy-start | bytes 12292
  30.5 6.0 %collective-permute-start.9 = (bf16[7,128,128]{2,1,0:T(8,128)(2,1)S(1)}, bf16[7,128,128]{2,1,0:T(8,128)(2,1)S(1)}, u32[]{:S(2)}, u32[]{:S(2)}) collective-permute-start(bf16[7,128,128]{2,1,0:T(8,128)(2,1)S(1)} %get-tuple-element.66.refs_0_), channel_id=1, source_target_pairs={{1,0},{0,1},{3,2},{2,3},{5,4},{4,5},{7,6},{6,7},{9,8},{8,9},{11,10... | collective-permute-start | bytes 688136 | tf_op jit(solution)/shard_map/ppermute | solution.py:105
  34.2 0.7 copy-start.15
  34.9 14.2 %copy-start = (bf16[1,2048,704]{1,2,0:T(8,128)(2,1)S(1)}, bf16[1,2048,704]{1,2,0:T(8,128)(2,1)}, u32[]{:S(2)}) copy-start(bf16[1,2048,704]{1,2,0:T(8,128)(2,1)} %param.22) | copy-start | bytes 8650756
  37.2 28.4 %all-to-all-start = ((bf16[16,272,128]{2,1,0:T(8,128)(2,1)}), bf16[16,272,128]{2,1,0:T(8,128)(2,1)}, u32[]{:S(2)}, u32[]{:S(2)}) async-start(bf16[16,272,128]{2,1,0:T(8,128)(2,1)} %copy-done.3), calls=%async_computation | async-start | bytes 2228224 | tf_op jit(solution)/shard_map/all_to_all | solution.py:426
  41.6 1.9 %collective-permute-start.10 = (bf16[7,128,128]{2,1,0:T(8,128)(2,1)}, bf16[7,128,128]{2,1,0:T(8,128)(2,1)}, u32[]{:S(2)}, u32[]{:S(2)}) collective-permute-start(bf16[7,128,128]{2,1,0:T(8,128)(2,1)} %copy-done.8), channel_id=1, source_target_pairs={{0,2},{2,0},{4,6},{6,4},{8,10},{10,8},{12,14},{14,12},{16,18},{18,... | collective-permute-start | bytes 688136 | tf_op jit(solution)/shard_map/ppermute | solution.py:101
  43.5 9.3 %collective-permute-start.11 = (bf16[7,128,128]{2,1,0:T(8,128)(2,1)}, bf16[7,128,128]{2,1,0:T(8,128)(2,1)}, u32[]{:S(2)}, u32[]{:S(2)}) collective-permute-start(bf16[7,128,128]{2,1,0:T(8,128)(2,1)} %collective-permute-done.10.refs_2_), channel_id=1, source_target_pairs={{1,0},{0,1},{3,2},{2,3},{5,4},{4,5},{7,6},{6,7},{9,8},{8,9},{11,10... | collective-permute-start | bytes 688136 | tf_op jit(solution)/shard_map/ppermute | solution.py:105
  45.0 0.9 copy-start.16
  46.2 1.3 collective-permute-start.14
  46.3 6.1 %collective-permute-start.13 = (bf16[1,128,128]{2,1,0:T(8,128)(2,1)S(1)}, bf16[1,128,128]{2,1,0:T(8,128)(2,1)S(1)}, u32[]{:S(2)}, u32[]{:S(2)}) collective-permute-start(bf16[1,128,128]{2,1,0:T(8,128)(2,1)S(1)} %get-tuple-element.69.refs_4_), channel_id=1, source_target_pairs={{1,0},{0,1},{3,2},{2,3},{5,4},{4,5},{7,6},{6,7},{9,8},{8,9},{11,10... | collective-permute-start | bytes 98312 | tf_op jit(solution)/shard_map/ppermute | solution.py:105
  47.5 5.3 %collective-permute-start.15 = (bf16[1,128,128]{2,1,0:T(8,128)(2,1)S(1)}, bf16[1,128,128]{2,1,0:T(8,128)(2,1)S(1)}, u32[]{:S(2)}, u32[]{:S(2)}) collective-permute-start(bf16[1,128,128]{2,1,0:T(8,128)(2,1)S(1)} %collective-permute-done.14.refs_6_), channel_id=1, source_target_pairs={{1,0},{0,1},{3,2},{2,3},{5,4},{4,5},{7,6},{6,7},{9,8},{8,9},{11,10... | collective-permute-start | bytes 98312 | tf_op jit(solution)/shard_map/ppermute | solution.py:105
  49.1 23.6 %collective-permute-start.17 = (bf16[704,2048]{1,0:T(8,128)(2,1)S(1)}, bf16[704,2048]{1,0:T(8,128)(2,1)}, u32[]{:S(2)}, u32[]{:S(2)}) collective-permute-start(bf16[704,2048]{1,0:T(8,128)(2,1)S(1)} %bitcast.42), channel_id=1, source_target_pairs={{0,2},{2,0},{4,6},{6,4},{8,10},{10,8},{12,14},{14,12},{16,18},{18,... | collective-permute-start | bytes 8650760 | tf_op jit(solution)/shard_map/ppermute | solution.py:101
  49.1 23.6 %collective-permute-start.18 = (bf16[704,2048]{1,0:T(8,128)(2,1)}, bf16[704,2048]{1,0:T(8,128)(2,1)}, u32[]{:S(2)}, u32[]{:S(2)}) collective-permute-start(bf16[704,2048]{1,0:T(8,128)(2,1)} %bitcast.48), channel_id=1, source_target_pairs={{0,2},{2,0},{4,6},{6,4},{8,10},{10,8},{12,14},{14,12},{16,18},{18,... | collective-permute-start | bytes 8650760 | tf_op jit(solution)/shard_map/ppermute | solution.py:101
  52.4 20.3 %collective-permute-start.19 = (bf16[704,2048]{1,0:T(8,128)(2,1)}, bf16[704,2048]{1,0:T(8,128)(2,1)}, u32[]{:S(2)}, u32[]{:S(2)}) collective-permute-start(bf16[704,2048]{1,0:T(8,128)(2,1)} %bitcast.54), channel_id=1, source_target_pairs={{0,2},{2,0},{4,6},{6,4},{8,10},{10,8},{12,14},{14,12},{16,18},{18,... | collective-permute-start | bytes 8650760 | tf_op jit(solution)/shard_map/ppermute | solution.py:101
  52.8 0.9 copy-start.7
  53.7 0.9 copy-start.17
  54.7 0.9 copy-start.19
  55.6 0.9 copy-start.21
  60.2 0.7 copy-start.13
  60.9 22.4 %collective-permute-start.21 = (bf16[128,2048]{1,0:T(8,128)(2,1)}, bf16[128,2048]{1,0:T(8,128)(2,1)S(1)}, u32[]{:S(2)}, u32[]{:S(2)}) collective-permute-start(bf16[128,2048]{1,0:T(8,128)(2,1)} %get-tuple-element.74.refs_2_), channel_id=1, source_target_pairs={{8,0},{10,2},{16,8},{18,10},{24,16},{26,18},{28,24},{30,26},{20,28... | collective-permute-start | bytes 1572872 | tf_op jit(solution)/shard_map/ppermute | solution.py:69
  65.6 3.3 %collective-permute-start.16 = (bf16[272,16,128]{2,0,1:T(8,128)(2,1)}, bf16[272,16,128]{2,0,1:T(8,128)(2,1)S(1)}, u32[]{:S(2)}, u32[]{:S(2)}) collective-permute-start(bf16[272,16,128]{2,0,1:T(8,128)(2,1)} %bitcast.5), channel_id=1, source_target_pairs={{0,2},{2,0},{4,6},{6,4},{8,10},{10,8},{12,14},{14,12},{16,18},{18,... | collective-permute-start | bytes 3342344 | tf_op jit(solution)/shard_map/ppermute | solution.py:101
  68.4 4.3 %copy-start.2 = (bf16[1,704,2048]{2,1,0:T(8,128)(2,1)S(1)}, bf16[1,704,2048]{2,1,0:T(8,128)(2,1)}, u32[]{:S(2)}) copy-start(bf16[1,704,2048]{2,1,0:T(8,128)(2,1)} %param.24) | copy-start | bytes 8650756
  68.9 15.6 %collective-permute-start.20 = (bf16[128,2048]{1,0:T(8,128)(2,1)}, bf16[128,2048]{1,0:T(8,128)(2,1)S(1)}, u32[]{:S(2)}, u32[]{:S(2)}) collective-permute-start(bf16[128,2048]{1,0:T(8,128)(2,1)} %get-tuple-element.74.refs_2_), channel_id=1, source_target_pairs={{8,16},{10,18},{16,24},{18,26},{24,28},{26,30},{28,20},{30,22},{20... | collective-permute-start | bytes 1572872 | tf_op jit(solution)/shard_map/ppermute | solution.py:69
  72.5 1.8 %copy-start.1 = (bf16[1,2048,704]{1,2,0:T(8,128)(2,1)S(1)}, bf16[1,2048,704]{1,2,0:T(8,128)(2,1)}, u32[]{:S(2)}) copy-start(bf16[1,2048,704]{1,2,0:T(8,128)(2,1)} %param.23) | copy-start | bytes 8650756
  84.5 14.6 %collective-permute-start.22 = (bf16[128,2048]{1,0:T(8,128)(2,1)S(1)}, bf16[128,2048]{1,0:T(8,128)(2,1)S(1)}, u32[]{:S(2)}, u32[]{:S(2)}) collective-permute-start(bf16[128,2048]{1,0:T(8,128)(2,1)S(1)} %collective-permute-done.20.refs_2_), channel_id=1, source_target_pairs={{8,16},{10,18},{16,24},{18,26},{24,28},{26,30},{28,20},{30,22},{20... | collective-permute-start | bytes 1572872 | tf_op jit(solution)/shard_map/ppermute | solution.py:69
  86.9 13.4 %collective-permute-start.23 = (bf16[128,2048]{1,0:T(8,128)(2,1)S(1)}, bf16[128,2048]{1,0:T(8,128)(2,1)S(1)}, u32[]{:S(2)}, u32[]{:S(2)}) collective-permute-start(bf16[128,2048]{1,0:T(8,128)(2,1)S(1)} %collective-permute-done.21.refs_3_), channel_id=1, source_target_pairs={{8,0},{10,2},{16,8},{18,10},{24,16},{26,18},{28,24},{30,26},{20,28... | collective-permute-start | bytes 1572872 | tf_op jit(solution)/shard_map/ppermute | solution.py:69
  87.2 10.9 %collective-permute-start.24 = (bf16[128,1024]{1,0:T(8,128)(2,1)S(1)}, bf16[128,1024]{1,0:T(8,128)(2,1)S(1)}, u32[]{:S(2)}, u32[]{:S(2)}) collective-permute-start(bf16[128,1024]{1,0:T(8,128)(2,1)S(1)} %get-tuple-element.83), channel_id=1, source_target_pairs={{1,0},{0,1},{3,2},{2,3},{5,4},{4,5},{7,6},{6,7},{9,8},{8,9},{11,10... | collective-permute-start | bytes 786440 | tf_op jit(solution)/shard_map/ppermute | solution.py:105
  100.2 13.0 %collective-permute-start.27 = (bf16[256,1024]{1,0:T(8,128)(2,1)S(1)}, bf16[256,1024]{1,0:T(8,128)(2,1)S(1)}, u32[]{:S(2)}, u32[]{:S(2)}) collective-permute-start(bf16[256,1024]{1,0:T(8,128)(2,1)S(1)} %get-tuple-element.89), channel_id=1, source_target_pairs={{1,0},{0,1},{3,2},{2,3},{5,4},{4,5},{7,6},{6,7},{9,8},{8,9},{11,10... | collective-permute-start | bytes 1572872 | tf_op jit(solution)/shard_map/ppermute | solution.py:105
  101.7 11.9 %collective-permute-start.25 = (bf16[128,2048]{1,0:T(8,128)(2,1)S(1)}, bf16[128,2048]{1,0:T(8,128)(2,1)S(1)}, u32[]{:S(2)}, u32[]{:S(2)}) collective-permute-start(bf16[128,2048]{1,0:T(8,128)(2,1)S(1)} %collective-permute-done.22.refs_2_), channel_id=1, source_target_pairs={{8,16},{10,18},{16,24},{18,26},{24,28},{26,30},{28,20},{30,22},{20... | collective-permute-start | bytes 1572872 | tf_op jit(solution)/shard_map/ppermute | solution.py:69
  103.5 11.7 %collective-permute-start.26 = (bf16[128,2048]{1,0:T(8,128)(2,1)S(1)}, bf16[128,2048]{1,0:T(8,128)(2,1)S(1)}, u32[]{:S(2)}, u32[]{:S(2)}) collective-permute-start(bf16[128,2048]{1,0:T(8,128)(2,1)S(1)} %collective-permute-done.23.refs_3_), channel_id=1, source_target_pairs={{8,0},{10,2},{16,8},{18,10},{24,16},{26,18},{28,24},{30,26},{20,28... | collective-permute-start | bytes 1572872 | tf_op jit(solution)/shard_map/ppermute | solution.py:69
  115.2 17.0 %collective-permute-start.30 = (bf16[256,1024]{1,0:T(8,128)(2,1)S(1)}, bf16[256,1024]{1,0:T(8,128)(2,1)S(1)}, u32[]{:S(2)}, u32[]{:S(2)}) collective-permute-start(bf16[256,1024]{1,0:T(8,128)(2,1)S(1)} %get-tuple-element.95), channel_id=1, source_target_pairs={{1,0},{0,1},{3,2},{2,3},{5,4},{4,5},{7,6},{6,7},{9,8},{8,9},{11,10... | collective-permute-start | bytes 1572872 | tf_op jit(solution)/shard_map/ppermute | solution.py:105
  115.4 13.7 %collective-permute-start.29 = (bf16[64,2048]{1,0:T(8,128)(2,1)S(1)}, bf16[64,2048]{1,0:T(8,128)(2,1)S(1)}, u32[]{:S(2)}, u32[]{:S(2)}) collective-permute-start(bf16[64,2048]{1,0:T(8,128)(2,1)S(1)} %slice.66), channel_id=1, source_target_pairs={{8,0},{10,2},{16,8},{18,10},{24,16},{26,18},{28,24},{30,26},{20,28... | collective-permute-start | bytes 786440 | tf_op jit(solution)/shard_map/ppermute | solution.py:69
  116.0 15.1 %collective-permute-start.28 = (bf16[64,2048]{1,0:T(8,128)(2,1)S(1)}, bf16[64,2048]{1,0:T(8,128)(2,1)S(1)}, u32[]{:S(2)}, u32[]{:S(2)}) collective-permute-start(bf16[64,2048]{1,0:T(8,128)(2,1)S(1)} %slice.65), channel_id=1, source_target_pairs={{8,16},{10,18},{16,24},{18,26},{24,28},{26,30},{28,20},{30,22},{20... | collective-permute-start | bytes 786440 | tf_op jit(solution)/shard_map/ppermute | solution.py:69
  127.0 15.7 %collective-permute-start.31 = (bf16[128,1024]{1,0:T(8,128)(2,1)S(1)}, bf16[128,1024]{1,0:T(8,128)(2,1)S(1)}, u32[]{:S(2)}, u32[]{:S(2)}) collective-permute-start(bf16[128,1024]{1,0:T(8,128)(2,1)S(1)} %get-tuple-element.114), channel_id=1, source_target_pairs={{8,16},{10,18},{16,24},{18,26},{24,28},{26,30},{28,20},{30,22},{20... | collective-permute-start | bytes 786440 | tf_op jit(solution)/shard_map/ppermute | solution.py:69
  128.0 14.8 %collective-permute-start.35 = (bf16[128,1024]{1,0:T(8,128)(2,1)S(1)}, bf16[128,1024]{1,0:T(8,128)(2,1)S(1)}, u32[]{:S(2)}, u32[]{:S(2)}) collective-permute-start(bf16[128,1024]{1,0:T(8,128)(2,1)S(1)} %get-tuple-element.115), channel_id=1, source_target_pairs={{8,0},{10,2},{16,8},{18,10},{24,16},{26,18},{28,24},{30,26},{20,28... | collective-permute-start | bytes 786440 | tf_op jit(solution)/shard_map/ppermute | solution.py:69
  129.2 13.6 %collective-permute-start.32 = (bf16[128,1024]{1,0:T(8,128)(2,1)S(1)}, bf16[128,1024]{1,0:T(8,128)(2,1)S(1)}, u32[]{:S(2)}, u32[]{:S(2)}) collective-permute-start(bf16[128,1024]{1,0:T(8,128)(2,1)S(1)} %get-tuple-element.116), channel_id=1, source_target_pairs={{8,17},{9,16},{10,19},{11,18},{16,25},{17,24},{18,27},{19,26},{24,... | collective-permute-start | bytes 786440 | tf_op jit(solution)/shard_map/ppermute | solution.py:97
  131.1 11.7 %collective-permute-start.36 = (bf16[128,1024]{1,0:T(8,128)(2,1)S(1)}, bf16[128,1024]{1,0:T(8,128)(2,1)S(1)}, u32[]{:S(2)}, u32[]{:S(2)}) collective-permute-start(bf16[128,1024]{1,0:T(8,128)(2,1)S(1)} %get-tuple-element.117), channel_id=1, source_target_pairs={{8,1},{9,0},{10,3},{11,2},{16,9},{17,8},{18,11},{19,10},{24,17},{2... | collective-permute-start | bytes 786440 | tf_op jit(solution)/shard_map/ppermute | solution.py:97
  140.7 6.4 %collective-permute-start.39 = (bf16[128,1024]{1,0:T(8,128)(2,1)S(1)}, bf16[128,1024]{1,0:T(8,128)(2,1)S(1)}, u32[]{:S(2)}, u32[]{:S(2)}) collective-permute-start(bf16[128,1024]{1,0:T(8,128)(2,1)S(1)} %get-tuple-element.101), channel_id=1, source_target_pairs={{1,0},{0,1},{3,2},{2,3},{5,4},{4,5},{7,6},{6,7},{9,8},{8,9},{11,10... | collective-permute-start | bytes 786440 | tf_op jit(solution)/shard_map/ppermute | solution.py:105
  143.1 8.3 %collective-permute-start.33 = (bf16[128,1024]{1,0:T(8,128)(2,1)S(1)}, bf16[128,1024]{1,0:T(8,128)(2,1)S(1)}, u32[]{:S(2)}, u32[]{:S(2)}) collective-permute-start(bf16[128,1024]{1,0:T(8,128)(2,1)S(1)} %get-tuple-element.112), channel_id=1, source_target_pairs={{8,16},{10,18},{16,24},{18,26},{24,28},{26,30},{28,20},{30,22},{20... | collective-permute-start | bytes 786440 | tf_op jit(solution)/shard_map/ppermute | solution.py:69
  143.7 11.3 %collective-permute-start.37 = (bf16[128,1024]{1,0:T(8,128)(2,1)S(1)}, bf16[128,1024]{1,0:T(8,128)(2,1)S(1)}, u32[]{:S(2)}, u32[]{:S(2)}) collective-permute-start(bf16[128,1024]{1,0:T(8,128)(2,1)S(1)} %get-tuple-element.113), channel_id=1, source_target_pairs={{8,0},{10,2},{16,8},{18,10},{24,16},{26,18},{28,24},{30,26},{20,28... | collective-permute-start | bytes 786440 | tf_op jit(solution)/shard_map/ppermute | solution.py:69
  147.2 17.4 %copy-start.14 = (bf16[128,1024]{1,0:T(8,128)(2,1)S(1)}, bf16[128,1024]{1,0:T(8,128)(2,1)}, u32[]{:S(2)}) copy-start(bf16[128,1024]{1,0:T(8,128)(2,1)} %copy-done.13) | copy-start | bytes 786436
  147.2 13.1 %collective-permute-start.40 = (bf16[128,1024]{1,0:T(8,128)(2,1)S(1)}, bf16[128,1024]{1,0:T(8,128)(2,1)S(1)}, u32[]{:S(2)}, u32[]{:S(2)}) collective-permute-start(bf16[128,1024]{1,0:T(8,128)(2,1)S(1)} %add_convert_fusion.1), channel_id=1, source_target_pairs={{8,20},{10,22},{16,12},{18,14},{24,4},{26,6},{28,0},{30,2},{20,8},... | collective-permute-start | bytes 786440 | tf_op jit(solution)/shard_map/ppermute | solution.py:69
  155.2 14.7 %copy-start.24 = (f32[1024]{0:T(1024)S(1)}, f32[1024]{0:T(1024)}, u32[]{:S(2)}) copy-start(f32[1024]{0:T(1024)} %param.28) | copy-start | bytes 12292
  155.2 9.3 %collective-permute-start.34 = (bf16[128,1024]{1,0:T(8,128)(2,1)S(1)}, bf16[128,1024]{1,0:T(8,128)(2,1)S(1)}, u32[]{:S(2)}, u32[]{:S(2)}) collective-permute-start(bf16[128,1024]{1,0:T(8,128)(2,1)S(1)} %get-tuple-element.110), channel_id=1, source_target_pairs={{8,16},{10,18},{16,24},{18,26},{24,28},{26,30},{28,20},{30,22},{20... | collective-permute-start | bytes 786440 | tf_op jit(solution)/shard_map/ppermute | solution.py:69
  156.2 8.4 %collective-permute-start.38 = (bf16[128,1024]{1,0:T(8,128)(2,1)S(1)}, bf16[128,1024]{1,0:T(8,128)(2,1)S(1)}, u32[]{:S(2)}, u32[]{:S(2)}) collective-permute-start(bf16[128,1024]{1,0:T(8,128)(2,1)S(1)} %get-tuple-element.111), channel_id=1, source_target_pairs={{8,0},{10,2},{16,8},{18,10},{24,16},{26,18},{28,24},{30,26},{20,28... | collective-permute-start | bytes 786440 | tf_op jit(solution)/shard_map/ppermute | solution.py:69
  164.9 5.8 %copy-start.23 = (bf16[128,1024]{1,0:T(8,128)(2,1)}, bf16[128,1024]{1,0:T(8,128)(2,1)S(1)}, u32[]{:S(2)}) copy-start(bf16[128,1024]{1,0:T(8,128)(2,1)S(1)} %get-tuple-element.103) | copy-start | bytes 786436
  (3 other events, 2.0 us)

commit v2 on v1

--- a/solution.py
+++ b/solution.py
@@ -193,7 +193,7 @@
     normed_ref, own_ref, sums_ref, rest_ref, gain_ref, hidden_ref, sems, *held = refs
     copies = [
         pltpu.make_async_copy(stack, to, sems.at[i])
-        for i, (stack, to) in enumerate(zip(stacks, held))
+        for i, (stack, to) in enumerate(zip([*stacks, *residuals], held))
     ]
     for copy in copies:
         copy.start()
@@ -210,7 +210,8 @@
             sums_ref[info_ref[offset % chips] * CORES + lane] = total
     for k in range(mp_count):
         at = lax.rem(mp + k, mp_count)
-        rest_ref[at] = residuals[k][...]
+        copies[len(stacks) + k].wait()
+        rest_ref[at] = held[len(stacks) + k][...]
         gain_ref[at] = gains[k][...]
     rows, half = own_ref.shape
     width = sums_ref.shape[2]
@@ -241,17 +242,17 @@
             jax.ShapeDtypeStruct((rows, half), jnp.bfloat16),
         ],
         in_specs=[smem()]
-        + [pl.BlockSpec(memory_space=pl.ANY)] * len(stacks)
-        + [vmem()] * (2 * mp_count),
+        + [pl.BlockSpec(memory_space=pl.ANY)] * (len(stacks) + mp_count)
+        + [vmem()] * mp_count,
         out_specs=[vmem()] * 2,
         scratch_shapes=[
             pltpu.VMEM((count, rows, width), jnp.float32),
             pltpu.VMEM((mp_count, rows, half), jnp.bfloat16),
             pltpu.VMEM((mp_count, 1, half), jnp.float32),
             pltpu.VMEM((mp_count, rows, half), jnp.float32),
-            pltpu.SemaphoreType.DMA((len(stacks),)),
+            pltpu.SemaphoreType.DMA((len(stacks) + mp_count,)),
         ]
-        + [pltpu.VMEM(stack.shape, stack.dtype) for stack in stacks],
+        + [pltpu.VMEM(value.shape, value.dtype) for value in (*stacks, *residuals)],
         compiler_params=params(
             ((count, rows, width), jnp.float32), *[(stack.shape, stack.dtype) for stack in stacks]
         ),
@@ -423,46 +424,58 @@
             behind = moved[1]
             arrived.append(behind)
             listed.append(s)
-    shared = lax.all_to_all(after(shared, ahead, stacks[0][-1]), "dp", 0, 0, tiled=True)
+    shared = lax.all_to_all(after(shared, ahead), "dp", 0, 0, tiled=True)
     other = [moves.swap_core(after(w, ahead)) for w in mine]
     exchange(listed, *project(attention, other_attention, arrived, 0, len(arrived)))
     normed, own_hidden = norm(
         info, offsets, [piece for stack in stacks for piece in stack], residuals, gains
     )
-    shared = shared.transpose(1, 0, 2)
+    shared = after(shared, normed).transpose(1, 0, 2)
     shared = [shared, moves.swap_core(shared)]
-    spare = round_up(CORES * units, 16) - CORES * units
-    parts = []
-    for i in range(3):
-        part = [value[i * units : (i + 1) * units].reshape(units, D) for value in shared]
-        parts.append(jnp.pad(jnp.concatenate(part), ((0, spare), (0, 0))))
-    weights = [*mine, *parts, *other]
-    scores = []
-    for value in shared:
-        thirds = value[3 * units : used].transpose(1, 0, 2).reshape(dp_count, 3, rows)
-        scores.append(jnp.sum(thirds.astype(f32), axis=1))
+
+    def unpack(shared):
+        spare = round_up(CORES * units, 16) - CORES * units
+        parts = []
+        for i in range(3):
+            part = [value[i * units : (i + 1) * units].reshape(units, D) for value in shared]
+            parts.append(jnp.pad(jnp.concatenate(part), ((0, spare), (0, 0))))
+        weights = [*mine, *parts, *other]
+        scores = []
+        for value in shared:
+            thirds = value[3 * units : used].transpose(1, 0, 2).reshape(dp_count, 3, rows)
+            scores.append(jnp.sum(thirds.astype(f32), axis=1))
+        return weights, scores
 
     def swap_mp(sent):
         return [moves.from_mp(sent[k - 1], mp_count - k) for k in range(1, mp_count)]
 
     ahead = behind = normed
-    listed, blocks = [0], [normed]
     done = []
     for s in range(1, left + 1):
-        outs = list(ffn(listed, blocks, scores, weights, info, mp_count))
-        done.append([listed, outs, None])
+        if s > 1:
+            outs = list(ffn(listed, blocks, scores, weights, info, mp_count))
+            done.append([listed, outs, None])
         if s <= right:
             moved = [moves.step(ahead, 1), moves.step(behind, -1)]
         else:
             moved = [moves.step(ahead[: rows // 2], 1), moves.step(behind[rows // 2 :], -1)]
-        came = done[-2][2] if s >= 2 else []
-        moved, ties, came = lax.optimization_barrier((moved, outs[1:], came))
-        if s >= 2:
-            done[-2][2] = came
-        done[-1][2] = swap_mp(ties)
+        if s > 1:
+            came = done[-2][2] if s > 2 else []
+            moved, ties, came = lax.optimization_barrier((moved, outs[1:], came))
+            if s > 2:
+                done[-2][2] = came
+            done[-1][2] = swap_mp(ties)
+        else:
+            moved, shared = lax.optimization_barrier((moved, shared))
+            weights, scores = unpack(shared)
         ahead, behind = blocks = moved
         listed = [-s, s] if s <= right else [s]
-    done.append([listed, ffn(listed, blocks, scores, weights, info, mp_count), None])
+    outs = ffn([*listed, 0], [*blocks, normed], scores, weights, info, mp_count)
+    for start, stop, offsets in (
+        (0, rows * len(listed), listed),
+        (rows * len(listed), rows * (len(listed) + 1), [0]),
+    ):
+        done.append([offsets, [value[start:stop] for value in outs], None])
     parts, whole = {}, {}
     for listed, (kept, *sent), came in done:
         if right in listed:
@@ -493,10 +506,9 @@
 
     final = (own_hidden.astype(f32) + mixture).astype(bf16)
     final_float = final.astype(f32)
-    final_squares = lax.psum(jnp.sum(final_float * final_float, axis=1), "mp")
-    next_normed = (
-        final_float * lax.rsqrt(final_squares / D + EPSILON)[:, None] * next_gain
-    ).astype(bf16)
+    squares = moves.all_mp(jnp.sum(final_float * final_float, axis=1, keepdims=True).T)
+    scale = lax.rsqrt(sum(squares) / D + EPSILON).T
+    next_normed = (final_float * scale * next_gain).astype(bf16)
     return (final, next_normed)
 
 

time: 171 us -> 166 us (0.971)
  waiting for transfers between devices: 40.5 us -> 61.1 us
  Pallas kernels: 51.3 us -> 34.9 us
  blocking collectives: 4.94 us -> 0 us
  starting transfers between devices: 53.4 us -> 50.2 us
  local copies, waits for them, and re-layouts: 15 us -> 12.9 us
    pallas_call x5 -> x4, Pallas kernels: 45.7 us -> 30.2 us  [ffn(): pl.pallas_call(functools.partial(ffn_kernel, offsets, len(tokens), mp_cou...]
    ppermute x22, waiting for transfers between devices: 28.4 us -> 41.4 us  [step(): return lax.ppermute(value, 'dp', pairs)]
    ppermute x10 -> x11, waiting for transfers between devices: 6.38 us -> 15.1 us  [from_mp(): lax.ppermute(value, 'mp', [((i + k) % count, i) for i in range(count)])]
    psum x1 -> x0, blocking collectives: 4.94 us -> none  [local(): final_squares = lax.psum(jnp.sum(final_float * final_float, axis=1), 'mp')]
    ppermute x22, starting transfers between devices: 32.9 us -> 29.6 us  [step(): return lax.ppermute(value, 'dp', pairs)]
    unnamed x54 -> x50, local copies, waits for them, and re-layouts: 14.1 us -> 12 us
    ppermute x7, waiting for transfers between devices: 2.65 us -> 0.77 us  [swap_core(): return lax.ppermute(value, 'dp', [(d, d ^ 1) for d in range(count)])]
    ppermute x10 -> x11, starting transfers between devices: 11.6 us -> 11.5 us  [from_mp(): lax.ppermute(value, 'mp', [((i + k) % count, i) for i in range(count)])]
  transfers between devices with their start and end apart: 42 -> 43, of which waited for: 22 -> 25; matrix products, arithmetic and copies ran while one was open for 3% -> 4% of each run, Pallas kernels for 30% -> 21%
where the time goes in v2:
time: 166 us; the launch traced here: 165 us
  waiting for transfers between devices  61.1 us (37%)
  starting transfers between devices  50.2 us (30%)
  Pallas kernels  34.9 us (21%)
  local copies, waits for them, and re-layouts  12.9 us (8%)
  other arithmetic  4.56 us (3%)
    ppermute x22, waiting for transfers between devices, step(): return lax.ppermute(value, 'dp', pairs)  41.4 us
    pallas_call x4, Pallas kernels, ffn(): pl.pallas_call(functools.partial(ffn_kernel, offsets, len(tokens), mp_cou...  30.2 us
    ppermute x22, starting transfers between devices, step(): return lax.ppermute(value, 'dp', pairs)  29.6 us
    ppermute x11, waiting for transfers between devices, from_mp(): lax.ppermute(value, 'mp', [((i + k) % count, i) for i in range(count)])  15.1 us
    unnamed x50, local copies, waits for them, and re-layouts  12 us
    ppermute x11, starting transfers between devices, from_mp(): lax.ppermute(value, 'mp', [((i + k) % count, i) for i in range(count)])  11.5 us
    all_to_all x1, starting transfers between devices, local(): shared = lax.all_to_all(after(shared, ahead), 'dp', 0, 0, tiled=True)  4.65 us
  transfers between devices with their start and end apart: 43, of which 25 were waited for; matrix products, arithmetic and copies ran while one was open for 4% of the time, Pallas kernels for 21%

profile of v2, /device:TPU:0, one launch (start us, length us, event | category | flops | bytes accessed | tf_op | source)
XLA Modules:
  0.0 164.7 jit_solution(6464921955101532881)
XLA Ops:
  0.6 3.1 %collective-permute-start.1 = (bf16[1024,128]{1,0:T(8,128)(2,1)}, bf16[1024,128]{1,0:T(8,128)(2,1)S(1)}, u32[]{:S(2)}, u32[]{:S(2)}) collective-permute-start(bf16[1024,128]{1,0:T(8,128)(2,1)} %refs_2_.1), channel_id=1, source_target_pairs={{8,16},{10,18},{16,24},{18,26},{24,28},{26,30},{28,20},{30,22},{20... | collective-permute-start | bytes 786440 | tf_op jit(solution)/shard_map/ppermute | solution.py:69
  3.7 6.4 %collective-permute-done.1.refs_3_ = bf16[1024,128]{1,0:T(8,128)(2,1)S(1)} collective-permute-done((bf16[1024,128]{1,0:T(8,128)(2,1)}, bf16[1024,128]{1,0:T(8,128)(2,1)S(1)}, u32[]{:S(2)}, u32[]{:S(2)}) %collective-permute-start.1) | collective-permute-done | bytes 262176 | tf_op jit(solution)/shard_map/ppermute | solution.py:69
  10.2 1.5 collective-permute-done.2.refs_4_
  11.7 1.6 collective-permute-start.3
  13.7 1.5 collective-permute-start.8
  15.7 0.8 select_reduce_fusion.1
  16.5 0.8 select_reduce_fusion
  17.3 0.9 copy-done.4
  18.3 0.9 copy-done.12
  19.8 1.6 collective-permute-start.5
  22.3 1.0 copy-done.3
  23.8 2.5 %collective-permute-done.5.refs_2_ = bf16[1024,128]{1,0:T(8,128)(2,1)S(1)} collective-permute-done((bf16[1024,128]{1,0:T(8,128)(2,1)S(1)}, bf16[1024,128]{1,0:T(8,128)(2,1)S(1)}, u32[]{:S(2)}, u32[]{:S(2)}) %collective-permute-start.5) | collective-permute-done | bytes 262176 | tf_op jit(solution)/shard_map/ppermute | solution.py:69
  26.2 1.6 collective-permute-done.6.refs_3_
  27.8 1.6 collective-permute-start.12
  31.2 3.0 %collective-permute-done.12.refs_2_ = bf16[1024,128]{1,0:T(8,128)(2,1)S(1)} collective-permute-done((bf16[1024,128]{1,0:T(8,128)(2,1)S(1)}, bf16[1024,128]{1,0:T(8,128)(2,1)S(1)}, u32[]{:S(2)}, u32[]{:S(2)}) %collective-permute-start.12) | collective-permute-done | bytes 262176 | tf_op jit(solution)/shard_map/ppermute | solution.py:69
  34.2 0.7 copy-done.15
  34.9 4.7 %all-to-all-start = ((bf16[16,272,128]{2,1,0:T(8,128)(2,1)}), bf16[16,272,128]{2,1,0:T(8,128)(2,1)}, u32[]{:S(2)}, u32[]{:S(2)}) async-start(bf16[16,272,128]{2,1,0:T(8,128)(2,1)} %copy-done.3), calls=%async_computation | async-start | bytes 2228224 | tf_op jit(solution)/shard_map/all_to_all | solution.py:427
  39.8 1.5 collective-permute-start.9
  41.4 1.5 collective-permute-start.11
  42.9 0.9 copy-done.16
  45.4 0.9 collective-permute-start.15
  47.0 1.5 collective-permute-done.9.refs_1_
  48.5 5.3 %collective-permute-done.13.refs_5_ = bf16[1,128,128]{2,1,0:T(8,128)(2,1)S(1)} collective-permute-done((bf16[1,128,128]{2,1,0:T(8,128)(2,1)S(1)}, bf16[1,128,128]{2,1,0:T(8,128)(2,1)S(1)}, u32[]{:S(2)}, u32[]{:S(2)}) %collective-permute-start.13) | collective-permute-done | bytes 32800 | tf_op jit(solution)/shard_map/ppermute | solution.py:105
  54.2 0.9 copy-done.7
  55.1 0.9 copy-done.17
  56.1 0.9 copy-done.19
  57.0 2.7 %shard_map.163 = (bf16[128,2048]{1,0:T(8,128)(2,1)S(1)}, bf16[128,1024]{1,0:T(8,128)(2,1)S(1)}) custom-call(s32[10]{0:T(128)S(1)} %dynamic-slice_bitcast_fusion.info_ref, bf16[7,128,128]{2,1,0:T(8,128)(2,1)S(1)} %copy-done.7, bf16[7,128,128]{2,1,0:T(8,128)(2,1)} %collective-permute-done.9.refs_1_, bf16[7,128,128]{2,1,0:T(8,128)(2,1)} %collective-permute-done.10.refs_2_, ...), custom_call_target="tpu_custom_call" | custom-call | flops 1 | bytes 1 | tf_op jit(solution)/shard_map/pallas_call | solution.py:238
  60.4 3.2 %all-to-all-done = bf16[16,272,128]{2,1,0:T(8,128)(2,1)} async-done(((bf16[16,272,128]{2,1,0:T(8,128)(2,1)}), bf16[16,272,128]{2,1,0:T(8,128)(2,1)}, u32[]{:S(2)}, u32[]{:S(2)}) %all-to-all-start) | async-done | bytes 1114144 | tf_op jit(solution)/shard_map/all_to_all | solution.py:427
  63.6 0.7 collective-permute-start.18
  64.3 2.1 %collective-permute-start.17 = (bf16[128,2048]{1,0:T(8,128)(2,1)S(1)}, bf16[128,2048]{1,0:T(8,128)(2,1)S(1)}, u32[]{:S(2)}, u32[]{:S(2)}) collective-permute-start(bf16[128,2048]{1,0:T(8,128)(2,1)S(1)} %get-tuple-element.71.refs_4_), channel_id=1, source_target_pairs={{8,0},{10,2},{16,8},{18,10},{24,16},{26,18},{28,24},{30,26},{20,28... | collective-permute-start | bytes 1572872 | tf_op jit(solution)/shard_map/ppermute | solution.py:69
  66.3 1.5 collective-permute-start.16
  68.3 11.6 %collective-permute-done.17.refs_3_ = bf16[128,2048]{1,0:T(8,128)(2,1)S(1)} collective-permute-done((bf16[128,2048]{1,0:T(8,128)(2,1)S(1)}, bf16[128,2048]{1,0:T(8,128)(2,1)S(1)}, u32[]{:S(2)}, u32[]{:S(2)}) %collective-permute-start.17) | collective-permute-done | bytes 524320 | tf_op jit(solution)/shard_map/ppermute | solution.py:69
  79.9 1.5 collective-permute-done.16.refs_2_
  81.4 0.7 collective-permute-start.19
  82.1 1.3 collective-permute-start.20
  83.5 1.5 slice_bitcast_fusion
  85.2 1.0 convert_reduce_fusion
  86.2 0.8 copy-done.1
  87.1 7.5 %shard_map.164 = (f32[256,1024]{1,0:T(8,128)S(1)}, bf16[256,1024]{1,0:T(8,128)(2,1)S(1)}) custom-call(s32[10]{0:T(128)S(1)} %dynamic-slice_bitcast_fusion.info_ref, f32[16,128]{1,0:T(8,128)S(1)} %get-tuple-element.125.refs_0_, f32[16,128]{1,0:T(8,128)S(1)} %get-tuple-element.124.refs_1_, bf16[128,2048]{1,0:T(8,128)(2,1)S(1)} %collective-permute-done.16.refs_2_, ...), custom_call_target="tpu_custom_call" | custom-call | flops 1 | bytes 1 | tf_op jit(solution)/shard_map/pallas_call | solution.py:314
  94.7 1.5 collective-permute-done.20.refs_3_
  96.1 1.5 collective-permute-start.26
  97.6 1.7 %collective-permute-start.24 = (bf16[128,2048]{1,0:T(8,128)(2,1)S(1)}, bf16[128,2048]{1,0:T(8,128)(2,1)S(1)}, u32[]{:S(2)}, u32[]{:S(2)}) collective-permute-start(bf16[128,2048]{1,0:T(8,128)(2,1)S(1)} %collective-permute-done.19.refs_2_), channel_id=1, source_target_pairs={{8,16},{10,18},{16,24},{18,26},{24,28},{26,30},{28,20},{30,22},{20... | collective-permute-start | bytes 1572872 | tf_op jit(solution)/shard_map/ppermute | solution.py:69
  99.7 7.6 %shard_map.165 = (f32[256,1024]{1,0:T(8,128)S(1)}, bf16[256,1024]{1,0:T(8,128)(2,1)S(1)}) custom-call(s32[10]{0:T(128)S(1)} %dynamic-slice_bitcast_fusion.info_ref, f32[16,128]{1,0:T(8,128)S(1)} %get-tuple-element.125.refs_0_, f32[16,128]{1,0:T(8,128)S(1)} %get-tuple-element.124.refs_1_, bf16[128,2048]{1,0:T(8,128)(2,1)S(1)} %collective-permute-done.19.refs_2_, ...), custom_call_target="tpu_custom_call" | custom-call | flops 1 | bytes 1 | tf_op jit(solution)/shard_map/pallas_call | solution.py:314
  107.2 2.1 %collective-permute-done.26 = bf16[256,1024]{1,0:T(8,128)(2,1)S(1)} collective-permute-done((bf16[256,1024]{1,0:T(8,128)(2,1)S(1)}, bf16[256,1024]{1,0:T(8,128)(2,1)S(1)}, u32[]{:S(2)}, u32[]{:S(2)}) %collective-permute-start.26) | collective-permute-done | bytes 524320 | tf_op jit(solution)/shard_map/ppermute | solution.py:105
  109.3 1.2 collective-permute-done.24.refs_2_
  110.5 1.5 collective-permute-done.25.refs_3_
  112.9 1.7 %collective-permute-start.27 = (bf16[64,2048]{1,0:T(8,128)(2,1)S(1)}, bf16[64,2048]{1,0:T(8,128)(2,1)S(1)}, u32[]{:S(2)}, u32[]{:S(2)}) collective-permute-start(bf16[64,2048]{1,0:T(8,128)(2,1)S(1)} %slice.76), channel_id=1, source_target_pairs={{8,16},{10,18},{16,24},{18,26},{24,28},{26,30},{28,20},{30,22},{20... | collective-permute-start | bytes 786440 | tf_op jit(solution)/shard_map/ppermute | solution.py:69
  114.7 7.6 %shard_map.166 = (f32[256,1024]{1,0:T(8,128)S(1)}, bf16[256,1024]{1,0:T(8,128)(2,1)S(1)}) custom-call(s32[10]{0:T(128)S(1)} %dynamic-slice_bitcast_fusion.info_ref, f32[16,128]{1,0:T(8,128)S(1)} %get-tuple-element.125.refs_0_, f32[16,128]{1,0:T(8,128)S(1)} %get-tuple-element.124.refs_1_, bf16[128,2048]{1,0:T(8,128)(2,1)S(1)} %collective-permute-done.24.refs_2_, ...), custom_call_target="tpu_custom_call" | custom-call | flops 1 | bytes 1 | tf_op jit(solution)/shard_map/pallas_call | solution.py:314
  123.0 1.4 collective-permute-start.35
  124.5 1.6 collective-permute-start.32
  126.1 1.4 collective-permute-start.36
  127.5 7.5 %shard_map.167 = (f32[256,1024]{1,0:T(8,128)S(1)}, bf16[256,1024]{1,0:T(8,128)(2,1)S(1)}) custom-call(s32[10]{0:T(128)S(1)} %dynamic-slice_bitcast_fusion.info_ref, f32[16,128]{1,0:T(8,128)S(1)} %get-tuple-element.125.refs_0_, f32[16,128]{1,0:T(8,128)S(1)} %get-tuple-element.124.refs_1_, bf16[64,2048]{1,0:T(8,128)(2,1)S(1)} %collective-permute-done.27.refs_2_, ...), custom_call_target="tpu_custom_call" | custom-call | flops 1 | bytes 1 | tf_op jit(solution)/shard_map/pallas_call | solution.py:314
  135.1 1.6 collective-permute-start.39
  138.0 2.9 %collective-permute-start.37 = (bf16[128,1024]{1,0:T(8,128)(2,1)S(1)}, bf16[128,1024]{1,0:T(8,128)(2,1)S(1)}, u32[]{:S(2)}, u32[]{:S(2)}) collective-permute-start(bf16[128,1024]{1,0:T(8,128)(2,1)S(1)} %get-tuple-element.111), channel_id=1, source_target_pairs={{8,0},{10,2},{16,8},{18,10},{24,16},{26,18},{28,24},{30,26},{20,28... | collective-permute-start | bytes 786440 | tf_op jit(solution)/shard_map/ppermute | solution.py:69
  141.7 3.0 %collective-permute-done.39 = bf16[128,1024]{1,0:T(8,128)(2,1)S(1)} collective-permute-done((bf16[128,1024]{1,0:T(8,128)(2,1)S(1)}, bf16[128,1024]{1,0:T(8,128)(2,1)S(1)}, u32[]{:S(2)}, u32[]{:S(2)}) %collective-permute-start.39) | collective-permute-done | bytes 262176 | tf_op jit(solution)/shard_map/ppermute | solution.py:105
  144.8 2.0 %collective-permute-start.40 = (bf16[128,1024]{1,0:T(8,128)(2,1)S(1)}, bf16[128,1024]{1,0:T(8,128)(2,1)S(1)}, u32[]{:S(2)}, u32[]{:S(2)}) collective-permute-start(bf16[128,1024]{1,0:T(8,128)(2,1)S(1)} %add_convert_fusion.1), channel_id=1, source_target_pairs={{8,20},{10,22},{16,12},{18,14},{24,4},{26,6},{28,0},{30,2},{20,8},... | collective-permute-start | bytes 786440 | tf_op jit(solution)/shard_map/ppermute | solution.py:69
  146.7 2.7 %collective-permute-done.37 = bf16[128,1024]{1,0:T(8,128)(2,1)S(1)} collective-permute-done((bf16[128,1024]{1,0:T(8,128)(2,1)S(1)}, bf16[128,1024]{1,0:T(8,128)(2,1)S(1)}, u32[]{:S(2)}, u32[]{:S(2)}) %collective-permute-start.37) | collective-permute-done | bytes 262176 | tf_op jit(solution)/shard_map/ppermute | solution.py:69
  149.6 4.0 %collective-permute-start.34 = (bf16[128,1024]{1,0:T(8,128)(2,1)S(1)}, bf16[128,1024]{1,0:T(8,128)(2,1)S(1)}, u32[]{:S(2)}, u32[]{:S(2)}) collective-permute-start(bf16[128,1024]{1,0:T(8,128)(2,1)S(1)} %get-tuple-element.108), channel_id=1, source_target_pairs={{8,16},{10,18},{16,24},{18,26},{24,28},{26,30},{28,20},{30,22},{20... | collective-permute-start | bytes 786440 | tf_op jit(solution)/shard_map/ppermute | solution.py:69
  153.6 1.3 collective-permute-done.40
  154.9 2.7 %collective-permute-done.34 = bf16[128,1024]{1,0:T(8,128)(2,1)S(1)} collective-permute-done((bf16[128,1024]{1,0:T(8,128)(2,1)S(1)}, bf16[128,1024]{1,0:T(8,128)(2,1)S(1)}, u32[]{:S(2)}, u32[]{:S(2)}) %collective-permute-start.34) | collective-permute-done | bytes 262176 | tf_op jit(solution)/shard_map/ppermute | solution.py:69
  157.6 2.4 %collective-permute-done.38 = bf16[128,1024]{1,0:T(8,128)(2,1)S(1)} collective-permute-done((bf16[128,1024]{1,0:T(8,128)(2,1)S(1)}, bf16[128,1024]{1,0:T(8,128)(2,1)S(1)}, u32[]{:S(2)}, u32[]{:S(2)}) %collective-permute-start.38) | collective-permute-done | bytes 262176 | tf_op jit(solution)/shard_map/ppermute | solution.py:69
  160.3 0.7 collective-permute-start.41
  161.0 2.9 %collective-permute-done.41 = f32[1,128]{1,0:T(1,128)S(1)} collective-permute-done((f32[1,128]{1,0:T(1,128)S(1)}, f32[1,128]{1,0:T(1,128)S(1)}, u32[]{:S(2)}, u32[]{:S(2)}) %collective-permute-start.41) | collective-permute-done | bytes 544 | tf_op jit(solution)/shard_map/ppermute | solution.py:105
  163.9 0.8 fusion.2
  (105 shorter events, 13.8 us)
Async XLA Ops:
  0.6 9.5 %collective-permute-start.1 = (bf16[1024,128]{1,0:T(8,128)(2,1)}, bf16[1024,128]{1,0:T(8,128)(2,1)S(1)}, u32[]{:S(2)}, u32[]{:S(2)}) collective-permute-start(bf16[1024,128]{1,0:T(8,128)(2,1)} %refs_2_.1), channel_id=1, source_target_pairs={{8,16},{10,18},{16,24},{18,26},{24,28},{26,30},{28,20},{30,22},{20... | collective-permute-start | bytes 786440 | tf_op jit(solution)/shard_map/ppermute | solution.py:69
  3.7 8.0 %collective-permute-start.2 = (bf16[1024,128]{1,0:T(8,128)(2,1)}, bf16[1024,128]{1,0:T(8,128)(2,1)S(1)}, u32[]{:S(2)}, u32[]{:S(2)}) collective-permute-start(bf16[1024,128]{1,0:T(8,128)(2,1)} %refs_2_.1), channel_id=1, source_target_pairs={{8,0},{10,2},{16,8},{18,10},{24,16},{26,18},{28,24},{30,26},{20,28... | collective-permute-start | bytes 786440 | tf_op jit(solution)/shard_map/ppermute | solution.py:69
  3.7 13.6 %collective-permute-start = (bf16[128,1024]{1,0:T(8,128)(2,1)}, bf16[128,1024]{1,0:T(8,128)(2,1)S(1)}, u32[]{:S(2)}, u32[]{:S(2)}) collective-permute-start(bf16[128,1024]{1,0:T(8,128)(2,1)} %refs_0_.7), channel_id=1, source_target_pairs={{0,2},{2,0},{4,6},{6,4},{8,10},{10,8},{12,14},{14,12},{16,18},{18,... | collective-permute-start | bytes 786440 | tf_op jit(solution)/shard_map/ppermute | solution.py:101
  11.7 8.1 %collective-permute-start.3 = (bf16[1024,128]{1,0:T(8,128)(2,1)S(1)}, bf16[1024,128]{1,0:T(8,128)(2,1)S(1)}, u32[]{:S(2)}, u32[]{:S(2)}) collective-permute-start(bf16[1024,128]{1,0:T(8,128)(2,1)S(1)} %collective-permute-done.1.refs_3_), channel_id=1, source_target_pairs={{8,16},{10,18},{16,24},{18,26},{24,28},{26,30},{28,20},{30,22},{20... | collective-permute-start | bytes 786440 | tf_op jit(solution)/shard_map/ppermute | solution.py:69
  13.3 6.6 %collective-permute-start.4 = (bf16[1024,128]{1,0:T(8,128)(2,1)S(1)}, bf16[1024,128]{1,0:T(8,128)(2,1)S(1)}, u32[]{:S(2)}, u32[]{:S(2)}) collective-permute-start(bf16[1024,128]{1,0:T(8,128)(2,1)S(1)} %collective-permute-done.2.refs_4_), channel_id=1, source_target_pairs={{8,0},{10,2},{16,8},{18,10},{24,16},{26,18},{28,24},{30,26},{20,28... | collective-permute-start | bytes 786440 | tf_op jit(solution)/shard_map/ppermute | solution.py:69
  13.7 10.0 %collective-permute-start.8 = (f32[1,1024]{1,0:T(1,128)}, f32[1,1024]{1,0:T(1,128)S(1)}, u32[]{:S(2)}, u32[]{:S(2)}) collective-permute-start(f32[1,1024]{1,0:T(1,128)} %bitcast.61), channel_id=1, source_target_pairs={{1,0},{0,1},{3,2},{2,3},{5,4},{4,5},{7,6},{6,7},{9,8},{8,9},{11,10... | collective-permute-start | bytes 12296 | tf_op jit(solution)/shard_map/ppermute | solution.py:105
  15.2 8.5 %collective-permute-start.7 = (bf16[128,1024]{1,0:T(8,128)(2,1)}, bf16[128,1024]{1,0:T(8,128)(2,1)S(1)}, u32[]{:S(2)}, u32[]{:S(2)}) collective-permute-start(bf16[128,1024]{1,0:T(8,128)(2,1)} %refs_8_.1), channel_id=1, source_target_pairs={{1,0},{0,1},{3,2},{2,3},{5,4},{4,5},{7,6},{6,7},{9,8},{8,9},{11,10... | collective-permute-start | bytes 786440 | tf_op jit(solution)/shard_map/ppermute | solution.py:105
  17.3 1.0 copy-start.4
  18.2 0.9 copy-start.12
  19.2 2.7 %copy-start.9 = (bf16[128,1408]{1,0:T(8,128)(2,1)S(1)}, bf16[128,1408]{1,0:T(8,128)(2,1)}, u32[]{:S(2)}) copy-start(bf16[128,1408]{1,0:T(8,128)(2,1)} %gate_ref.1) | copy-start | bytes 1081348
  19.2 2.7 %copy-start.10 = (bf16[128,1408]{1,0:T(8,128)(2,1)S(1)}, bf16[128,1408]{1,0:T(8,128)(2,1)}, u32[]{:S(2)}) copy-start(bf16[128,1408]{1,0:T(8,128)(2,1)} %up_ref.1) | copy-start | bytes 1081348
  19.2 2.7 %copy-start.11 = (bf16[1408,128]{1,0:T(8,128)(2,1)S(1)}, bf16[1408,128]{1,0:T(8,128)(2,1)}, u32[]{:S(2)}) copy-start(bf16[1408,128]{1,0:T(8,128)(2,1)} %down_ref.1) | copy-start | bytes 1081348
  19.8 6.4 %collective-permute-start.5 = (bf16[1024,128]{1,0:T(8,128)(2,1)S(1)}, bf16[1024,128]{1,0:T(8,128)(2,1)S(1)}, u32[]{:S(2)}, u32[]{:S(2)}) collective-permute-start(bf16[1024,128]{1,0:T(8,128)(2,1)S(1)} %collective-permute-done.3.refs_2_), channel_id=1, source_target_pairs={{8,16},{10,18},{16,24},{18,26},{24,28},{26,30},{28,20},{30,22},{20... | collective-permute-start | bytes 786440 | tf_op jit(solution)/shard_map/ppermute | solution.py:69
  21.4 6.4 %collective-permute-start.6 = (bf16[1024,128]{1,0:T(8,128)(2,1)S(1)}, bf16[1024,128]{1,0:T(8,128)(2,1)S(1)}, u32[]{:S(2)}, u32[]{:S(2)}) collective-permute-start(bf16[1024,128]{1,0:T(8,128)(2,1)S(1)} %collective-permute-done.4.refs_3_), channel_id=1, source_target_pairs={{8,0},{10,2},{16,8},{18,10},{24,16},{26,18},{28,24},{30,26},{20,28... | collective-permute-start | bytes 786440 | tf_op jit(solution)/shard_map/ppermute | solution.py:69
  22.0 1.3 copy-start.5
  22.3 1.0 copy-start.3
  23.8 11.1 %copy-start.18 = (bf16[128,1024]{1,0:T(8,128)(2,1)}, bf16[128,1024]{1,0:T(8,128)(2,1)S(1)}, u32[]{:S(2)}) copy-start(bf16[128,1024]{1,0:T(8,128)(2,1)S(1)} %collective-permute-done.7.refs_9_) | copy-start | bytes 786436
  27.8 6.4 %collective-permute-start.12 = (bf16[1024,128]{1,0:T(8,128)(2,1)S(1)}, bf16[1024,128]{1,0:T(8,128)(2,1)S(1)}, u32[]{:S(2)}, u32[]{:S(2)}) collective-permute-start(bf16[1024,128]{1,0:T(8,128)(2,1)S(1)} %collective-permute-done.5.refs_2_), channel_id=1, source_target_pairs={{8,16},{10,18},{16,24},{18,26},{24,28},{26,30},{28,20},{30,22},{20... | collective-permute-start | bytes 786440 | tf_op jit(solution)/shard_map/ppermute | solution.py:69
  29.4 24.8 %copy-start.20 = (f32[1024]{0:T(1024)S(1)}, f32[1024]{0:T(1024)}, u32[]{:S(2)}) copy-start(f32[1024]{0:T(1024)} %param.18) | copy-start | bytes 12292
  34.2 0.7 copy-start.15
  34.9 33.0 %copy-start = (bf16[1,2048,704]{1,2,0:T(8,128)(2,1)S(1)}, bf16[1,2048,704]{1,2,0:T(8,128)(2,1)}, u32[]{:S(2)}) copy-start(bf16[1,2048,704]{1,2,0:T(8,128)(2,1)} %param.22) | copy-start | bytes 8650756
  34.9 28.7 %all-to-all-start = ((bf16[16,272,128]{2,1,0:T(8,128)(2,1)}), bf16[16,272,128]{2,1,0:T(8,128)(2,1)}, u32[]{:S(2)}, u32[]{:S(2)}) async-start(bf16[16,272,128]{2,1,0:T(8,128)(2,1)} %copy-done.3), calls=%async_computation | async-start | bytes 2228224 | tf_op jit(solution)/shard_map/all_to_all | solution.py:427
  39.5 1.9 %collective-permute-start.10 = (bf16[7,128,128]{2,1,0:T(8,128)(2,1)}, bf16[7,128,128]{2,1,0:T(8,128)(2,1)}, u32[]{:S(2)}, u32[]{:S(2)}) collective-permute-start(bf16[7,128,128]{2,1,0:T(8,128)(2,1)} %copy-done.8), channel_id=1, source_target_pairs={{0,2},{2,0},{4,6},{6,4},{8,10},{10,8},{12,14},{14,12},{16,18},{18,... | collective-permute-start | bytes 688136 | tf_op jit(solution)/shard_map/ppermute | solution.py:101
  39.8 8.7 %collective-permute-start.9 = (bf16[7,128,128]{2,1,0:T(8,128)(2,1)}, bf16[7,128,128]{2,1,0:T(8,128)(2,1)}, u32[]{:S(2)}, u32[]{:S(2)}) collective-permute-start(bf16[7,128,128]{2,1,0:T(8,128)(2,1)} %copy-done.6), channel_id=1, source_target_pairs={{1,0},{0,1},{3,2},{2,3},{5,4},{4,5},{7,6},{6,7},{9,8},{8,9},{11,10... | collective-permute-start | bytes 688136 | tf_op jit(solution)/shard_map/ppermute | solution.py:105
  41.4 12.7 %collective-permute-start.11 = (bf16[7,128,128]{2,1,0:T(8,128)(2,1)}, bf16[7,128,128]{2,1,0:T(8,128)(2,1)}, u32[]{:S(2)}, u32[]{:S(2)}) collective-permute-start(bf16[7,128,128]{2,1,0:T(8,128)(2,1)} %collective-permute-done.10.refs_2_), channel_id=1, source_target_pairs={{1,0},{0,1},{3,2},{2,3},{5,4},{4,5},{7,6},{6,7},{9,8},{8,9},{11,10... | collective-permute-start | bytes 688136 | tf_op jit(solution)/shard_map/ppermute | solution.py:105
  42.9 0.9 copy-start.16
  44.2 1.3 collective-permute-start.14
  44.3 9.6 %collective-permute-start.13 = (bf16[1,128,128]{2,1,0:T(8,128)(2,1)S(1)}, bf16[1,128,128]{2,1,0:T(8,128)(2,1)S(1)}, u32[]{:S(2)}, u32[]{:S(2)}) collective-permute-start(bf16[1,128,128]{2,1,0:T(8,128)(2,1)S(1)} %get-tuple-element.68.refs_4_), channel_id=1, source_target_pairs={{1,0},{0,1},{3,2},{2,3},{5,4},{4,5},{7,6},{6,7},{9,8},{8,9},{11,10... | collective-permute-start | bytes 98312 | tf_op jit(solution)/shard_map/ppermute | solution.py:105
  45.4 8.7 %collective-permute-start.15 = (bf16[1,128,128]{2,1,0:T(8,128)(2,1)S(1)}, bf16[1,128,128]{2,1,0:T(8,128)(2,1)S(1)}, u32[]{:S(2)}, u32[]{:S(2)}) collective-permute-start(bf16[1,128,128]{2,1,0:T(8,128)(2,1)S(1)} %collective-permute-done.14.refs_6_), channel_id=1, source_target_pairs={{1,0},{0,1},{3,2},{2,3},{5,4},{4,5},{7,6},{6,7},{9,8},{8,9},{11,10... | collective-permute-start | bytes 98312 | tf_op jit(solution)/shard_map/ppermute | solution.py:105
  54.2 0.9 copy-start.7
  55.1 0.9 copy-start.17
  56.1 0.9 copy-start.19
  59.7 0.7 copy-start.13
  63.6 17.9 %collective-permute-start.18 = (bf16[272,16,128]{2,0,1:T(8,128)(2,1)}, bf16[272,16,128]{2,0,1:T(8,128)(2,1)S(1)}, u32[]{:S(2)}, u32[]{:S(2)}) collective-permute-start(bf16[272,16,128]{2,0,1:T(8,128)(2,1)} %bitcast.5), channel_id=1, source_target_pairs={{0,2},{2,0},{4,6},{6,4},{8,10},{10,8},{12,14},{14,12},{16,18},{18,... | collective-permute-start | bytes 3342344 | tf_op jit(solution)/shard_map/ppermute | solution.py:101
  64.3 15.6 %collective-permute-start.17 = (bf16[128,2048]{1,0:T(8,128)(2,1)S(1)}, bf16[128,2048]{1,0:T(8,128)(2,1)S(1)}, u32[]{:S(2)}, u32[]{:S(2)}) collective-permute-start(bf16[128,2048]{1,0:T(8,128)(2,1)S(1)} %get-tuple-element.71.refs_4_), channel_id=1, source_target_pairs={{8,0},{10,2},{16,8},{18,10},{24,16},{26,18},{28,24},{30,26},{20,28... | collective-permute-start | bytes 1572872 | tf_op jit(solution)/shard_map/ppermute | solution.py:69
  66.3 15.1 %collective-permute-start.16 = (bf16[128,2048]{1,0:T(8,128)(2,1)S(1)}, bf16[128,2048]{1,0:T(8,128)(2,1)S(1)}, u32[]{:S(2)}, u32[]{:S(2)}) collective-permute-start(bf16[128,2048]{1,0:T(8,128)(2,1)S(1)} %get-tuple-element.71.refs_4_), channel_id=1, source_target_pairs={{8,16},{10,18},{16,24},{18,26},{24,28},{26,30},{28,20},{30,22},{20... | collective-permute-start | bytes 1572872 | tf_op jit(solution)/shard_map/ppermute | solution.py:69
  67.8 18.4 %collective-permute-start.21 = (bf16[704,2048]{1,0:T(8,128)(2,1)S(1)}, bf16[704,2048]{1,0:T(8,128)(2,1)S(1)}, u32[]{:S(2)}, u32[]{:S(2)}) collective-permute-start(bf16[704,2048]{1,0:T(8,128)(2,1)S(1)} %bitcast.46), channel_id=1, source_target_pairs={{0,2},{2,0},{4,6},{6,4},{8,10},{10,8},{12,14},{14,12},{16,18},{18,... | collective-permute-start | bytes 8650760 | tf_op jit(solution)/shard_map/ppermute | solution.py:101
  67.8 18.4 %collective-permute-start.22 = (bf16[704,2048]{1,0:T(8,128)(2,1)}, bf16[704,2048]{1,0:T(8,128)(2,1)S(1)}, u32[]{:S(2)}, u32[]{:S(2)}) collective-permute-start(bf16[704,2048]{1,0:T(8,128)(2,1)} %bitcast.51), channel_id=1, source_target_pairs={{0,2},{2,0},{4,6},{6,4},{8,10},{10,8},{12,14},{14,12},{16,18},{18,... | collective-permute-start | bytes 8650760 | tf_op jit(solution)/shard_map/ppermute | solution.py:101
  79.9 6.3 %collective-permute-start.23 = (bf16[704,2048]{1,0:T(8,128)(2,1)}, bf16[704,2048]{1,0:T(8,128)(2,1)S(1)}, u32[]{:S(2)}, u32[]{:S(2)}) collective-permute-start(bf16[704,2048]{1,0:T(8,128)(2,1)} %bitcast.56), channel_id=1, source_target_pairs={{0,2},{2,0},{4,6},{6,4},{8,10},{10,8},{12,14},{14,12},{16,18},{18,... | collective-permute-start | bytes 8650760 | tf_op jit(solution)/shard_map/ppermute | solution.py:101
  81.4 13.2 %collective-permute-start.19 = (bf16[128,2048]{1,0:T(8,128)(2,1)S(1)}, bf16[128,2048]{1,0:T(8,128)(2,1)S(1)}, u32[]{:S(2)}, u32[]{:S(2)}) collective-permute-start(bf16[128,2048]{1,0:T(8,128)(2,1)S(1)} %collective-permute-done.16.refs_2_), channel_id=1, source_target_pairs={{8,16},{10,18},{16,24},{18,26},{24,28},{26,30},{28,20},{30,22},{20... | collective-permute-start | bytes 1572872 | tf_op jit(solution)/shard_map/ppermute | solution.py:69
  82.1 14.0 %collective-permute-start.20 = (bf16[128,2048]{1,0:T(8,128)(2,1)S(1)}, bf16[128,2048]{1,0:T(8,128)(2,1)S(1)}, u32[]{:S(2)}, u32[]{:S(2)}) collective-permute-start(bf16[128,2048]{1,0:T(8,128)(2,1)S(1)} %collective-permute-done.17.refs_3_), channel_id=1, source_target_pairs={{8,0},{10,2},{16,8},{18,10},{24,16},{26,18},{28,24},{30,26},{20,28... | collective-permute-start | bytes 1572872 | tf_op jit(solution)/shard_map/ppermute | solution.py:69
  83.5 2.8 %copy-start.2 = (bf16[1,704,2048]{2,1,0:T(8,128)(2,1)S(1)}, bf16[1,704,2048]{2,1,0:T(8,128)(2,1)}, u32[]{:S(2)}) copy-start(bf16[1,704,2048]{2,1,0:T(8,128)(2,1)} %param.24) | copy-start | bytes 8650756
  85.1 2.0 %copy-start.1 = (bf16[1,2048,704]{1,2,0:T(8,128)(2,1)S(1)}, bf16[1,2048,704]{1,2,0:T(8,128)(2,1)}, u32[]{:S(2)}) copy-start(bf16[1,2048,704]{1,2,0:T(8,128)(2,1)} %param.23) | copy-start | bytes 8650756
  96.1 13.2 %collective-permute-start.26 = (bf16[256,1024]{1,0:T(8,128)(2,1)S(1)}, bf16[256,1024]{1,0:T(8,128)(2,1)S(1)}, u32[]{:S(2)}, u32[]{:S(2)}) collective-permute-start(bf16[256,1024]{1,0:T(8,128)(2,1)S(1)} %get-tuple-element.86), channel_id=1, source_target_pairs={{1,0},{0,1},{3,2},{2,3},{5,4},{4,5},{7,6},{6,7},{9,8},{8,9},{11,10... | collective-permute-start | bytes 1572872 | tf_op jit(solution)/shard_map/ppermute | solution.py:105
  97.6 12.9 %collective-permute-start.24 = (bf16[128,2048]{1,0:T(8,128)(2,1)S(1)}, bf16[128,2048]{1,0:T(8,128)(2,1)S(1)}, u32[]{:S(2)}, u32[]{:S(2)}) collective-permute-start(bf16[128,2048]{1,0:T(8,128)(2,1)S(1)} %collective-permute-done.19.refs_2_), channel_id=1, source_target_pairs={{8,16},{10,18},{16,24},{18,26},{24,28},{26,30},{28,20},{30,22},{20... | collective-permute-start | bytes 1572872 | tf_op jit(solution)/shard_map/ppermute | solution.py:69
  99.4 12.6 %collective-permute-start.25 = (bf16[128,2048]{1,0:T(8,128)(2,1)S(1)}, bf16[128,2048]{1,0:T(8,128)(2,1)S(1)}, u32[]{:S(2)}, u32[]{:S(2)}) collective-permute-start(bf16[128,2048]{1,0:T(8,128)(2,1)S(1)} %collective-permute-done.20.refs_3_), channel_id=1, source_target_pairs={{8,0},{10,2},{16,8},{18,10},{24,16},{26,18},{28,24},{30,26},{20,28... | collective-permute-start | bytes 1572872 | tf_op jit(solution)/shard_map/ppermute | solution.py:69
  112.0 15.5 %collective-permute-start.29 = (bf16[256,1024]{1,0:T(8,128)(2,1)S(1)}, bf16[256,1024]{1,0:T(8,128)(2,1)S(1)}, u32[]{:S(2)}, u32[]{:S(2)}) collective-permute-start(bf16[256,1024]{1,0:T(8,128)(2,1)S(1)} %get-tuple-element.90), channel_id=1, source_target_pairs={{1,0},{0,1},{3,2},{2,3},{5,4},{4,5},{7,6},{6,7},{9,8},{8,9},{11,10... | collective-permute-start | bytes 1572872 | tf_op jit(solution)/shard_map/ppermute | solution.py:105
  112.6 11.9 %collective-permute-start.28 = (bf16[64,2048]{1,0:T(8,128)(2,1)S(1)}, bf16[64,2048]{1,0:T(8,128)(2,1)S(1)}, u32[]{:S(2)}, u32[]{:S(2)}) collective-permute-start(bf16[64,2048]{1,0:T(8,128)(2,1)S(1)} %slice.77), channel_id=1, source_target_pairs={{8,0},{10,2},{16,8},{18,10},{24,16},{26,18},{28,24},{30,26},{20,28... | collective-permute-start | bytes 786440 | tf_op jit(solution)/shard_map/ppermute | solution.py:69
  112.9 13.2 %collective-permute-start.27 = (bf16[64,2048]{1,0:T(8,128)(2,1)S(1)}, bf16[64,2048]{1,0:T(8,128)(2,1)S(1)}, u32[]{:S(2)}, u32[]{:S(2)}) collective-permute-start(bf16[64,2048]{1,0:T(8,128)(2,1)S(1)} %slice.76), channel_id=1, source_target_pairs={{8,16},{10,18},{16,24},{18,26},{24,28},{26,30},{28,20},{30,22},{20... | collective-permute-start | bytes 786440 | tf_op jit(solution)/shard_map/ppermute | solution.py:69
  122.4 14.4 %collective-permute-start.31 = (bf16[128,1024]{1,0:T(8,128)(2,1)S(1)}, bf16[128,1024]{1,0:T(8,128)(2,1)S(1)}, u32[]{:S(2)}, u32[]{:S(2)}) collective-permute-start(bf16[128,1024]{1,0:T(8,128)(2,1)S(1)} %get-tuple-element.114), channel_id=1, source_target_pairs={{8,16},{10,18},{16,24},{18,26},{24,28},{26,30},{28,20},{30,22},{20... | collective-permute-start | bytes 786440 | tf_op jit(solution)/shard_map/ppermute | solution.py:69
  123.0 13.8 %collective-permute-start.35 = (bf16[128,1024]{1,0:T(8,128)(2,1)S(1)}, bf16[128,1024]{1,0:T(8,128)(2,1)S(1)}, u32[]{:S(2)}, u32[]{:S(2)}) collective-permute-start(bf16[128,1024]{1,0:T(8,128)(2,1)S(1)} %get-tuple-element.115), channel_id=1, source_target_pairs={{8,0},{10,2},{16,8},{18,10},{24,16},{26,18},{28,24},{30,26},{20,28... | collective-permute-start | bytes 786440 | tf_op jit(solution)/shard_map/ppermute | solution.py:69
  124.5 13.0 %collective-permute-start.32 = (bf16[128,1024]{1,0:T(8,128)(2,1)S(1)}, bf16[128,1024]{1,0:T(8,128)(2,1)S(1)}, u32[]{:S(2)}, u32[]{:S(2)}) collective-permute-start(bf16[128,1024]{1,0:T(8,128)(2,1)S(1)} %get-tuple-element.116), channel_id=1, source_target_pairs={{8,17},{9,16},{10,19},{11,18},{16,25},{17,24},{18,27},{19,26},{24,... | collective-permute-start | bytes 786440 | tf_op jit(solution)/shard_map/ppermute | solution.py:97
  126.1 11.4 %collective-permute-start.36 = (bf16[128,1024]{1,0:T(8,128)(2,1)S(1)}, bf16[128,1024]{1,0:T(8,128)(2,1)S(1)}, u32[]{:S(2)}, u32[]{:S(2)}) collective-permute-start(bf16[128,1024]{1,0:T(8,128)(2,1)S(1)} %get-tuple-element.117), channel_id=1, source_target_pairs={{8,1},{9,0},{10,3},{11,2},{16,9},{17,8},{18,11},{19,10},{24,17},{2... | collective-permute-start | bytes 786440 | tf_op jit(solution)/shard_map/ppermute | solution.py:97
  135.1 9.6 %collective-permute-start.39 = (bf16[128,1024]{1,0:T(8,128)(2,1)S(1)}, bf16[128,1024]{1,0:T(8,128)(2,1)S(1)}, u32[]{:S(2)}, u32[]{:S(2)}) collective-permute-start(bf16[128,1024]{1,0:T(8,128)(2,1)S(1)} %get-tuple-element.113), channel_id=1, source_target_pairs={{1,0},{0,1},{3,2},{2,3},{5,4},{4,5},{7,6},{6,7},{9,8},{8,9},{11,10... | collective-permute-start | bytes 786440 | tf_op jit(solution)/shard_map/ppermute | solution.py:105
  137.8 9.0 %collective-permute-start.33 = (bf16[128,1024]{1,0:T(8,128)(2,1)S(1)}, bf16[128,1024]{1,0:T(8,128)(2,1)S(1)}, u32[]{:S(2)}, u32[]{:S(2)}) collective-permute-start(bf16[128,1024]{1,0:T(8,128)(2,1)S(1)} %get-tuple-element.110), channel_id=1, source_target_pairs={{8,16},{10,18},{16,24},{18,26},{24,28},{26,30},{28,20},{30,22},{20... | collective-permute-start | bytes 786440 | tf_op jit(solution)/shard_map/ppermute | solution.py:69
  138.0 11.4 %collective-permute-start.37 = (bf16[128,1024]{1,0:T(8,128)(2,1)S(1)}, bf16[128,1024]{1,0:T(8,128)(2,1)S(1)}, u32[]{:S(2)}, u32[]{:S(2)}) collective-permute-start(bf16[128,1024]{1,0:T(8,128)(2,1)S(1)} %get-tuple-element.111), channel_id=1, source_target_pairs={{8,0},{10,2},{16,8},{18,10},{24,16},{26,18},{28,24},{30,26},{20,28... | collective-permute-start | bytes 786440 | tf_op jit(solution)/shard_map/ppermute | solution.py:69
  141.1 12.5 %collective-permute-start.30 = (bf16[128,1024]{1,0:T(8,128)(2,1)S(1)}, bf16[128,1024]{1,0:T(8,128)(2,1)S(1)}, u32[]{:S(2)}, u32[]{:S(2)}) collective-permute-start(bf16[128,1024]{1,0:T(8,128)(2,1)S(1)} %get-tuple-element.112), channel_id=1, source_target_pairs={{1,0},{0,1},{3,2},{2,3},{5,4},{4,5},{7,6},{6,7},{9,8},{8,9},{11,10... | collective-permute-start | bytes 786440 | tf_op jit(solution)/shard_map/ppermute | solution.py:105
  144.7 15.2 %copy-start.14 = (bf16[128,1024]{1,0:T(8,128)(2,1)S(1)}, bf16[128,1024]{1,0:T(8,128)(2,1)}, u32[]{:S(2)}) copy-start(bf16[128,1024]{1,0:T(8,128)(2,1)} %copy-done.13) | copy-start | bytes 786436
  144.8 10.1 %collective-permute-start.40 = (bf16[128,1024]{1,0:T(8,128)(2,1)S(1)}, bf16[128,1024]{1,0:T(8,128)(2,1)S(1)}, u32[]{:S(2)}, u32[]{:S(2)}) collective-permute-start(bf16[128,1024]{1,0:T(8,128)(2,1)S(1)} %add_convert_fusion.1), channel_id=1, source_target_pairs={{8,20},{10,22},{16,12},{18,14},{24,4},{26,6},{28,0},{30,2},{20,8},... | collective-permute-start | bytes 786440 | tf_op jit(solution)/shard_map/ppermute | solution.py:69
  149.6 14.3 %copy-start.22 = (f32[1024]{0:T(1024)S(1)}, f32[1024]{0:T(1024)}, u32[]{:S(2)}) copy-start(f32[1024]{0:T(1024)} %param.28) | copy-start | bytes 12292
  149.6 8.0 %collective-permute-start.34 = (bf16[128,1024]{1,0:T(8,128)(2,1)S(1)}, bf16[128,1024]{1,0:T(8,128)(2,1)S(1)}, u32[]{:S(2)}, u32[]{:S(2)}) collective-permute-start(bf16[128,1024]{1,0:T(8,128)(2,1)S(1)} %get-tuple-element.108), channel_id=1, source_target_pairs={{8,16},{10,18},{16,24},{18,26},{24,28},{26,30},{28,20},{30,22},{20... | collective-permute-start | bytes 786440 | tf_op jit(solution)/shard_map/ppermute | solution.py:69
  153.6 6.4 %collective-permute-start.38 = (bf16[128,1024]{1,0:T(8,128)(2,1)S(1)}, bf16[128,1024]{1,0:T(8,128)(2,1)S(1)}, u32[]{:S(2)}, u32[]{:S(2)}) collective-permute-start(bf16[128,1024]{1,0:T(8,128)(2,1)S(1)} %get-tuple-element.109), channel_id=1, source_target_pairs={{8,0},{10,2},{16,8},{18,10},{24,16},{26,18},{28,24},{30,26},{20,28... | collective-permute-start | bytes 786440 | tf_op jit(solution)/shard_map/ppermute | solution.py:69
  160.3 4.5 %copy-start.21 = (bf16[128,1024]{1,0:T(8,128)(2,1)}, bf16[128,1024]{1,0:T(8,128)(2,1)S(1)}, u32[]{:S(2)}) copy-start(bf16[128,1024]{1,0:T(8,128)(2,1)S(1)} %get-tuple-element.101) | copy-start | bytes 786436
  160.3 3.6 %collective-permute-start.41 = (f32[1,128]{1,0:T(1,128)S(1)}, f32[1,128]{1,0:T(1,128)S(1)}, u32[]{:S(2)}, u32[]{:S(2)}) collective-permute-start(f32[1,128]{1,0:T(1,128)S(1)} %bitcast.69), channel_id=1, source_target_pairs={{1,0},{0,1},{3,2},{2,3},{5,4},{4,5},{7,6},{6,7},{9,8},{8,9},{11,10... | collective-permute-start | bytes 1544 | tf_op jit(solution)/shard_map/ppermute | solution.py:105
  (2 other events, 1.4 us)

commit v3 on v2

--- a/solution.py
+++ b/solution.py
@@ -449,6 +449,9 @@
     def swap_mp(sent):
         return [moves.from_mp(sent[k - 1], mp_count - k) for k in range(1, mp_count)]
 
+    gate = moves.from_mp(normed[:16, :LANES], 1)
+    shared = [after(value, gate) for value in shared]
+    weights, scores = unpack(shared)
     ahead = behind = normed
     done = []
     for s in range(1, left + 1):
@@ -458,17 +461,16 @@
         if s <= right:
             moved = [moves.step(ahead, 1), moves.step(behind, -1)]
         else:
-            moved = [moves.step(ahead[: rows // 2], 1), moves.step(behind[rows // 2 :], -1)]
+            moved = [moves.step(ahead, 1)]
         if s > 1:
             came = done[-2][2] if s > 2 else []
             moved, ties, came = lax.optimization_barrier((moved, outs[1:], came))
             if s > 2:
                 done[-2][2] = came
-            done[-1][2] = swap_mp(ties)
+            done[-1][2] = swap_mp(outs[1:])
         else:
-            moved, shared = lax.optimization_barrier((moved, shared))
-            weights, scores = unpack(shared)
-        ahead, behind = blocks = moved
+            moved, weights[3:6], scores = lax.optimization_barrier((moved, weights[3:6], scores))
+        ahead, behind, blocks = moved[0], moved[-1], moved
         listed = [-s, s] if s <= right else [s]
     outs = ffn([*listed, 0], [*blocks, normed], scores, weights, info, mp_count)
     for start, stop, offsets in (

time: 166 us -> 163 us (0.982)
  waiting for transfers between devices: 61.1 us -> 56.4 us
  starting transfers between devices: 50.2 us -> 52.8 us
    ppermute x22 -> x21, waiting for transfers between devices: 41.4 us -> 36.2 us  [step(): return lax.ppermute(value, 'dp', pairs)]
    ppermute x11 -> x12, starting transfers between devices: 11.5 us -> 13.5 us  [from_mp(): lax.ppermute(value, 'mp', [((i + k) % count, i) for i in range(count)])]
    unnamed x50 -> x48, local copies, waits for them, and re-layouts: 12 us -> 10.9 us
    ppermute x11 -> x12, waiting for transfers between devices: 15.1 us -> 15.7 us  [from_mp(): lax.ppermute(value, 'mp', [((i + k) % count, i) for i in range(count)])]
    ppermute x22 -> x21, starting transfers between devices: 29.6 us -> 30.1 us  [step(): return lax.ppermute(value, 'dp', pairs)]
  transfers between devices with their start and end apart: 43 -> 43, of which waited for: 25 -> 26; matrix products, arithmetic and copies ran while one was open for 4% -> 4% of each run, Pallas kernels for 21% -> 22%
where the time goes in v3:
time: 163 us; the launch traced here: 162 us
  waiting for transfers between devices  56.4 us (35%)
  starting transfers between devices  52.8 us (32%)
  Pallas kernels  34.9 us (21%)
  local copies, waits for them, and re-layouts  11.9 us (7%)
  other arithmetic  4.76 us (3%)
    ppermute x21, waiting for transfers between devices, step(): return lax.ppermute(value, 'dp', pairs)  36.2 us
    pallas_call x4, Pallas kernels, ffn(): pl.pallas_call(functools.partial(ffn_kernel, offsets, len(tokens), mp_cou...  30.2 us
    ppermute x21, starting transfers between devices, step(): return lax.ppermute(value, 'dp', pairs)  30.1 us
    ppermute x12, waiting for transfers between devices, from_mp(): lax.ppermute(value, 'mp', [((i + k) % count, i) for i in range(count)])  15.7 us
    ppermute x12, starting transfers between devices, from_mp(): lax.ppermute(value, 'mp', [((i + k) % count, i) for i in range(count)])  13.5 us
    unnamed x48, local copies, waits for them, and re-layouts  10.9 us
    all_to_all x1, starting transfers between devices, local(): shared = lax.all_to_all(after(shared, ahead), 'dp', 0, 0, tiled=True)  4.65 us
  transfers between devices with their start and end apart: 43, of which 26 were waited for; matrix products, arithmetic and copies ran while one was open for 4% of the time, Pallas kernels for 22%

profile of v3, /device:TPU:0, one launch (start us, length us, event | category | flops | bytes accessed | tf_op | source)
XLA Modules:
  0.0 161.9 jit_solution(14372815558624203513)
XLA Ops:
  0.6 3.1 %collective-permute-start.1 = (bf16[1024,128]{1,0:T(8,128)(2,1)}, bf16[1024,128]{1,0:T(8,128)(2,1)S(1)}, u32[]{:S(2)}, u32[]{:S(2)}) collective-permute-start(bf16[1024,128]{1,0:T(8,128)(2,1)} %refs_2_.1), channel_id=1, source_target_pairs={{8,16},{10,18},{16,24},{18,26},{24,28},{26,30},{28,20},{30,22},{20... | collective-permute-start | bytes 786440 | tf_op jit(solution)/shard_map/ppermute | solution.py:69
  3.7 6.4 %collective-permute-done.1.refs_3_ = bf16[1024,128]{1,0:T(8,128)(2,1)S(1)} collective-permute-done((bf16[1024,128]{1,0:T(8,128)(2,1)}, bf16[1024,128]{1,0:T(8,128)(2,1)S(1)}, u32[]{:S(2)}, u32[]{:S(2)}) %collective-permute-start.1) | collective-permute-done | bytes 262176 | tf_op jit(solution)/shard_map/ppermute | solution.py:69
  10.2 1.5 collective-permute-done.2.refs_4_
  11.7 1.6 collective-permute-start.3
  13.7 1.5 collective-permute-start.8
  15.7 0.8 select_reduce_fusion.1
  16.5 0.8 select_reduce_fusion
  17.3 0.9 copy-done.4
  18.3 0.9 copy-done.12
  19.8 1.6 collective-permute-start.5
  22.3 1.0 copy-done.3
  23.8 2.5 %collective-permute-done.5.refs_2_ = bf16[1024,128]{1,0:T(8,128)(2,1)S(1)} collective-permute-done((bf16[1024,128]{1,0:T(8,128)(2,1)S(1)}, bf16[1024,128]{1,0:T(8,128)(2,1)S(1)}, u32[]{:S(2)}, u32[]{:S(2)}) %collective-permute-start.5) | collective-permute-done | bytes 262176 | tf_op jit(solution)/shard_map/ppermute | solution.py:69
  26.2 1.6 collective-permute-done.6.refs_3_
  27.8 1.6 collective-permute-start.12
  31.2 3.0 %collective-permute-done.12.refs_2_ = bf16[1024,128]{1,0:T(8,128)(2,1)S(1)} collective-permute-done((bf16[1024,128]{1,0:T(8,128)(2,1)S(1)}, bf16[1024,128]{1,0:T(8,128)(2,1)S(1)}, u32[]{:S(2)}, u32[]{:S(2)}) %collective-permute-start.12) | collective-permute-done | bytes 262176 | tf_op jit(solution)/shard_map/ppermute | solution.py:69
  34.2 0.7 copy-done.15
  34.9 4.6 %all-to-all-start = ((bf16[16,272,128]{2,1,0:T(8,128)(2,1)}), bf16[16,272,128]{2,1,0:T(8,128)(2,1)}, u32[]{:S(2)}, u32[]{:S(2)}) async-start(bf16[16,272,128]{2,1,0:T(8,128)(2,1)} %copy-done.3), calls=%async_computation | async-start | bytes 2228224 | tf_op jit(solution)/shard_map/all_to_all | solution.py:427
  39.8 1.5 collective-permute-start.9
  41.4 1.5 collective-permute-start.11
  42.9 0.9 copy-done.16
  45.4 0.9 collective-permute-start.15
  47.0 1.5 collective-permute-done.9.refs_1_
  48.5 5.3 %collective-permute-done.13.refs_5_ = bf16[1,128,128]{2,1,0:T(8,128)(2,1)S(1)} collective-permute-done((bf16[1,128,128]{2,1,0:T(8,128)(2,1)S(1)}, bf16[1,128,128]{2,1,0:T(8,128)(2,1)S(1)}, u32[]{:S(2)}, u32[]{:S(2)}) %collective-permute-start.13) | collective-permute-done | bytes 32800 | tf_op jit(solution)/shard_map/ppermute | solution.py:105
  54.2 0.9 copy-done.7
  55.1 0.9 copy-done.17
  56.1 0.9 copy-done.19
  57.0 2.7 %shard_map.163 = (bf16[128,2048]{1,0:T(8,128)(2,1)S(1)}, bf16[128,1024]{1,0:T(8,128)(2,1)S(1)}) custom-call(s32[10]{0:T(128)S(1)} %dynamic-slice_bitcast_fusion.info_ref, bf16[7,128,128]{2,1,0:T(8,128)(2,1)S(1)} %copy-done.7, bf16[7,128,128]{2,1,0:T(8,128)(2,1)} %collective-permute-done.9.refs_1_, bf16[7,128,128]{2,1,0:T(8,128)(2,1)} %collective-permute-done.10.refs_2_, ...), custom_call_target="tpu_custom_call" | custom-call | flops 1 | bytes 1 | tf_op jit(solution)/shard_map/pallas_call | solution.py:238
  60.4 3.2 %all-to-all-done = bf16[16,272,128]{2,1,0:T(8,128)(2,1)} async-done(((bf16[16,272,128]{2,1,0:T(8,128)(2,1)}), bf16[16,272,128]{2,1,0:T(8,128)(2,1)}, u32[]{:S(2)}, u32[]{:S(2)}) %all-to-all-start) | async-done | bytes 1114144 | tf_op jit(solution)/shard_map/all_to_all | solution.py:427
  63.6 0.7 collective-permute-start.19
  64.3 1.5 collective-permute-start.18
  66.3 1.6 collective-permute-done.18
  67.9 2.1 %collective-permute-start.17 = (bf16[128,2048]{1,0:T(8,128)(2,1)S(1)}, bf16[128,2048]{1,0:T(8,128)(2,1)S(1)}, u32[]{:S(2)}, u32[]{:S(2)}) collective-permute-start(bf16[128,2048]{1,0:T(8,128)(2,1)S(1)} %get-tuple-element.73.refs_3_), channel_id=1, source_target_pairs={{8,0},{10,2},{16,8},{18,10},{24,16},{26,18},{28,24},{30,26},{20,28... | collective-permute-start | bytes 1572872 | tf_op jit(solution)/shard_map/ppermute | solution.py:69
  70.0 1.3 slice_bitcast_fusion.1
  71.3 1.5 collective-permute-start.16
  73.2 1.0 convert_reduce_fusion
  74.3 8.1 %collective-permute-done.17.refs_3_ = bf16[128,2048]{1,0:T(8,128)(2,1)S(1)} collective-permute-done((bf16[128,2048]{1,0:T(8,128)(2,1)S(1)}, bf16[128,2048]{1,0:T(8,128)(2,1)S(1)}, u32[]{:S(2)}, u32[]{:S(2)}) %collective-permute-start.17) | collective-permute-done | bytes 524320 | tf_op jit(solution)/shard_map/ppermute | solution.py:69
  82.4 2.9 %collective-permute-done.16.refs_2_ = bf16[128,2048]{1,0:T(8,128)(2,1)S(1)} collective-permute-done((bf16[128,2048]{1,0:T(8,128)(2,1)S(1)}, bf16[128,2048]{1,0:T(8,128)(2,1)S(1)}, u32[]{:S(2)}, u32[]{:S(2)}) %collective-permute-start.16) | collective-permute-done | bytes 524320 | tf_op jit(solution)/shard_map/ppermute | solution.py:69
  85.6 1.7 %collective-permute-start.21 = (bf16[128,2048]{1,0:T(8,128)(2,1)S(1)}, bf16[128,2048]{1,0:T(8,128)(2,1)S(1)}, u32[]{:S(2)}, u32[]{:S(2)}) collective-permute-start(bf16[128,2048]{1,0:T(8,128)(2,1)S(1)} %collective-permute-done.17.refs_3_), channel_id=1, source_target_pairs={{8,0},{10,2},{16,8},{18,10},{24,16},{26,18},{28,24},{30,26},{20,28... | collective-permute-start | bytes 1572872 | tf_op jit(solution)/shard_map/ppermute | solution.py:69
  87.4 7.5 %shard_map.164 = (f32[256,1024]{1,0:T(8,128)S(1)}, bf16[256,1024]{1,0:T(8,128)(2,1)S(1)}) custom-call(s32[10]{0:T(128)S(1)} %dynamic-slice_bitcast_fusion.info_ref, f32[16,128]{1,0:T(8,128)S(1)} %get-tuple-element.79.refs_0_, f32[16,128]{1,0:T(8,128)S(1)} %get-tuple-element.80.refs_1_, bf16[128,2048]{1,0:T(8,128)(2,1)S(1)} %collective-permute-done.16.refs_2_, ...), custom_call_target="tpu_custom_call" | custom-call | flops 1 | bytes 1 | tf_op jit(solution)/shard_map/pallas_call | solution.py:314
  94.9 1.5 collective-permute-start.27
  96.5 0.8 collective-permute-done.20.refs_2_
  97.6 1.8 %collective-permute-start.25 = (bf16[128,2048]{1,0:T(8,128)(2,1)S(1)}, bf16[128,2048]{1,0:T(8,128)(2,1)S(1)}, u32[]{:S(2)}, u32[]{:S(2)}) collective-permute-start(bf16[128,2048]{1,0:T(8,128)(2,1)S(1)} %collective-permute-done.20.refs_2_), channel_id=1, source_target_pairs={{8,16},{10,18},{16,24},{18,26},{24,28},{26,30},{28,20},{30,22},{20... | collective-permute-start | bytes 1572872 | tf_op jit(solution)/shard_map/ppermute | solution.py:69
  99.6 7.6 %shard_map.165 = (f32[256,1024]{1,0:T(8,128)S(1)}, bf16[256,1024]{1,0:T(8,128)(2,1)S(1)}) custom-call(s32[10]{0:T(128)S(1)} %dynamic-slice_bitcast_fusion.info_ref, f32[16,128]{1,0:T(8,128)S(1)} %get-tuple-element.79.refs_0_, f32[16,128]{1,0:T(8,128)S(1)} %get-tuple-element.80.refs_1_, bf16[128,2048]{1,0:T(8,128)(2,1)S(1)} %collective-permute-done.20.refs_2_, ...), custom_call_target="tpu_custom_call" | custom-call | flops 1 | bytes 1 | tf_op jit(solution)/shard_map/pallas_call | solution.py:314
  107.2 1.6 collective-permute-start.29
  108.8 1.2 collective-permute-done.26.refs_3_
  109.9 1.7 %collective-permute-start.28 = (bf16[128,2048]{1,0:T(8,128)(2,1)S(1)}, bf16[128,2048]{1,0:T(8,128)(2,1)S(1)}, u32[]{:S(2)}, u32[]{:S(2)}) collective-permute-start(bf16[128,2048]{1,0:T(8,128)(2,1)S(1)} %collective-permute-done.25.refs_2_), channel_id=1, source_target_pairs={{8,16},{10,18},{16,24},{18,26},{24,28},{26,30},{28,20},{30,22},{20... | collective-permute-start | bytes 1572872 | tf_op jit(solution)/shard_map/ppermute | solution.py:69
  111.7 7.6 %shard_map.166 = (f32[256,1024]{1,0:T(8,128)S(1)}, bf16[256,1024]{1,0:T(8,128)(2,1)S(1)}) custom-call(s32[10]{0:T(128)S(1)} %dynamic-slice_bitcast_fusion.info_ref, f32[16,128]{1,0:T(8,128)S(1)} %get-tuple-element.79.refs_0_, f32[16,128]{1,0:T(8,128)S(1)} %get-tuple-element.80.refs_1_, bf16[128,2048]{1,0:T(8,128)(2,1)S(1)} %collective-permute-done.25.refs_2_, ...), custom_call_target="tpu_custom_call" | custom-call | flops 1 | bytes 1 | tf_op jit(solution)/shard_map/pallas_call | solution.py:314
  119.4 1.1 collective-permute-start.31
  120.5 1.0 collective-permute-start.35
  121.5 2.0 %collective-permute-start.32 = (bf16[128,1024]{1,0:T(8,128)(2,1)S(1)}, bf16[128,1024]{1,0:T(8,128)(2,1)S(1)}, u32[]{:S(2)}, u32[]{:S(2)}) collective-permute-start(bf16[128,1024]{1,0:T(8,128)(2,1)S(1)} %get-tuple-element.120), channel_id=1, source_target_pairs={{8,17},{9,16},{10,19},{11,18},{16,25},{17,24},{18,27},{19,26},{24,... | collective-permute-start | bytes 786440 | tf_op jit(solution)/shard_map/ppermute | solution.py:97
  123.5 1.0 collective-permute-start.36
  124.8 7.5 %shard_map.167 = (f32[256,1024]{1,0:T(8,128)S(1)}, bf16[256,1024]{1,0:T(8,128)(2,1)S(1)}) custom-call(s32[10]{0:T(128)S(1)} %dynamic-slice_bitcast_fusion.info_ref, f32[16,128]{1,0:T(8,128)S(1)} %get-tuple-element.79.refs_0_, f32[16,128]{1,0:T(8,128)S(1)} %get-tuple-element.80.refs_1_, bf16[128,2048]{1,0:T(8,128)(2,1)S(1)} %collective-permute-done.28.refs_2_, ...), custom_call_target="tpu_custom_call" | custom-call | flops 1 | bytes 1 | tf_op jit(solution)/shard_map/pallas_call | solution.py:314
  132.4 1.5 collective-permute-start.39
  135.0 1.5 collective-permute-start.33
  136.5 0.7 collective-permute-start.37
  137.4 0.8 collective-permute-start.30
  138.1 3.4 %collective-permute-done.39 = bf16[128,1024]{1,0:T(8,128)(2,1)S(1)} collective-permute-done((bf16[128,1024]{1,0:T(8,128)(2,1)S(1)}, bf16[128,1024]{1,0:T(8,128)(2,1)S(1)}, u32[]{:S(2)}, u32[]{:S(2)}) %collective-permute-start.39) | collective-permute-done | bytes 262176 | tf_op jit(solution)/shard_map/ppermute | solution.py:105
  141.6 2.1 %collective-permute-start.40 = (bf16[128,1024]{1,0:T(8,128)(2,1)S(1)}, bf16[128,1024]{1,0:T(8,128)(2,1)S(1)}, u32[]{:S(2)}, u32[]{:S(2)}) collective-permute-start(bf16[128,1024]{1,0:T(8,128)(2,1)S(1)} %add_convert_fusion.1), channel_id=1, source_target_pairs={{8,20},{10,22},{16,12},{18,14},{24,4},{26,6},{28,0},{30,2},{20,8},... | collective-permute-start | bytes 786440 | tf_op jit(solution)/shard_map/ppermute | solution.py:69
  145.2 5.6 %collective-permute-start.34 = (bf16[128,1024]{1,0:T(8,128)(2,1)S(1)}, bf16[128,1024]{1,0:T(8,128)(2,1)S(1)}, u32[]{:S(2)}, u32[]{:S(2)}) collective-permute-start(bf16[128,1024]{1,0:T(8,128)(2,1)S(1)} %get-tuple-element.112), channel_id=1, source_target_pairs={{8,16},{10,18},{16,24},{18,26},{24,28},{26,30},{28,20},{30,22},{20... | collective-permute-start | bytes 786440 | tf_op jit(solution)/shard_map/ppermute | solution.py:69
  150.8 1.3 collective-permute-done.40
  152.0 2.6 %collective-permute-done.34 = bf16[128,1024]{1,0:T(8,128)(2,1)S(1)} collective-permute-done((bf16[128,1024]{1,0:T(8,128)(2,1)S(1)}, bf16[128,1024]{1,0:T(8,128)(2,1)S(1)}, u32[]{:S(2)}, u32[]{:S(2)}) %collective-permute-start.34) | collective-permute-done | bytes 262176 | tf_op jit(solution)/shard_map/ppermute | solution.py:69
  154.6 2.5 %collective-permute-done.38 = bf16[128,1024]{1,0:T(8,128)(2,1)S(1)} collective-permute-done((bf16[128,1024]{1,0:T(8,128)(2,1)S(1)}, bf16[128,1024]{1,0:T(8,128)(2,1)S(1)}, u32[]{:S(2)}, u32[]{:S(2)}) %collective-permute-start.38) | collective-permute-done | bytes 262176 | tf_op jit(solution)/shard_map/ppermute | solution.py:69
  157.5 3.5 %collective-permute-done.41 = f32[1,128]{1,0:T(1,128)S(1)} collective-permute-done((f32[1,128]{1,0:T(1,128)S(1)}, f32[1,128]{1,0:T(1,128)S(1)}, u32[]{:S(2)}, u32[]{:S(2)}) %collective-permute-start.41) | collective-permute-done | bytes 544 | tf_op jit(solution)/shard_map/ppermute | solution.py:105
  161.1 0.8 fusion.2
  (105 shorter events, 13.7 us)
Async XLA Ops:
  0.6 9.5 %collective-permute-start.1 = (bf16[1024,128]{1,0:T(8,128)(2,1)}, bf16[1024,128]{1,0:T(8,128)(2,1)S(1)}, u32[]{:S(2)}, u32[]{:S(2)}) collective-permute-start(bf16[1024,128]{1,0:T(8,128)(2,1)} %refs_2_.1), channel_id=1, source_target_pairs={{8,16},{10,18},{16,24},{18,26},{24,28},{26,30},{28,20},{30,22},{20... | collective-permute-start | bytes 786440 | tf_op jit(solution)/shard_map/ppermute | solution.py:69
  3.7 8.0 %collective-permute-start.2 = (bf16[1024,128]{1,0:T(8,128)(2,1)}, bf16[1024,128]{1,0:T(8,128)(2,1)S(1)}, u32[]{:S(2)}, u32[]{:S(2)}) collective-permute-start(bf16[1024,128]{1,0:T(8,128)(2,1)} %refs_2_.1), channel_id=1, source_target_pairs={{8,0},{10,2},{16,8},{18,10},{24,16},{26,18},{28,24},{30,26},{20,28... | collective-permute-start | bytes 786440 | tf_op jit(solution)/shard_map/ppermute | solution.py:69
  3.7 13.6 %collective-permute-start = (bf16[128,1024]{1,0:T(8,128)(2,1)}, bf16[128,1024]{1,0:T(8,128)(2,1)S(1)}, u32[]{:S(2)}, u32[]{:S(2)}) collective-permute-start(bf16[128,1024]{1,0:T(8,128)(2,1)} %refs_0_.7), channel_id=1, source_target_pairs={{0,2},{2,0},{4,6},{6,4},{8,10},{10,8},{12,14},{14,12},{16,18},{18,... | collective-permute-start | bytes 786440 | tf_op jit(solution)/shard_map/ppermute | solution.py:101
  11.7 8.1 %collective-permute-start.3 = (bf16[1024,128]{1,0:T(8,128)(2,1)S(1)}, bf16[1024,128]{1,0:T(8,128)(2,1)S(1)}, u32[]{:S(2)}, u32[]{:S(2)}) collective-permute-start(bf16[1024,128]{1,0:T(8,128)(2,1)S(1)} %collective-permute-done.1.refs_3_), channel_id=1, source_target_pairs={{8,16},{10,18},{16,24},{18,26},{24,28},{26,30},{28,20},{30,22},{20... | collective-permute-start | bytes 786440 | tf_op jit(solution)/shard_map/ppermute | solution.py:69
  13.3 6.6 %collective-permute-start.4 = (bf16[1024,128]{1,0:T(8,128)(2,1)S(1)}, bf16[1024,128]{1,0:T(8,128)(2,1)S(1)}, u32[]{:S(2)}, u32[]{:S(2)}) collective-permute-start(bf16[1024,128]{1,0:T(8,128)(2,1)S(1)} %collective-permute-done.2.refs_4_), channel_id=1, source_target_pairs={{8,0},{10,2},{16,8},{18,10},{24,16},{26,18},{28,24},{30,26},{20,28... | collective-permute-start | bytes 786440 | tf_op jit(solution)/shard_map/ppermute | solution.py:69
  13.7 10.0 %collective-permute-start.8 = (f32[1,1024]{1,0:T(1,128)}, f32[1,1024]{1,0:T(1,128)S(1)}, u32[]{:S(2)}, u32[]{:S(2)}) collective-permute-start(f32[1,1024]{1,0:T(1,128)} %bitcast.61), channel_id=1, source_target_pairs={{1,0},{0,1},{3,2},{2,3},{5,4},{4,5},{7,6},{6,7},{9,8},{8,9},{11,10... | collective-permute-start | bytes 12296 | tf_op jit(solution)/shard_map/ppermute | solution.py:105
  15.2 8.5 %collective-permute-start.7 = (bf16[128,1024]{1,0:T(8,128)(2,1)}, bf16[128,1024]{1,0:T(8,128)(2,1)S(1)}, u32[]{:S(2)}, u32[]{:S(2)}) collective-permute-start(bf16[128,1024]{1,0:T(8,128)(2,1)} %refs_8_.1), channel_id=1, source_target_pairs={{1,0},{0,1},{3,2},{2,3},{5,4},{4,5},{7,6},{6,7},{9,8},{8,9},{11,10... | collective-permute-start | bytes 786440 | tf_op jit(solution)/shard_map/ppermute | solution.py:105
  17.3 1.0 copy-start.4
  18.2 0.9 copy-start.12
  19.2 2.7 %copy-start.9 = (bf16[128,1408]{1,0:T(8,128)(2,1)S(1)}, bf16[128,1408]{1,0:T(8,128)(2,1)}, u32[]{:S(2)}) copy-start(bf16[128,1408]{1,0:T(8,128)(2,1)} %gate_ref.1) | copy-start | bytes 1081348
  19.2 2.7 %copy-start.10 = (bf16[128,1408]{1,0:T(8,128)(2,1)S(1)}, bf16[128,1408]{1,0:T(8,128)(2,1)}, u32[]{:S(2)}) copy-start(bf16[128,1408]{1,0:T(8,128)(2,1)} %up_ref.1) | copy-start | bytes 1081348
  19.2 2.7 %copy-start.11 = (bf16[1408,128]{1,0:T(8,128)(2,1)S(1)}, bf16[1408,128]{1,0:T(8,128)(2,1)}, u32[]{:S(2)}) copy-start(bf16[1408,128]{1,0:T(8,128)(2,1)} %down_ref.1) | copy-start | bytes 1081348
  19.8 3.5 %copy-start.5 = (bf16[128,1024]{1,0:T(8,128)(2,1)S(1)}, bf16[128,1024]{1,0:T(8,128)(2,1)}, u32[]{:S(2)}) copy-start(bf16[128,1024]{1,0:T(8,128)(2,1)} %refs_0_.7) | copy-start | bytes 786436
  19.8 6.4 %collective-permute-start.5 = (bf16[1024,128]{1,0:T(8,128)(2,1)S(1)}, bf16[1024,128]{1,0:T(8,128)(2,1)S(1)}, u32[]{:S(2)}, u32[]{:S(2)}) collective-permute-start(bf16[1024,128]{1,0:T(8,128)(2,1)S(1)} %collective-permute-done.3.refs_2_), channel_id=1, source_target_pairs={{8,16},{10,18},{16,24},{18,26},{24,28},{26,30},{28,20},{30,22},{20... | collective-permute-start | bytes 786440 | tf_op jit(solution)/shard_map/ppermute | solution.py:69
  21.4 6.4 %collective-permute-start.6 = (bf16[1024,128]{1,0:T(8,128)(2,1)S(1)}, bf16[1024,128]{1,0:T(8,128)(2,1)S(1)}, u32[]{:S(2)}, u32[]{:S(2)}) collective-permute-start(bf16[1024,128]{1,0:T(8,128)(2,1)S(1)} %collective-permute-done.4.refs_3_), channel_id=1, source_target_pairs={{8,0},{10,2},{16,8},{18,10},{24,16},{26,18},{28,24},{30,26},{20,28... | collective-permute-start | bytes 786440 | tf_op jit(solution)/shard_map/ppermute | solution.py:69
  22.3 1.0 copy-start.3
  23.8 11.1 %copy-start.18 = (bf16[128,1024]{1,0:T(8,128)(2,1)}, bf16[128,1024]{1,0:T(8,128)(2,1)S(1)}, u32[]{:S(2)}) copy-start(bf16[128,1024]{1,0:T(8,128)(2,1)S(1)} %collective-permute-done.7.refs_9_) | copy-start | bytes 786436
  27.8 6.4 %collective-permute-start.12 = (bf16[1024,128]{1,0:T(8,128)(2,1)S(1)}, bf16[1024,128]{1,0:T(8,128)(2,1)S(1)}, u32[]{:S(2)}, u32[]{:S(2)}) collective-permute-start(bf16[1024,128]{1,0:T(8,128)(2,1)S(1)} %collective-permute-done.5.refs_2_), channel_id=1, source_target_pairs={{8,16},{10,18},{16,24},{18,26},{24,28},{26,30},{28,20},{30,22},{20... | collective-permute-start | bytes 786440 | tf_op jit(solution)/shard_map/ppermute | solution.py:69
  29.4 24.8 %copy-start.20 = (f32[1024]{0:T(1024)S(1)}, f32[1024]{0:T(1024)}, u32[]{:S(2)}) copy-start(f32[1024]{0:T(1024)} %param.18) | copy-start | bytes 12292
  34.2 0.7 copy-start.15
  34.9 30.9 %copy-start = (bf16[1,2048,704]{1,2,0:T(8,128)(2,1)S(1)}, bf16[1,2048,704]{1,2,0:T(8,128)(2,1)}, u32[]{:S(2)}) copy-start(bf16[1,2048,704]{1,2,0:T(8,128)(2,1)} %param.22) | copy-start | bytes 8650756
  34.9 28.7 %all-to-all-start = ((bf16[16,272,128]{2,1,0:T(8,128)(2,1)}), bf16[16,272,128]{2,1,0:T(8,128)(2,1)}, u32[]{:S(2)}, u32[]{:S(2)}) async-start(bf16[16,272,128]{2,1,0:T(8,128)(2,1)} %copy-done.3), calls=%async_computation | async-start | bytes 2228224 | tf_op jit(solution)/shard_map/all_to_all | solution.py:427
  39.5 1.9 %collective-permute-start.10 = (bf16[7,128,128]{2,1,0:T(8,128)(2,1)}, bf16[7,128,128]{2,1,0:T(8,128)(2,1)}, u32[]{:S(2)}, u32[]{:S(2)}) collective-permute-start(bf16[7,128,128]{2,1,0:T(8,128)(2,1)} %copy-done.8), channel_id=1, source_target_pairs={{0,2},{2,0},{4,6},{6,4},{8,10},{10,8},{12,14},{14,12},{16,18},{18,... | collective-permute-start | bytes 688136 | tf_op jit(solution)/shard_map/ppermute | solution.py:101
  39.8 8.7 %collective-permute-start.9 = (bf16[7,128,128]{2,1,0:T(8,128)(2,1)}, bf16[7,128,128]{2,1,0:T(8,128)(2,1)}, u32[]{:S(2)}, u32[]{:S(2)}) collective-permute-start(bf16[7,128,128]{2,1,0:T(8,128)(2,1)} %copy-done.6), channel_id=1, source_target_pairs={{1,0},{0,1},{3,2},{2,3},{5,4},{4,5},{7,6},{6,7},{9,8},{8,9},{11,10... | collective-permute-start | bytes 688136 | tf_op jit(solution)/shard_map/ppermute | solution.py:105
  41.4 12.7 %collective-permute-start.11 = (bf16[7,128,128]{2,1,0:T(8,128)(2,1)}, bf16[7,128,128]{2,1,0:T(8,128)(2,1)}, u32[]{:S(2)}, u32[]{:S(2)}) collective-permute-start(bf16[7,128,128]{2,1,0:T(8,128)(2,1)} %collective-permute-done.10.refs_2_), channel_id=1, source_target_pairs={{1,0},{0,1},{3,2},{2,3},{5,4},{4,5},{7,6},{6,7},{9,8},{8,9},{11,10... | collective-permute-start | bytes 688136 | tf_op jit(solution)/shard_map/ppermute | solution.py:105
  42.9 0.9 copy-start.16
  44.2 1.3 collective-permute-start.14
  44.3 9.6 %collective-permute-start.13 = (bf16[1,128,128]{2,1,0:T(8,128)(2,1)S(1)}, bf16[1,128,128]{2,1,0:T(8,128)(2,1)S(1)}, u32[]{:S(2)}, u32[]{:S(2)}) collective-permute-start(bf16[1,128,128]{2,1,0:T(8,128)(2,1)S(1)} %get-tuple-element.70.refs_4_), channel_id=1, source_target_pairs={{1,0},{0,1},{3,2},{2,3},{5,4},{4,5},{7,6},{6,7},{9,8},{8,9},{11,10... | collective-permute-start | bytes 98312 | tf_op jit(solution)/shard_map/ppermute | solution.py:105
  45.4 8.7 %collective-permute-start.15 = (bf16[1,128,128]{2,1,0:T(8,128)(2,1)S(1)}, bf16[1,128,128]{2,1,0:T(8,128)(2,1)S(1)}, u32[]{:S(2)}, u32[]{:S(2)}) collective-permute-start(bf16[1,128,128]{2,1,0:T(8,128)(2,1)S(1)} %collective-permute-done.14.refs_6_), channel_id=1, source_target_pairs={{1,0},{0,1},{3,2},{2,3},{5,4},{4,5},{7,6},{6,7},{9,8},{8,9},{11,10... | collective-permute-start | bytes 98312 | tf_op jit(solution)/shard_map/ppermute | solution.py:105
  54.2 0.9 copy-start.7
  55.1 0.9 copy-start.17
  56.1 0.9 copy-start.19
  59.7 0.7 copy-start.13
  63.6 7.8 %collective-permute-start.19 = (bf16[272,16,128]{2,0,1:T(8,128)(2,1)}, bf16[272,16,128]{2,0,1:T(8,128)(2,1)S(1)}, u32[]{:S(2)}, u32[]{:S(2)}) collective-permute-start(bf16[272,16,128]{2,0,1:T(8,128)(2,1)} %bitcast.5), channel_id=1, source_target_pairs={{0,2},{2,0},{4,6},{6,4},{8,10},{10,8},{12,14},{14,12},{16,18},{18,... | collective-permute-start | bytes 3342344 | tf_op jit(solution)/shard_map/ppermute | solution.py:101
  64.3 3.6 %collective-permute-start.18 = (bf16[16,128]{1,0:T(8,128)(2,1)S(1)}, bf16[16,128]{1,0:T(8,128)(2,1)S(1)}, u32[]{:S(2)}, u32[]{:S(2)}) collective-permute-start(bf16[16,128]{1,0:T(8,128)(2,1)S(1)} %slice.65), channel_id=1, source_target_pairs={{1,0},{0,1},{3,2},{2,3},{5,4},{4,5},{7,6},{6,7},{9,8},{8,9},{11,10... | collective-permute-start | bytes 12296 | tf_op jit(solution)/shard_map/ppermute | solution.py:105
  65.8 21.6 %collective-permute-start.22 = (bf16[704,2048]{1,0:T(8,128)(2,1)S(1)}, bf16[704,2048]{1,0:T(8,128)(2,1)S(1)}, u32[]{:S(2)}, u32[]{:S(2)}) collective-permute-start(bf16[704,2048]{1,0:T(8,128)(2,1)S(1)} %bitcast.46), channel_id=1, source_target_pairs={{0,2},{2,0},{4,6},{6,4},{8,10},{10,8},{12,14},{14,12},{16,18},{18,... | collective-permute-start | bytes 8650760 | tf_op jit(solution)/shard_map/ppermute | solution.py:101
  65.8 21.6 %collective-permute-start.23 = (bf16[704,2048]{1,0:T(8,128)(2,1)}, bf16[704,2048]{1,0:T(8,128)(2,1)S(1)}, u32[]{:S(2)}, u32[]{:S(2)}) collective-permute-start(bf16[704,2048]{1,0:T(8,128)(2,1)} %bitcast.51), channel_id=1, source_target_pairs={{0,2},{2,0},{4,6},{6,4},{8,10},{10,8},{12,14},{14,12},{16,18},{18,... | collective-permute-start | bytes 8650760 | tf_op jit(solution)/shard_map/ppermute | solution.py:101
  66.3 21.1 %collective-permute-start.24 = (bf16[704,2048]{1,0:T(8,128)(2,1)}, bf16[704,2048]{1,0:T(8,128)(2,1)S(1)}, u32[]{:S(2)}, u32[]{:S(2)}) collective-permute-start(bf16[704,2048]{1,0:T(8,128)(2,1)} %bitcast.56), channel_id=1, source_target_pairs={{0,2},{2,0},{4,6},{6,4},{8,10},{10,8},{12,14},{14,12},{16,18},{18,... | collective-permute-start | bytes 8650760 | tf_op jit(solution)/shard_map/ppermute | solution.py:101
  67.9 14.5 %collective-permute-start.17 = (bf16[128,2048]{1,0:T(8,128)(2,1)S(1)}, bf16[128,2048]{1,0:T(8,128)(2,1)S(1)}, u32[]{:S(2)}, u32[]{:S(2)}) collective-permute-start(bf16[128,2048]{1,0:T(8,128)(2,1)S(1)} %get-tuple-element.73.refs_3_), channel_id=1, source_target_pairs={{8,0},{10,2},{16,8},{18,10},{24,16},{26,18},{28,24},{30,26},{20,28... | collective-permute-start | bytes 1572872 | tf_op jit(solution)/shard_map/ppermute | solution.py:69
  71.3 14.0 %collective-permute-start.16 = (bf16[128,2048]{1,0:T(8,128)(2,1)S(1)}, bf16[128,2048]{1,0:T(8,128)(2,1)S(1)}, u32[]{:S(2)}, u32[]{:S(2)}) collective-permute-start(bf16[128,2048]{1,0:T(8,128)(2,1)S(1)} %get-tuple-element.73.refs_3_), channel_id=1, source_target_pairs={{8,16},{10,18},{16,24},{18,26},{24,28},{26,30},{28,20},{30,22},{20... | collective-permute-start | bytes 1572872 | tf_op jit(solution)/shard_map/ppermute | solution.py:69
  73.0 14.3 %copy-start.2 = (bf16[1,704,2048]{2,1,0:T(8,128)(2,1)S(1)}, bf16[1,704,2048]{2,1,0:T(8,128)(2,1)}, u32[]{:S(2)}) copy-start(bf16[1,704,2048]{2,1,0:T(8,128)(2,1)} %param.24) | copy-start | bytes 8650756
  74.2 13.2 %copy-start.1 = (bf16[1,2048,704]{1,2,0:T(8,128)(2,1)S(1)}, bf16[1,2048,704]{1,2,0:T(8,128)(2,1)}, u32[]{:S(2)}) copy-start(bf16[1,2048,704]{1,2,0:T(8,128)(2,1)} %param.23) | copy-start | bytes 8650756
  85.3 12.0 %collective-permute-start.20 = (bf16[128,2048]{1,0:T(8,128)(2,1)S(1)}, bf16[128,2048]{1,0:T(8,128)(2,1)S(1)}, u32[]{:S(2)}, u32[]{:S(2)}) collective-permute-start(bf16[128,2048]{1,0:T(8,128)(2,1)S(1)} %collective-permute-done.16.refs_2_), channel_id=1, source_target_pairs={{8,16},{10,18},{16,24},{18,26},{24,28},{26,30},{28,20},{30,22},{20... | collective-permute-start | bytes 1572872 | tf_op jit(solution)/shard_map/ppermute | solution.py:69
  85.6 12.0 %collective-permute-start.21 = (bf16[128,2048]{1,0:T(8,128)(2,1)S(1)}, bf16[128,2048]{1,0:T(8,128)(2,1)S(1)}, u32[]{:S(2)}, u32[]{:S(2)}) collective-permute-start(bf16[128,2048]{1,0:T(8,128)(2,1)S(1)} %collective-permute-done.17.refs_3_), channel_id=1, source_target_pairs={{8,0},{10,2},{16,8},{18,10},{24,16},{26,18},{28,24},{30,26},{20,28... | collective-permute-start | bytes 1572872 | tf_op jit(solution)/shard_map/ppermute | solution.py:69
  94.9 13.8 %collective-permute-start.27 = (bf16[256,1024]{1,0:T(8,128)(2,1)S(1)}, bf16[256,1024]{1,0:T(8,128)(2,1)S(1)}, u32[]{:S(2)}, u32[]{:S(2)}) collective-permute-start(bf16[256,1024]{1,0:T(8,128)(2,1)S(1)} %get-tuple-element.89), channel_id=1, source_target_pairs={{1,0},{0,1},{3,2},{2,3},{5,4},{4,5},{7,6},{6,7},{9,8},{8,9},{11,10... | collective-permute-start | bytes 1572872 | tf_op jit(solution)/shard_map/ppermute | solution.py:105
  97.6 11.2 %collective-permute-start.25 = (bf16[128,2048]{1,0:T(8,128)(2,1)S(1)}, bf16[128,2048]{1,0:T(8,128)(2,1)S(1)}, u32[]{:S(2)}, u32[]{:S(2)}) collective-permute-start(bf16[128,2048]{1,0:T(8,128)(2,1)S(1)} %collective-permute-done.20.refs_2_), channel_id=1, source_target_pairs={{8,16},{10,18},{16,24},{18,26},{24,28},{26,30},{28,20},{30,22},{20... | collective-permute-start | bytes 1572872 | tf_op jit(solution)/shard_map/ppermute | solution.py:69
  99.4 10.5 %collective-permute-start.26 = (bf16[128,2048]{1,0:T(8,128)(2,1)S(1)}, bf16[128,2048]{1,0:T(8,128)(2,1)S(1)}, u32[]{:S(2)}, u32[]{:S(2)}) collective-permute-start(bf16[128,2048]{1,0:T(8,128)(2,1)S(1)} %collective-permute-done.21.refs_3_), channel_id=1, source_target_pairs={{8,0},{10,2},{16,8},{18,10},{24,16},{26,18},{28,24},{30,26},{20,28... | collective-permute-start | bytes 1572872 | tf_op jit(solution)/shard_map/ppermute | solution.py:69
  107.2 16.3 %collective-permute-start.29 = (bf16[256,1024]{1,0:T(8,128)(2,1)S(1)}, bf16[256,1024]{1,0:T(8,128)(2,1)S(1)}, u32[]{:S(2)}, u32[]{:S(2)}) collective-permute-start(bf16[256,1024]{1,0:T(8,128)(2,1)S(1)} %get-tuple-element.92), channel_id=1, source_target_pairs={{1,0},{0,1},{3,2},{2,3},{5,4},{4,5},{7,6},{6,7},{9,8},{8,9},{11,10... | collective-permute-start | bytes 1572872 | tf_op jit(solution)/shard_map/ppermute | solution.py:105
  109.9 14.9 %collective-permute-start.28 = (bf16[128,2048]{1,0:T(8,128)(2,1)S(1)}, bf16[128,2048]{1,0:T(8,128)(2,1)S(1)}, u32[]{:S(2)}, u32[]{:S(2)}) collective-permute-start(bf16[128,2048]{1,0:T(8,128)(2,1)S(1)} %collective-permute-done.25.refs_2_), channel_id=1, source_target_pairs={{8,16},{10,18},{16,24},{18,26},{24,28},{26,30},{28,20},{30,22},{20... | collective-permute-start | bytes 1572872 | tf_op jit(solution)/shard_map/ppermute | solution.py:69
  119.4 14.7 %collective-permute-start.31 = (bf16[128,1024]{1,0:T(8,128)(2,1)S(1)}, bf16[128,1024]{1,0:T(8,128)(2,1)S(1)}, u32[]{:S(2)}, u32[]{:S(2)}) collective-permute-start(bf16[128,1024]{1,0:T(8,128)(2,1)S(1)} %get-tuple-element.118), channel_id=1, source_target_pairs={{8,16},{10,18},{16,24},{18,26},{24,28},{26,30},{28,20},{30,22},{20... | collective-permute-start | bytes 786440 | tf_op jit(solution)/shard_map/ppermute | solution.py:69
  120.5 13.7 %collective-permute-start.35 = (bf16[128,1024]{1,0:T(8,128)(2,1)S(1)}, bf16[128,1024]{1,0:T(8,128)(2,1)S(1)}, u32[]{:S(2)}, u32[]{:S(2)}) collective-permute-start(bf16[128,1024]{1,0:T(8,128)(2,1)S(1)} %get-tuple-element.119), channel_id=1, source_target_pairs={{8,0},{10,2},{16,8},{18,10},{24,16},{26,18},{28,24},{30,26},{20,28... | collective-permute-start | bytes 786440 | tf_op jit(solution)/shard_map/ppermute | solution.py:69
  121.5 13.2 %collective-permute-start.32 = (bf16[128,1024]{1,0:T(8,128)(2,1)S(1)}, bf16[128,1024]{1,0:T(8,128)(2,1)S(1)}, u32[]{:S(2)}, u32[]{:S(2)}) collective-permute-start(bf16[128,1024]{1,0:T(8,128)(2,1)S(1)} %get-tuple-element.120), channel_id=1, source_target_pairs={{8,17},{9,16},{10,19},{11,18},{16,25},{17,24},{18,27},{19,26},{24,... | collective-permute-start | bytes 786440 | tf_op jit(solution)/shard_map/ppermute | solution.py:97
  123.5 11.2 %collective-permute-start.36 = (bf16[128,1024]{1,0:T(8,128)(2,1)S(1)}, bf16[128,1024]{1,0:T(8,128)(2,1)S(1)}, u32[]{:S(2)}, u32[]{:S(2)}) collective-permute-start(bf16[128,1024]{1,0:T(8,128)(2,1)S(1)} %get-tuple-element.121), channel_id=1, source_target_pairs={{8,1},{9,0},{10,3},{11,2},{16,9},{17,8},{18,11},{19,10},{24,17},{2... | collective-permute-start | bytes 786440 | tf_op jit(solution)/shard_map/ppermute | solution.py:97
  132.4 9.2 %collective-permute-start.39 = (bf16[128,1024]{1,0:T(8,128)(2,1)S(1)}, bf16[128,1024]{1,0:T(8,128)(2,1)S(1)}, u32[]{:S(2)}, u32[]{:S(2)}) collective-permute-start(bf16[128,1024]{1,0:T(8,128)(2,1)S(1)} %get-tuple-element.117), channel_id=1, source_target_pairs={{1,0},{0,1},{3,2},{2,3},{5,4},{4,5},{7,6},{6,7},{9,8},{8,9},{11,10... | collective-permute-start | bytes 786440 | tf_op jit(solution)/shard_map/ppermute | solution.py:105
  135.0 9.4 %collective-permute-start.33 = (bf16[128,1024]{1,0:T(8,128)(2,1)S(1)}, bf16[128,1024]{1,0:T(8,128)(2,1)S(1)}, u32[]{:S(2)}, u32[]{:S(2)}) collective-permute-start(bf16[128,1024]{1,0:T(8,128)(2,1)S(1)} %get-tuple-element.114), channel_id=1, source_target_pairs={{8,16},{10,18},{16,24},{18,26},{24,28},{26,30},{28,20},{30,22},{20... | collective-permute-start | bytes 786440 | tf_op jit(solution)/shard_map/ppermute | solution.py:69
  136.5 8.6 %collective-permute-start.37 = (bf16[128,1024]{1,0:T(8,128)(2,1)S(1)}, bf16[128,1024]{1,0:T(8,128)(2,1)S(1)}, u32[]{:S(2)}, u32[]{:S(2)}) collective-permute-start(bf16[128,1024]{1,0:T(8,128)(2,1)S(1)} %get-tuple-element.115), channel_id=1, source_target_pairs={{8,0},{10,2},{16,8},{18,10},{24,16},{26,18},{28,24},{30,26},{20,28... | collective-permute-start | bytes 786440 | tf_op jit(solution)/shard_map/ppermute | solution.py:69
  137.4 13.4 %collective-permute-start.30 = (bf16[128,1024]{1,0:T(8,128)(2,1)S(1)}, bf16[128,1024]{1,0:T(8,128)(2,1)S(1)}, u32[]{:S(2)}, u32[]{:S(2)}) collective-permute-start(bf16[128,1024]{1,0:T(8,128)(2,1)S(1)} %get-tuple-element.116), channel_id=1, source_target_pairs={{1,0},{0,1},{3,2},{2,3},{5,4},{4,5},{7,6},{6,7},{9,8},{8,9},{11,10... | collective-permute-start | bytes 786440 | tf_op jit(solution)/shard_map/ppermute | solution.py:105
  141.6 15.5 %copy-start.14 = (bf16[128,1024]{1,0:T(8,128)(2,1)S(1)}, bf16[128,1024]{1,0:T(8,128)(2,1)}, u32[]{:S(2)}) copy-start(bf16[128,1024]{1,0:T(8,128)(2,1)} %copy-done.13) | copy-start | bytes 786436
  141.6 10.4 %collective-permute-start.40 = (bf16[128,1024]{1,0:T(8,128)(2,1)S(1)}, bf16[128,1024]{1,0:T(8,128)(2,1)S(1)}, u32[]{:S(2)}, u32[]{:S(2)}) collective-permute-start(bf16[128,1024]{1,0:T(8,128)(2,1)S(1)} %add_convert_fusion.1), channel_id=1, source_target_pairs={{8,20},{10,22},{16,12},{18,14},{24,4},{26,6},{28,0},{30,2},{20,8},... | collective-permute-start | bytes 786440 | tf_op jit(solution)/shard_map/ppermute | solution.py:69
  145.2 15.9 %copy-start.22 = (f32[1024]{0:T(1024)S(1)}, f32[1024]{0:T(1024)}, u32[]{:S(2)}) copy-start(f32[1024]{0:T(1024)} %param.28) | copy-start | bytes 12292
  145.2 9.5 %collective-permute-start.34 = (bf16[128,1024]{1,0:T(8,128)(2,1)S(1)}, bf16[128,1024]{1,0:T(8,128)(2,1)S(1)}, u32[]{:S(2)}, u32[]{:S(2)}) collective-permute-start(bf16[128,1024]{1,0:T(8,128)(2,1)S(1)} %get-tuple-element.112), channel_id=1, source_target_pairs={{8,16},{10,18},{16,24},{18,26},{24,28},{26,30},{28,20},{30,22},{20... | collective-permute-start | bytes 786440 | tf_op jit(solution)/shard_map/ppermute | solution.py:69
  150.7 6.4 %collective-permute-start.38 = (bf16[128,1024]{1,0:T(8,128)(2,1)S(1)}, bf16[128,1024]{1,0:T(8,128)(2,1)S(1)}, u32[]{:S(2)}, u32[]{:S(2)}) collective-permute-start(bf16[128,1024]{1,0:T(8,128)(2,1)S(1)} %get-tuple-element.113), channel_id=1, source_target_pairs={{8,0},{10,2},{16,8},{18,10},{24,16},{26,18},{28,24},{30,26},{20,28... | collective-permute-start | bytes 786440 | tf_op jit(solution)/shard_map/ppermute | solution.py:69
  157.5 4.5 %copy-start.21 = (bf16[128,1024]{1,0:T(8,128)(2,1)}, bf16[128,1024]{1,0:T(8,128)(2,1)S(1)}, u32[]{:S(2)}) copy-start(bf16[128,1024]{1,0:T(8,128)(2,1)S(1)} %get-tuple-element.105) | copy-start | bytes 786436
  157.5 3.6 %collective-permute-start.41 = (f32[1,128]{1,0:T(1,128)S(1)}, f32[1,128]{1,0:T(1,128)S(1)}, u32[]{:S(2)}, u32[]{:S(2)}) collective-permute-start(f32[1,128]{1,0:T(1,128)S(1)} %bitcast.69), channel_id=1, source_target_pairs={{1,0},{0,1},{3,2},{2,3},{5,4},{4,5},{7,6},{6,7},{9,8},{8,9},{11,10... | collective-permute-start | bytes 1544 | tf_op jit(solution)/shard_map/ppermute | solution.py:105
  (2 other events, 1.4 us)

commit v4 on v3

--- a/solution.py
+++ b/solution.py
@@ -13,7 +13,7 @@
 CORES = 2
 LANES = 128
 VMEM_BYTES = 8 * 2**20
-FFN_VMEM = 28 * 2**20
+FFN_VMEM = 20 * 2**20
 
 
 def matmul(left, right):

time: 163 us -> 163 us (level)
  no operation moved by 1% of the time
where the time goes in v4:
time: 163 us; the launch traced here: 162 us
  waiting for transfers between devices  56.4 us (35%)
  starting transfers between devices  52.8 us (32%)
  Pallas kernels  34.9 us (21%)
  local copies, waits for them, and re-layouts  11.9 us (7%)
  other arithmetic  4.76 us (3%)
    ppermute x21, waiting for transfers between devices, step(): return lax.ppermute(value, 'dp', pairs)  36.2 us
    pallas_call x4, Pallas kernels, ffn(): pl.pallas_call(functools.partial(ffn_kernel, offsets, len(tokens), mp_cou...  30.2 us
    ppermute x21, starting transfers between devices, step(): return lax.ppermute(value, 'dp', pairs)  30.1 us
    ppermute x12, waiting for transfers between devices, from_mp(): lax.ppermute(value, 'mp', [((i + k) % count, i) for i in range(count)])  15.7 us
    ppermute x12, starting transfers between devices, from_mp(): lax.ppermute(value, 'mp', [((i + k) % count, i) for i in range(count)])  13.5 us
    unnamed x48, local copies, waits for them, and re-layouts  10.9 us
    all_to_all x1, starting transfers between devices, local(): shared = lax.all_to_all(after(shared, ahead), 'dp', 0, 0, tiled=True)  4.65 us
  transfers between devices with their start and end apart: 43, of which 26 were waited for; matrix products, arithmetic and copies ran while one was open for 4% of the time, Pallas kernels for 22%

profile of v4, /device:TPU:0, one launch (start us, length us, event | category | flops | bytes accessed | tf_op | source)
XLA Modules:
  0.0 161.9 jit_solution(16043411573141963227)
XLA Ops:
  0.6 3.1 %collective-permute-start.1 = (bf16[1024,128]{1,0:T(8,128)(2,1)}, bf16[1024,128]{1,0:T(8,128)(2,1)S(1)}, u32[]{:S(2)}, u32[]{:S(2)}) collective-permute-start(bf16[1024,128]{1,0:T(8,128)(2,1)} %refs_2_.1), channel_id=1, source_target_pairs={{8,16},{10,18},{16,24},{18,26},{24,28},{26,30},{28,20},{30,22},{20... | collective-permute-start | bytes 786440 | tf_op jit(solution)/shard_map/ppermute | solution.py:69
  3.7 6.4 %collective-permute-done.1.refs_3_ = bf16[1024,128]{1,0:T(8,128)(2,1)S(1)} collective-permute-done((bf16[1024,128]{1,0:T(8,128)(2,1)}, bf16[1024,128]{1,0:T(8,128)(2,1)S(1)}, u32[]{:S(2)}, u32[]{:S(2)}) %collective-permute-start.1) | collective-permute-done | bytes 262176 | tf_op jit(solution)/shard_map/ppermute | solution.py:69
  10.2 1.5 collective-permute-done.2.refs_4_
  11.7 1.6 collective-permute-start.3
  13.7 1.5 collective-permute-start.8
  15.7 0.8 select_reduce_fusion.1
  16.5 0.8 select_reduce_fusion
  17.3 0.9 copy-done.4
  18.3 0.9 copy-done.12
  19.8 1.6 collective-permute-start.5
  22.3 1.0 copy-done.3
  23.8 2.5 %collective-permute-done.5.refs_2_ = bf16[1024,128]{1,0:T(8,128)(2,1)S(1)} collective-permute-done((bf16[1024,128]{1,0:T(8,128)(2,1)S(1)}, bf16[1024,128]{1,0:T(8,128)(2,1)S(1)}, u32[]{:S(2)}, u32[]{:S(2)}) %collective-permute-start.5) | collective-permute-done | bytes 262176 | tf_op jit(solution)/shard_map/ppermute | solution.py:69
  26.2 1.6 collective-permute-done.6.refs_3_
  27.8 1.6 collective-permute-start.12
  31.2 3.0 %collective-permute-done.12.refs_2_ = bf16[1024,128]{1,0:T(8,128)(2,1)S(1)} collective-permute-done((bf16[1024,128]{1,0:T(8,128)(2,1)S(1)}, bf16[1024,128]{1,0:T(8,128)(2,1)S(1)}, u32[]{:S(2)}, u32[]{:S(2)}) %collective-permute-start.12) | collective-permute-done | bytes 262176 | tf_op jit(solution)/shard_map/ppermute | solution.py:69
  34.2 0.7 copy-done.15
  34.9 4.6 %all-to-all-start = ((bf16[16,272,128]{2,1,0:T(8,128)(2,1)}), bf16[16,272,128]{2,1,0:T(8,128)(2,1)}, u32[]{:S(2)}, u32[]{:S(2)}) async-start(bf16[16,272,128]{2,1,0:T(8,128)(2,1)} %copy-done.3), calls=%async_computation | async-start | bytes 2228224 | tf_op jit(solution)/shard_map/all_to_all | solution.py:427
  39.8 1.5 collective-permute-start.9
  41.4 1.5 collective-permute-start.11
  42.9 0.9 copy-done.16
  45.4 0.9 collective-permute-start.15
  47.0 1.5 collective-permute-done.9.refs_1_
  48.5 5.3 %collective-permute-done.13.refs_5_ = bf16[1,128,128]{2,1,0:T(8,128)(2,1)S(1)} collective-permute-done((bf16[1,128,128]{2,1,0:T(8,128)(2,1)S(1)}, bf16[1,128,128]{2,1,0:T(8,128)(2,1)S(1)}, u32[]{:S(2)}, u32[]{:S(2)}) %collective-permute-start.13) | collective-permute-done | bytes 32800 | tf_op jit(solution)/shard_map/ppermute | solution.py:105
  54.2 0.9 copy-done.7
  55.1 0.9 copy-done.17
  56.1 0.9 copy-done.19
  57.0 2.7 %shard_map.163 = (bf16[128,2048]{1,0:T(8,128)(2,1)S(1)}, bf16[128,1024]{1,0:T(8,128)(2,1)S(1)}) custom-call(s32[10]{0:T(128)S(1)} %dynamic-slice_bitcast_fusion.info_ref, bf16[7,128,128]{2,1,0:T(8,128)(2,1)S(1)} %copy-done.7, bf16[7,128,128]{2,1,0:T(8,128)(2,1)} %collective-permute-done.9.refs_1_, bf16[7,128,128]{2,1,0:T(8,128)(2,1)} %collective-permute-done.10.refs_2_, ...), custom_call_target="tpu_custom_call" | custom-call | flops 1 | bytes 1 | tf_op jit(solution)/shard_map/pallas_call | solution.py:238
  60.4 3.2 %all-to-all-done = bf16[16,272,128]{2,1,0:T(8,128)(2,1)} async-done(((bf16[16,272,128]{2,1,0:T(8,128)(2,1)}), bf16[16,272,128]{2,1,0:T(8,128)(2,1)}, u32[]{:S(2)}, u32[]{:S(2)}) %all-to-all-start) | async-done | bytes 1114144 | tf_op jit(solution)/shard_map/all_to_all | solution.py:427
  63.6 0.7 collective-permute-start.19
  64.3 1.5 collective-permute-start.18
  66.3 1.6 collective-permute-done.18
  67.9 2.1 %collective-permute-start.17 = (bf16[128,2048]{1,0:T(8,128)(2,1)S(1)}, bf16[128,2048]{1,0:T(8,128)(2,1)S(1)}, u32[]{:S(2)}, u32[]{:S(2)}) collective-permute-start(bf16[128,2048]{1,0:T(8,128)(2,1)S(1)} %get-tuple-element.73.refs_3_), channel_id=1, source_target_pairs={{8,0},{10,2},{16,8},{18,10},{24,16},{26,18},{28,24},{30,26},{20,28... | collective-permute-start | bytes 1572872 | tf_op jit(solution)/shard_map/ppermute | solution.py:69
  70.0 1.3 slice_bitcast_fusion.1
  71.3 1.5 collective-permute-start.16
  73.2 1.0 convert_reduce_fusion
  74.3 8.1 %collective-permute-done.17.refs_3_ = bf16[128,2048]{1,0:T(8,128)(2,1)S(1)} collective-permute-done((bf16[128,2048]{1,0:T(8,128)(2,1)S(1)}, bf16[128,2048]{1,0:T(8,128)(2,1)S(1)}, u32[]{:S(2)}, u32[]{:S(2)}) %collective-permute-start.17) | collective-permute-done | bytes 524320 | tf_op jit(solution)/shard_map/ppermute | solution.py:69
  82.4 2.9 %collective-permute-done.16.refs_2_ = bf16[128,2048]{1,0:T(8,128)(2,1)S(1)} collective-permute-done((bf16[128,2048]{1,0:T(8,128)(2,1)S(1)}, bf16[128,2048]{1,0:T(8,128)(2,1)S(1)}, u32[]{:S(2)}, u32[]{:S(2)}) %collective-permute-start.16) | collective-permute-done | bytes 524320 | tf_op jit(solution)/shard_map/ppermute | solution.py:69
  85.6 1.7 %collective-permute-start.21 = (bf16[128,2048]{1,0:T(8,128)(2,1)S(1)}, bf16[128,2048]{1,0:T(8,128)(2,1)S(1)}, u32[]{:S(2)}, u32[]{:S(2)}) collective-permute-start(bf16[128,2048]{1,0:T(8,128)(2,1)S(1)} %collective-permute-done.17.refs_3_), channel_id=1, source_target_pairs={{8,0},{10,2},{16,8},{18,10},{24,16},{26,18},{28,24},{30,26},{20,28... | collective-permute-start | bytes 1572872 | tf_op jit(solution)/shard_map/ppermute | solution.py:69
  87.4 7.5 %shard_map.164 = (f32[256,1024]{1,0:T(8,128)S(1)}, bf16[256,1024]{1,0:T(8,128)(2,1)S(1)}) custom-call(s32[10]{0:T(128)S(1)} %dynamic-slice_bitcast_fusion.info_ref, f32[16,128]{1,0:T(8,128)S(1)} %get-tuple-element.79.refs_0_, f32[16,128]{1,0:T(8,128)S(1)} %get-tuple-element.80.refs_1_, bf16[128,2048]{1,0:T(8,128)(2,1)S(1)} %collective-permute-done.16.refs_2_, ...), custom_call_target="tpu_custom_call" | custom-call | flops 1 | bytes 1 | tf_op jit(solution)/shard_map/pallas_call | solution.py:314
  94.9 1.5 collective-permute-start.27
  96.5 0.8 collective-permute-done.20.refs_2_
  97.6 1.8 %collective-permute-start.25 = (bf16[128,2048]{1,0:T(8,128)(2,1)S(1)}, bf16[128,2048]{1,0:T(8,128)(2,1)S(1)}, u32[]{:S(2)}, u32[]{:S(2)}) collective-permute-start(bf16[128,2048]{1,0:T(8,128)(2,1)S(1)} %collective-permute-done.20.refs_2_), channel_id=1, source_target_pairs={{8,16},{10,18},{16,24},{18,26},{24,28},{26,30},{28,20},{30,22},{20... | collective-permute-start | bytes 1572872 | tf_op jit(solution)/shard_map/ppermute | solution.py:69
  99.6 7.6 %shard_map.165 = (f32[256,1024]{1,0:T(8,128)S(1)}, bf16[256,1024]{1,0:T(8,128)(2,1)S(1)}) custom-call(s32[10]{0:T(128)S(1)} %dynamic-slice_bitcast_fusion.info_ref, f32[16,128]{1,0:T(8,128)S(1)} %get-tuple-element.79.refs_0_, f32[16,128]{1,0:T(8,128)S(1)} %get-tuple-element.80.refs_1_, bf16[128,2048]{1,0:T(8,128)(2,1)S(1)} %collective-permute-done.20.refs_2_, ...), custom_call_target="tpu_custom_call" | custom-call | flops 1 | bytes 1 | tf_op jit(solution)/shard_map/pallas_call | solution.py:314
  107.2 1.6 collective-permute-start.29
  108.8 1.2 collective-permute-done.26.refs_3_
  109.9 1.7 %collective-permute-start.28 = (bf16[128,2048]{1,0:T(8,128)(2,1)S(1)}, bf16[128,2048]{1,0:T(8,128)(2,1)S(1)}, u32[]{:S(2)}, u32[]{:S(2)}) collective-permute-start(bf16[128,2048]{1,0:T(8,128)(2,1)S(1)} %collective-permute-done.25.refs_2_), channel_id=1, source_target_pairs={{8,16},{10,18},{16,24},{18,26},{24,28},{26,30},{28,20},{30,22},{20... | collective-permute-start | bytes 1572872 | tf_op jit(solution)/shard_map/ppermute | solution.py:69
  111.7 7.6 %shard_map.166 = (f32[256,1024]{1,0:T(8,128)S(1)}, bf16[256,1024]{1,0:T(8,128)(2,1)S(1)}) custom-call(s32[10]{0:T(128)S(1)} %dynamic-slice_bitcast_fusion.info_ref, f32[16,128]{1,0:T(8,128)S(1)} %get-tuple-element.79.refs_0_, f32[16,128]{1,0:T(8,128)S(1)} %get-tuple-element.80.refs_1_, bf16[128,2048]{1,0:T(8,128)(2,1)S(1)} %collective-permute-done.25.refs_2_, ...), custom_call_target="tpu_custom_call" | custom-call | flops 1 | bytes 1 | tf_op jit(solution)/shard_map/pallas_call | solution.py:314
  119.4 1.1 collective-permute-start.31
  120.5 1.0 collective-permute-start.35
  121.5 2.0 %collective-permute-start.32 = (bf16[128,1024]{1,0:T(8,128)(2,1)S(1)}, bf16[128,1024]{1,0:T(8,128)(2,1)S(1)}, u32[]{:S(2)}, u32[]{:S(2)}) collective-permute-start(bf16[128,1024]{1,0:T(8,128)(2,1)S(1)} %get-tuple-element.120), channel_id=1, source_target_pairs={{8,17},{9,16},{10,19},{11,18},{16,25},{17,24},{18,27},{19,26},{24,... | collective-permute-start | bytes 786440 | tf_op jit(solution)/shard_map/ppermute | solution.py:97
  123.5 1.0 collective-permute-start.36
  124.8 7.5 %shard_map.167 = (f32[256,1024]{1,0:T(8,128)S(1)}, bf16[256,1024]{1,0:T(8,128)(2,1)S(1)}) custom-call(s32[10]{0:T(128)S(1)} %dynamic-slice_bitcast_fusion.info_ref, f32[16,128]{1,0:T(8,128)S(1)} %get-tuple-element.79.refs_0_, f32[16,128]{1,0:T(8,128)S(1)} %get-tuple-element.80.refs_1_, bf16[128,2048]{1,0:T(8,128)(2,1)S(1)} %collective-permute-done.28.refs_2_, ...), custom_call_target="tpu_custom_call" | custom-call | flops 1 | bytes 1 | tf_op jit(solution)/shard_map/pallas_call | solution.py:314
  132.4 1.5 collective-permute-start.39
  135.0 1.5 collective-permute-start.33
  136.5 0.7 collective-permute-start.37
  137.4 0.8 collective-permute-start.30
  138.1 3.4 %collective-permute-done.39 = bf16[128,1024]{1,0:T(8,128)(2,1)S(1)} collective-permute-done((bf16[128,1024]{1,0:T(8,128)(2,1)S(1)}, bf16[128,1024]{1,0:T(8,128)(2,1)S(1)}, u32[]{:S(2)}, u32[]{:S(2)}) %collective-permute-start.39) | collective-permute-done | bytes 262176 | tf_op jit(solution)/shard_map/ppermute | solution.py:105
  141.6 2.1 %collective-permute-start.40 = (bf16[128,1024]{1,0:T(8,128)(2,1)S(1)}, bf16[128,1024]{1,0:T(8,128)(2,1)S(1)}, u32[]{:S(2)}, u32[]{:S(2)}) collective-permute-start(bf16[128,1024]{1,0:T(8,128)(2,1)S(1)} %add_convert_fusion.1), channel_id=1, source_target_pairs={{8,20},{10,22},{16,12},{18,14},{24,4},{26,6},{28,0},{30,2},{20,8},... | collective-permute-start | bytes 786440 | tf_op jit(solution)/shard_map/ppermute | solution.py:69
  145.2 5.6 %collective-permute-start.34 = (bf16[128,1024]{1,0:T(8,128)(2,1)S(1)}, bf16[128,1024]{1,0:T(8,128)(2,1)S(1)}, u32[]{:S(2)}, u32[]{:S(2)}) collective-permute-start(bf16[128,1024]{1,0:T(8,128)(2,1)S(1)} %get-tuple-element.112), channel_id=1, source_target_pairs={{8,16},{10,18},{16,24},{18,26},{24,28},{26,30},{28,20},{30,22},{20... | collective-permute-start | bytes 786440 | tf_op jit(solution)/shard_map/ppermute | solution.py:69
  150.8 1.3 collective-permute-done.40
  152.0 2.6 %collective-permute-done.34 = bf16[128,1024]{1,0:T(8,128)(2,1)S(1)} collective-permute-done((bf16[128,1024]{1,0:T(8,128)(2,1)S(1)}, bf16[128,1024]{1,0:T(8,128)(2,1)S(1)}, u32[]{:S(2)}, u32[]{:S(2)}) %collective-permute-start.34) | collective-permute-done | bytes 262176 | tf_op jit(solution)/shard_map/ppermute | solution.py:69
  154.6 2.5 %collective-permute-done.38 = bf16[128,1024]{1,0:T(8,128)(2,1)S(1)} collective-permute-done((bf16[128,1024]{1,0:T(8,128)(2,1)S(1)}, bf16[128,1024]{1,0:T(8,128)(2,1)S(1)}, u32[]{:S(2)}, u32[]{:S(2)}) %collective-permute-start.38) | collective-permute-done | bytes 262176 | tf_op jit(solution)/shard_map/ppermute | solution.py:69
  157.5 3.5 %collective-permute-done.41 = f32[1,128]{1,0:T(1,128)S(1)} collective-permute-done((f32[1,128]{1,0:T(1,128)S(1)}, f32[1,128]{1,0:T(1,128)S(1)}, u32[]{:S(2)}, u32[]{:S(2)}) %collective-permute-start.41) | collective-permute-done | bytes 544 | tf_op jit(solution)/shard_map/ppermute | solution.py:105
  161.1 0.8 fusion.2
  (105 shorter events, 13.7 us)
Async XLA Ops:
  0.6 9.5 %collective-permute-start.1 = (bf16[1024,128]{1,0:T(8,128)(2,1)}, bf16[1024,128]{1,0:T(8,128)(2,1)S(1)}, u32[]{:S(2)}, u32[]{:S(2)}) collective-permute-start(bf16[1024,128]{1,0:T(8,128)(2,1)} %refs_2_.1), channel_id=1, source_target_pairs={{8,16},{10,18},{16,24},{18,26},{24,28},{26,30},{28,20},{30,22},{20... | collective-permute-start | bytes 786440 | tf_op jit(solution)/shard_map/ppermute | solution.py:69
  3.7 8.0 %collective-permute-start.2 = (bf16[1024,128]{1,0:T(8,128)(2,1)}, bf16[1024,128]{1,0:T(8,128)(2,1)S(1)}, u32[]{:S(2)}, u32[]{:S(2)}) collective-permute-start(bf16[1024,128]{1,0:T(8,128)(2,1)} %refs_2_.1), channel_id=1, source_target_pairs={{8,0},{10,2},{16,8},{18,10},{24,16},{26,18},{28,24},{30,26},{20,28... | collective-permute-start | bytes 786440 | tf_op jit(solution)/shard_map/ppermute | solution.py:69
  3.7 13.6 %collective-permute-start = (bf16[128,1024]{1,0:T(8,128)(2,1)}, bf16[128,1024]{1,0:T(8,128)(2,1)S(1)}, u32[]{:S(2)}, u32[]{:S(2)}) collective-permute-start(bf16[128,1024]{1,0:T(8,128)(2,1)} %refs_0_.7), channel_id=1, source_target_pairs={{0,2},{2,0},{4,6},{6,4},{8,10},{10,8},{12,14},{14,12},{16,18},{18,... | collective-permute-start | bytes 786440 | tf_op jit(solution)/shard_map/ppermute | solution.py:101
  11.7 8.1 %collective-permute-start.3 = (bf16[1024,128]{1,0:T(8,128)(2,1)S(1)}, bf16[1024,128]{1,0:T(8,128)(2,1)S(1)}, u32[]{:S(2)}, u32[]{:S(2)}) collective-permute-start(bf16[1024,128]{1,0:T(8,128)(2,1)S(1)} %collective-permute-done.1.refs_3_), channel_id=1, source_target_pairs={{8,16},{10,18},{16,24},{18,26},{24,28},{26,30},{28,20},{30,22},{20... | collective-permute-start | bytes 786440 | tf_op jit(solution)/shard_map/ppermute | solution.py:69
  13.3 6.6 %collective-permute-start.4 = (bf16[1024,128]{1,0:T(8,128)(2,1)S(1)}, bf16[1024,128]{1,0:T(8,128)(2,1)S(1)}, u32[]{:S(2)}, u32[]{:S(2)}) collective-permute-start(bf16[1024,128]{1,0:T(8,128)(2,1)S(1)} %collective-permute-done.2.refs_4_), channel_id=1, source_target_pairs={{8,0},{10,2},{16,8},{18,10},{24,16},{26,18},{28,24},{30,26},{20,28... | collective-permute-start | bytes 786440 | tf_op jit(solution)/shard_map/ppermute | solution.py:69
  13.7 10.0 %collective-permute-start.8 = (f32[1,1024]{1,0:T(1,128)}, f32[1,1024]{1,0:T(1,128)S(1)}, u32[]{:S(2)}, u32[]{:S(2)}) collective-permute-start(f32[1,1024]{1,0:T(1,128)} %bitcast.61), channel_id=1, source_target_pairs={{1,0},{0,1},{3,2},{2,3},{5,4},{4,5},{7,6},{6,7},{9,8},{8,9},{11,10... | collective-permute-start | bytes 12296 | tf_op jit(solution)/shard_map/ppermute | solution.py:105
  15.2 8.5 %collective-permute-start.7 = (bf16[128,1024]{1,0:T(8,128)(2,1)}, bf16[128,1024]{1,0:T(8,128)(2,1)S(1)}, u32[]{:S(2)}, u32[]{:S(2)}) collective-permute-start(bf16[128,1024]{1,0:T(8,128)(2,1)} %refs_8_.1), channel_id=1, source_target_pairs={{1,0},{0,1},{3,2},{2,3},{5,4},{4,5},{7,6},{6,7},{9,8},{8,9},{11,10... | collective-permute-start | bytes 786440 | tf_op jit(solution)/shard_map/ppermute | solution.py:105
  17.3 1.0 copy-start.4
  18.2 0.9 copy-start.12
  19.2 2.7 %copy-start.9 = (bf16[128,1408]{1,0:T(8,128)(2,1)S(1)}, bf16[128,1408]{1,0:T(8,128)(2,1)}, u32[]{:S(2)}) copy-start(bf16[128,1408]{1,0:T(8,128)(2,1)} %gate_ref.1) | copy-start | bytes 1081348
  19.2 2.7 %copy-start.10 = (bf16[128,1408]{1,0:T(8,128)(2,1)S(1)}, bf16[128,1408]{1,0:T(8,128)(2,1)}, u32[]{:S(2)}) copy-start(bf16[128,1408]{1,0:T(8,128)(2,1)} %up_ref.1) | copy-start | bytes 1081348
  19.2 2.7 %copy-start.11 = (bf16[1408,128]{1,0:T(8,128)(2,1)S(1)}, bf16[1408,128]{1,0:T(8,128)(2,1)}, u32[]{:S(2)}) copy-start(bf16[1408,128]{1,0:T(8,128)(2,1)} %down_ref.1) | copy-start | bytes 1081348
  19.8 3.5 %copy-start.5 = (bf16[128,1024]{1,0:T(8,128)(2,1)S(1)}, bf16[128,1024]{1,0:T(8,128)(2,1)}, u32[]{:S(2)}) copy-start(bf16[128,1024]{1,0:T(8,128)(2,1)} %refs_0_.7) | copy-start | bytes 786436
  19.8 6.4 %collective-permute-start.5 = (bf16[1024,128]{1,0:T(8,128)(2,1)S(1)}, bf16[1024,128]{1,0:T(8,128)(2,1)S(1)}, u32[]{:S(2)}, u32[]{:S(2)}) collective-permute-start(bf16[1024,128]{1,0:T(8,128)(2,1)S(1)} %collective-permute-done.3.refs_2_), channel_id=1, source_target_pairs={{8,16},{10,18},{16,24},{18,26},{24,28},{26,30},{28,20},{30,22},{20... | collective-permute-start | bytes 786440 | tf_op jit(solution)/shard_map/ppermute | solution.py:69
  21.4 6.4 %collective-permute-start.6 = (bf16[1024,128]{1,0:T(8,128)(2,1)S(1)}, bf16[1024,128]{1,0:T(8,128)(2,1)S(1)}, u32[]{:S(2)}, u32[]{:S(2)}) collective-permute-start(bf16[1024,128]{1,0:T(8,128)(2,1)S(1)} %collective-permute-done.4.refs_3_), channel_id=1, source_target_pairs={{8,0},{10,2},{16,8},{18,10},{24,16},{26,18},{28,24},{30,26},{20,28... | collective-permute-start | bytes 786440 | tf_op jit(solution)/shard_map/ppermute | solution.py:69
  22.3 1.0 copy-start.3
  23.8 11.1 %copy-start.18 = (bf16[128,1024]{1,0:T(8,128)(2,1)}, bf16[128,1024]{1,0:T(8,128)(2,1)S(1)}, u32[]{:S(2)}) copy-start(bf16[128,1024]{1,0:T(8,128)(2,1)S(1)} %collective-permute-done.7.refs_9_) | copy-start | bytes 786436
  27.8 6.4 %collective-permute-start.12 = (bf16[1024,128]{1,0:T(8,128)(2,1)S(1)}, bf16[1024,128]{1,0:T(8,128)(2,1)S(1)}, u32[]{:S(2)}, u32[]{:S(2)}) collective-permute-start(bf16[1024,128]{1,0:T(8,128)(2,1)S(1)} %collective-permute-done.5.refs_2_), channel_id=1, source_target_pairs={{8,16},{10,18},{16,24},{18,26},{24,28},{26,30},{28,20},{30,22},{20... | collective-permute-start | bytes 786440 | tf_op jit(solution)/shard_map/ppermute | solution.py:69
  29.4 24.8 %copy-start.20 = (f32[1024]{0:T(1024)S(1)}, f32[1024]{0:T(1024)}, u32[]{:S(2)}) copy-start(f32[1024]{0:T(1024)} %param.18) | copy-start | bytes 12292
  34.2 0.7 copy-start.15
  34.9 30.9 %copy-start = (bf16[1,2048,704]{1,2,0:T(8,128)(2,1)S(1)}, bf16[1,2048,704]{1,2,0:T(8,128)(2,1)}, u32[]{:S(2)}) copy-start(bf16[1,2048,704]{1,2,0:T(8,128)(2,1)} %param.22) | copy-start | bytes 8650756
  34.9 28.7 %all-to-all-start = ((bf16[16,272,128]{2,1,0:T(8,128)(2,1)}), bf16[16,272,128]{2,1,0:T(8,128)(2,1)}, u32[]{:S(2)}, u32[]{:S(2)}) async-start(bf16[16,272,128]{2,1,0:T(8,128)(2,1)} %copy-done.3), calls=%async_computation | async-start | bytes 2228224 | tf_op jit(solution)/shard_map/all_to_all | solution.py:427
  39.5 1.9 %collective-permute-start.10 = (bf16[7,128,128]{2,1,0:T(8,128)(2,1)}, bf16[7,128,128]{2,1,0:T(8,128)(2,1)}, u32[]{:S(2)}, u32[]{:S(2)}) collective-permute-start(bf16[7,128,128]{2,1,0:T(8,128)(2,1)} %copy-done.8), channel_id=1, source_target_pairs={{0,2},{2,0},{4,6},{6,4},{8,10},{10,8},{12,14},{14,12},{16,18},{18,... | collective-permute-start | bytes 688136 | tf_op jit(solution)/shard_map/ppermute | solution.py:101
  39.8 8.7 %collective-permute-start.9 = (bf16[7,128,128]{2,1,0:T(8,128)(2,1)}, bf16[7,128,128]{2,1,0:T(8,128)(2,1)}, u32[]{:S(2)}, u32[]{:S(2)}) collective-permute-start(bf16[7,128,128]{2,1,0:T(8,128)(2,1)} %copy-done.6), channel_id=1, source_target_pairs={{1,0},{0,1},{3,2},{2,3},{5,4},{4,5},{7,6},{6,7},{9,8},{8,9},{11,10... | collective-permute-start | bytes 688136 | tf_op jit(solution)/shard_map/ppermute | solution.py:105
  41.4 12.7 %collective-permute-start.11 = (bf16[7,128,128]{2,1,0:T(8,128)(2,1)}, bf16[7,128,128]{2,1,0:T(8,128)(2,1)}, u32[]{:S(2)}, u32[]{:S(2)}) collective-permute-start(bf16[7,128,128]{2,1,0:T(8,128)(2,1)} %collective-permute-done.10.refs_2_), channel_id=1, source_target_pairs={{1,0},{0,1},{3,2},{2,3},{5,4},{4,5},{7,6},{6,7},{9,8},{8,9},{11,10... | collective-permute-start | bytes 688136 | tf_op jit(solution)/shard_map/ppermute | solution.py:105
  42.9 0.9 copy-start.16
  44.2 1.3 collective-permute-start.14
  44.3 9.6 %collective-permute-start.13 = (bf16[1,128,128]{2,1,0:T(8,128)(2,1)S(1)}, bf16[1,128,128]{2,1,0:T(8,128)(2,1)S(1)}, u32[]{:S(2)}, u32[]{:S(2)}) collective-permute-start(bf16[1,128,128]{2,1,0:T(8,128)(2,1)S(1)} %get-tuple-element.70.refs_4_), channel_id=1, source_target_pairs={{1,0},{0,1},{3,2},{2,3},{5,4},{4,5},{7,6},{6,7},{9,8},{8,9},{11,10... | collective-permute-start | bytes 98312 | tf_op jit(solution)/shard_map/ppermute | solution.py:105
  45.4 8.7 %collective-permute-start.15 = (bf16[1,128,128]{2,1,0:T(8,128)(2,1)S(1)}, bf16[1,128,128]{2,1,0:T(8,128)(2,1)S(1)}, u32[]{:S(2)}, u32[]{:S(2)}) collective-permute-start(bf16[1,128,128]{2,1,0:T(8,128)(2,1)S(1)} %collective-permute-done.14.refs_6_), channel_id=1, source_target_pairs={{1,0},{0,1},{3,2},{2,3},{5,4},{4,5},{7,6},{6,7},{9,8},{8,9},{11,10... | collective-permute-start | bytes 98312 | tf_op jit(solution)/shard_map/ppermute | solution.py:105
  54.2 0.9 copy-start.7
  55.1 0.9 copy-start.17
  56.1 0.9 copy-start.19
  59.7 0.7 copy-start.13
  63.6 7.8 %collective-permute-start.19 = (bf16[272,16,128]{2,0,1:T(8,128)(2,1)}, bf16[272,16,128]{2,0,1:T(8,128)(2,1)S(1)}, u32[]{:S(2)}, u32[]{:S(2)}) collective-permute-start(bf16[272,16,128]{2,0,1:T(8,128)(2,1)} %bitcast.5), channel_id=1, source_target_pairs={{0,2},{2,0},{4,6},{6,4},{8,10},{10,8},{12,14},{14,12},{16,18},{18,... | collective-permute-start | bytes 3342344 | tf_op jit(solution)/shard_map/ppermute | solution.py:101
  64.3 3.6 %collective-permute-start.18 = (bf16[16,128]{1,0:T(8,128)(2,1)S(1)}, bf16[16,128]{1,0:T(8,128)(2,1)S(1)}, u32[]{:S(2)}, u32[]{:S(2)}) collective-permute-start(bf16[16,128]{1,0:T(8,128)(2,1)S(1)} %slice.65), channel_id=1, source_target_pairs={{1,0},{0,1},{3,2},{2,3},{5,4},{4,5},{7,6},{6,7},{9,8},{8,9},{11,10... | collective-permute-start | bytes 12296 | tf_op jit(solution)/shard_map/ppermute | solution.py:105
  65.8 21.6 %collective-permute-start.22 = (bf16[704,2048]{1,0:T(8,128)(2,1)S(1)}, bf16[704,2048]{1,0:T(8,128)(2,1)S(1)}, u32[]{:S(2)}, u32[]{:S(2)}) collective-permute-start(bf16[704,2048]{1,0:T(8,128)(2,1)S(1)} %bitcast.46), channel_id=1, source_target_pairs={{0,2},{2,0},{4,6},{6,4},{8,10},{10,8},{12,14},{14,12},{16,18},{18,... | collective-permute-start | bytes 8650760 | tf_op jit(solution)/shard_map/ppermute | solution.py:101
  65.8 21.6 %collective-permute-start.23 = (bf16[704,2048]{1,0:T(8,128)(2,1)}, bf16[704,2048]{1,0:T(8,128)(2,1)S(1)}, u32[]{:S(2)}, u32[]{:S(2)}) collective-permute-start(bf16[704,2048]{1,0:T(8,128)(2,1)} %bitcast.51), channel_id=1, source_target_pairs={{0,2},{2,0},{4,6},{6,4},{8,10},{10,8},{12,14},{14,12},{16,18},{18,... | collective-permute-start | bytes 8650760 | tf_op jit(solution)/shard_map/ppermute | solution.py:101
  66.3 21.1 %collective-permute-start.24 = (bf16[704,2048]{1,0:T(8,128)(2,1)}, bf16[704,2048]{1,0:T(8,128)(2,1)S(1)}, u32[]{:S(2)}, u32[]{:S(2)}) collective-permute-start(bf16[704,2048]{1,0:T(8,128)(2,1)} %bitcast.56), channel_id=1, source_target_pairs={{0,2},{2,0},{4,6},{6,4},{8,10},{10,8},{12,14},{14,12},{16,18},{18,... | collective-permute-start | bytes 8650760 | tf_op jit(solution)/shard_map/ppermute | solution.py:101
  67.9 14.5 %collective-permute-start.17 = (bf16[128,2048]{1,0:T(8,128)(2,1)S(1)}, bf16[128,2048]{1,0:T(8,128)(2,1)S(1)}, u32[]{:S(2)}, u32[]{:S(2)}) collective-permute-start(bf16[128,2048]{1,0:T(8,128)(2,1)S(1)} %get-tuple-element.73.refs_3_), channel_id=1, source_target_pairs={{8,0},{10,2},{16,8},{18,10},{24,16},{26,18},{28,24},{30,26},{20,28... | collective-permute-start | bytes 1572872 | tf_op jit(solution)/shard_map/ppermute | solution.py:69
  71.3 14.0 %collective-permute-start.16 = (bf16[128,2048]{1,0:T(8,128)(2,1)S(1)}, bf16[128,2048]{1,0:T(8,128)(2,1)S(1)}, u32[]{:S(2)}, u32[]{:S(2)}) collective-permute-start(bf16[128,2048]{1,0:T(8,128)(2,1)S(1)} %get-tuple-element.73.refs_3_), channel_id=1, source_target_pairs={{8,16},{10,18},{16,24},{18,26},{24,28},{26,30},{28,20},{30,22},{20... | collective-permute-start | bytes 1572872 | tf_op jit(solution)/shard_map/ppermute | solution.py:69
  73.0 14.3 %copy-start.2 = (bf16[1,704,2048]{2,1,0:T(8,128)(2,1)S(1)}, bf16[1,704,2048]{2,1,0:T(8,128)(2,1)}, u32[]{:S(2)}) copy-start(bf16[1,704,2048]{2,1,0:T(8,128)(2,1)} %param.24) | copy-start | bytes 8650756
  74.2 13.2 %copy-start.1 = (bf16[1,2048,704]{1,2,0:T(8,128)(2,1)S(1)}, bf16[1,2048,704]{1,2,0:T(8,128)(2,1)}, u32[]{:S(2)}) copy-start(bf16[1,2048,704]{1,2,0:T(8,128)(2,1)} %param.23) | copy-start | bytes 8650756
  85.3 12.0 %collective-permute-start.20 = (bf16[128,2048]{1,0:T(8,128)(2,1)S(1)}, bf16[128,2048]{1,0:T(8,128)(2,1)S(1)}, u32[]{:S(2)}, u32[]{:S(2)}) collective-permute-start(bf16[128,2048]{1,0:T(8,128)(2,1)S(1)} %collective-permute-done.16.refs_2_), channel_id=1, source_target_pairs={{8,16},{10,18},{16,24},{18,26},{24,28},{26,30},{28,20},{30,22},{20... | collective-permute-start | bytes 1572872 | tf_op jit(solution)/shard_map/ppermute | solution.py:69
  85.6 12.0 %collective-permute-start.21 = (bf16[128,2048]{1,0:T(8,128)(2,1)S(1)}, bf16[128,2048]{1,0:T(8,128)(2,1)S(1)}, u32[]{:S(2)}, u32[]{:S(2)}) collective-permute-start(bf16[128,2048]{1,0:T(8,128)(2,1)S(1)} %collective-permute-done.17.refs_3_), channel_id=1, source_target_pairs={{8,0},{10,2},{16,8},{18,10},{24,16},{26,18},{28,24},{30,26},{20,28... | collective-permute-start | bytes 1572872 | tf_op jit(solution)/shard_map/ppermute | solution.py:69
  94.9 13.8 %collective-permute-start.27 = (bf16[256,1024]{1,0:T(8,128)(2,1)S(1)}, bf16[256,1024]{1,0:T(8,128)(2,1)S(1)}, u32[]{:S(2)}, u32[]{:S(2)}) collective-permute-start(bf16[256,1024]{1,0:T(8,128)(2,1)S(1)} %get-tuple-element.89), channel_id=1, source_target_pairs={{1,0},{0,1},{3,2},{2,3},{5,4},{4,5},{7,6},{6,7},{9,8},{8,9},{11,10... | collective-permute-start | bytes 1572872 | tf_op jit(solution)/shard_map/ppermute | solution.py:105
  97.6 11.2 %collective-permute-start.25 = (bf16[128,2048]{1,0:T(8,128)(2,1)S(1)}, bf16[128,2048]{1,0:T(8,128)(2,1)S(1)}, u32[]{:S(2)}, u32[]{:S(2)}) collective-permute-start(bf16[128,2048]{1,0:T(8,128)(2,1)S(1)} %collective-permute-done.20.refs_2_), channel_id=1, source_target_pairs={{8,16},{10,18},{16,24},{18,26},{24,28},{26,30},{28,20},{30,22},{20... | collective-permute-start | bytes 1572872 | tf_op jit(solution)/shard_map/ppermute | solution.py:69
  99.4 10.5 %collective-permute-start.26 = (bf16[128,2048]{1,0:T(8,128)(2,1)S(1)}, bf16[128,2048]{1,0:T(8,128)(2,1)S(1)}, u32[]{:S(2)}, u32[]{:S(2)}) collective-permute-start(bf16[128,2048]{1,0:T(8,128)(2,1)S(1)} %collective-permute-done.21.refs_3_), channel_id=1, source_target_pairs={{8,0},{10,2},{16,8},{18,10},{24,16},{26,18},{28,24},{30,26},{20,28... | collective-permute-start | bytes 1572872 | tf_op jit(solution)/shard_map/ppermute | solution.py:69
  107.2 16.3 %collective-permute-start.29 = (bf16[256,1024]{1,0:T(8,128)(2,1)S(1)}, bf16[256,1024]{1,0:T(8,128)(2,1)S(1)}, u32[]{:S(2)}, u32[]{:S(2)}) collective-permute-start(bf16[256,1024]{1,0:T(8,128)(2,1)S(1)} %get-tuple-element.92), channel_id=1, source_target_pairs={{1,0},{0,1},{3,2},{2,3},{5,4},{4,5},{7,6},{6,7},{9,8},{8,9},{11,10... | collective-permute-start | bytes 1572872 | tf_op jit(solution)/shard_map/ppermute | solution.py:105
  109.9 14.9 %collective-permute-start.28 = (bf16[128,2048]{1,0:T(8,128)(2,1)S(1)}, bf16[128,2048]{1,0:T(8,128)(2,1)S(1)}, u32[]{:S(2)}, u32[]{:S(2)}) collective-permute-start(bf16[128,2048]{1,0:T(8,128)(2,1)S(1)} %collective-permute-done.25.refs_2_), channel_id=1, source_target_pairs={{8,16},{10,18},{16,24},{18,26},{24,28},{26,30},{28,20},{30,22},{20... | collective-permute-start | bytes 1572872 | tf_op jit(solution)/shard_map/ppermute | solution.py:69
  119.4 14.7 %collective-permute-start.31 = (bf16[128,1024]{1,0:T(8,128)(2,1)S(1)}, bf16[128,1024]{1,0:T(8,128)(2,1)S(1)}, u32[]{:S(2)}, u32[]{:S(2)}) collective-permute-start(bf16[128,1024]{1,0:T(8,128)(2,1)S(1)} %get-tuple-element.118), channel_id=1, source_target_pairs={{8,16},{10,18},{16,24},{18,26},{24,28},{26,30},{28,20},{30,22},{20... | collective-permute-start | bytes 786440 | tf_op jit(solution)/shard_map/ppermute | solution.py:69
  120.5 13.7 %collective-permute-start.35 = (bf16[128,1024]{1,0:T(8,128)(2,1)S(1)}, bf16[128,1024]{1,0:T(8,128)(2,1)S(1)}, u32[]{:S(2)}, u32[]{:S(2)}) collective-permute-start(bf16[128,1024]{1,0:T(8,128)(2,1)S(1)} %get-tuple-element.119), channel_id=1, source_target_pairs={{8,0},{10,2},{16,8},{18,10},{24,16},{26,18},{28,24},{30,26},{20,28... | collective-permute-start | bytes 786440 | tf_op jit(solution)/shard_map/ppermute | solution.py:69
  121.5 13.2 %collective-permute-start.32 = (bf16[128,1024]{1,0:T(8,128)(2,1)S(1)}, bf16[128,1024]{1,0:T(8,128)(2,1)S(1)}, u32[]{:S(2)}, u32[]{:S(2)}) collective-permute-start(bf16[128,1024]{1,0:T(8,128)(2,1)S(1)} %get-tuple-element.120), channel_id=1, source_target_pairs={{8,17},{9,16},{10,19},{11,18},{16,25},{17,24},{18,27},{19,26},{24,... | collective-permute-start | bytes 786440 | tf_op jit(solution)/shard_map/ppermute | solution.py:97
  123.5 11.2 %collective-permute-start.36 = (bf16[128,1024]{1,0:T(8,128)(2,1)S(1)}, bf16[128,1024]{1,0:T(8,128)(2,1)S(1)}, u32[]{:S(2)}, u32[]{:S(2)}) collective-permute-start(bf16[128,1024]{1,0:T(8,128)(2,1)S(1)} %get-tuple-element.121), channel_id=1, source_target_pairs={{8,1},{9,0},{10,3},{11,2},{16,9},{17,8},{18,11},{19,10},{24,17},{2... | collective-permute-start | bytes 786440 | tf_op jit(solution)/shard_map/ppermute | solution.py:97
  132.4 9.2 %collective-permute-start.39 = (bf16[128,1024]{1,0:T(8,128)(2,1)S(1)}, bf16[128,1024]{1,0:T(8,128)(2,1)S(1)}, u32[]{:S(2)}, u32[]{:S(2)}) collective-permute-start(bf16[128,1024]{1,0:T(8,128)(2,1)S(1)} %get-tuple-element.117), channel_id=1, source_target_pairs={{1,0},{0,1},{3,2},{2,3},{5,4},{4,5},{7,6},{6,7},{9,8},{8,9},{11,10... | collective-permute-start | bytes 786440 | tf_op jit(solution)/shard_map/ppermute | solution.py:105
  135.0 9.4 %collective-permute-start.33 = (bf16[128,1024]{1,0:T(8,128)(2,1)S(1)}, bf16[128,1024]{1,0:T(8,128)(2,1)S(1)}, u32[]{:S(2)}, u32[]{:S(2)}) collective-permute-start(bf16[128,1024]{1,0:T(8,128)(2,1)S(1)} %get-tuple-element.114), channel_id=1, source_target_pairs={{8,16},{10,18},{16,24},{18,26},{24,28},{26,30},{28,20},{30,22},{20... | collective-permute-start | bytes 786440 | tf_op jit(solution)/shard_map/ppermute | solution.py:69
  136.5 8.6 %collective-permute-start.37 = (bf16[128,1024]{1,0:T(8,128)(2,1)S(1)}, bf16[128,1024]{1,0:T(8,128)(2,1)S(1)}, u32[]{:S(2)}, u32[]{:S(2)}) collective-permute-start(bf16[128,1024]{1,0:T(8,128)(2,1)S(1)} %get-tuple-element.115), channel_id=1, source_target_pairs={{8,0},{10,2},{16,8},{18,10},{24,16},{26,18},{28,24},{30,26},{20,28... | collective-permute-start | bytes 786440 | tf_op jit(solution)/shard_map/ppermute | solution.py:69
  137.4 13.4 %collective-permute-start.30 = (bf16[128,1024]{1,0:T(8,128)(2,1)S(1)}, bf16[128,1024]{1,0:T(8,128)(2,1)S(1)}, u32[]{:S(2)}, u32[]{:S(2)}) collective-permute-start(bf16[128,1024]{1,0:T(8,128)(2,1)S(1)} %get-tuple-element.116), channel_id=1, source_target_pairs={{1,0},{0,1},{3,2},{2,3},{5,4},{4,5},{7,6},{6,7},{9,8},{8,9},{11,10... | collective-permute-start | bytes 786440 | tf_op jit(solution)/shard_map/ppermute | solution.py:105
  141.6 15.5 %copy-start.14 = (bf16[128,1024]{1,0:T(8,128)(2,1)S(1)}, bf16[128,1024]{1,0:T(8,128)(2,1)}, u32[]{:S(2)}) copy-start(bf16[128,1024]{1,0:T(8,128)(2,1)} %copy-done.13) | copy-start | bytes 786436
  141.6 10.4 %collective-permute-start.40 = (bf16[128,1024]{1,0:T(8,128)(2,1)S(1)}, bf16[128,1024]{1,0:T(8,128)(2,1)S(1)}, u32[]{:S(2)}, u32[]{:S(2)}) collective-permute-start(bf16[128,1024]{1,0:T(8,128)(2,1)S(1)} %add_convert_fusion.1), channel_id=1, source_target_pairs={{8,20},{10,22},{16,12},{18,14},{24,4},{26,6},{28,0},{30,2},{20,8},... | collective-permute-start | bytes 786440 | tf_op jit(solution)/shard_map/ppermute | solution.py:69
  145.2 15.9 %copy-start.22 = (f32[1024]{0:T(1024)S(1)}, f32[1024]{0:T(1024)}, u32[]{:S(2)}) copy-start(f32[1024]{0:T(1024)} %param.28) | copy-start | bytes 12292
  145.2 9.5 %collective-permute-start.34 = (bf16[128,1024]{1,0:T(8,128)(2,1)S(1)}, bf16[128,1024]{1,0:T(8,128)(2,1)S(1)}, u32[]{:S(2)}, u32[]{:S(2)}) collective-permute-start(bf16[128,1024]{1,0:T(8,128)(2,1)S(1)} %get-tuple-element.112), channel_id=1, source_target_pairs={{8,16},{10,18},{16,24},{18,26},{24,28},{26,30},{28,20},{30,22},{20... | collective-permute-start | bytes 786440 | tf_op jit(solution)/shard_map/ppermute | solution.py:69
  150.7 6.4 %collective-permute-start.38 = (bf16[128,1024]{1,0:T(8,128)(2,1)S(1)}, bf16[128,1024]{1,0:T(8,128)(2,1)S(1)}, u32[]{:S(2)}, u32[]{:S(2)}) collective-permute-start(bf16[128,1024]{1,0:T(8,128)(2,1)S(1)} %get-tuple-element.113), channel_id=1, source_target_pairs={{8,0},{10,2},{16,8},{18,10},{24,16},{26,18},{28,24},{30,26},{20,28... | collective-permute-start | bytes 786440 | tf_op jit(solution)/shard_map/ppermute | solution.py:69
  157.5 4.5 %copy-start.21 = (bf16[128,1024]{1,0:T(8,128)(2,1)}, bf16[128,1024]{1,0:T(8,128)(2,1)S(1)}, u32[]{:S(2)}) copy-start(bf16[128,1024]{1,0:T(8,128)(2,1)S(1)} %get-tuple-element.105) | copy-start | bytes 786436
  157.5 3.6 %collective-permute-start.41 = (f32[1,128]{1,0:T(1,128)S(1)}, f32[1,128]{1,0:T(1,128)S(1)}, u32[]{:S(2)}, u32[]{:S(2)}) collective-permute-start(f32[1,128]{1,0:T(1,128)S(1)} %bitcast.69), channel_id=1, source_target_pairs={{1,0},{0,1},{3,2},{2,3},{5,4},{4,5},{7,6},{6,7},{9,8},{8,9},{11,10... | collective-permute-start | bytes 1544 | tf_op jit(solution)/shard_map/ppermute | solution.py:105
  (2 other events, 1.4 us)
